TPU v7x, 128 devices: a whole 4x4x4 slice. The times are simulated.
128 devices in a mesh: seq: 16 (over x, y), exp: 8 (over z, core).
Axes of the slice: x: 4, y: 4, z: 4, core: 2. Of those that a mesh axis runs over, the one named last changes fastest.
Arguments:
- x_in: bfloat16 [4096, 8192], P('seq', 'exp'), may hold values from -6 to 6
- z_in: bfloat16 [4096, 8192], P('seq', 'exp'), may hold values from -6 to 6
- conv_weight: float32 [4, 8192], P(None, 'exp'), may hold values from -3 to 3
- conv_bias: float32 [8192], P('exp'), may hold values from -0.5 to 0.5
- x_proj: bfloat16 [8192, 288], P('exp'), may hold values from -0.0625 to 0.0625
- dt_proj: bfloat16 [256, 8192], P(None, 'exp'), may hold values from -0.375 to 0.375
- dt_bias: float32 [8192], P('exp'), may hold values from -3 to -1.5
- a_log: float32 [8192, 16], P('exp'), may hold values from -8.5 to -1.2
- d_skip: float32 [8192], P('exp'), may hold values from 0.5 to 1.5
- out_proj: bfloat16 [8192, 4096], P('exp', 'seq'), may hold values from -0.0625 to 0.0625
- residual: bfloat16 [4096, 4096], P(('seq', 'exp')), may hold values from -3 to 3
- expert_ids: int32 [4096, 2], P(('seq', 'exp')), may hold values from 0 to 15, all different within a row; in each aligned block of 32 rows (0 to 31, 32 to 63, ...) at most 8 rows name the same one
- gate_weights: float32 [4096, 2], P(('seq', 'exp')), may hold values from 0.1 to 1
- w_gate: bfloat16 [8, 4096, 12288], P('exp', None, 'seq'), may hold values from -0.09375 to 0.09375
- w_up: bfloat16 [8, 4096, 12288], P('exp', None, 'seq'), may hold values from -0.09375 to 0.09375
- w_down: bfloat16 [8, 12288, 4096], P('exp', 'seq'), may hold values from -0.0546875 to 0.0546875
Outputs:
- layer_out: float32 [4096, 4096], P(('seq', 'exp'))
Inputs may be any that keep to these rules, and one draw needn't show every extreme that they name: `expert_ids`: each token names 2 different experts; among the 32 tokens of one device no expert is named by more than 8 tokens.
All inputs are finite; a program needn't handle non-finite values.
Results may differ from a plain program's by a relative error of at most 0.0043.
Values may be sent and summed in bfloat16 or wider, within the bound.
No kernel may reach another device: no remote copies, remote signals or barrier semaphores. Data moves between devices by JAX's collectives and lax.ppermute only.
A program may use at most 128 MiB of HBM per device.

v0:
```python
import functools
import math

import jax
import jax.numpy as jnp
from jax import lax
from jax.experimental import pallas as pl
from jax.experimental.pallas import tpu as pltpu
from jax.sharding import PartitionSpec as P

RANK = 256
STATE = 16
CONV = 4
SEG = 8
LANES = 128
LOG2E = math.log2(math.e)
F32 = jnp.float32
BF16 = jnp.bfloat16
MIB = 1024 * 1024


def whole():
    return pl.BlockSpec(memory_space=pltpu.VMEM)


def far():
    return pl.BlockSpec(memory_space=pltpu.HBM)


def params(mib):
    return pltpu.CompilerParams(vmem_limit_bytes=mib * MIB)


def lines(stage):
    side = math.isqrt(lax.axis_size("seq"))
    owners = lax.axis_size("exp")
    groups = []
    for owner in range(owners):
        along_x = (owner % 2 == 0) == (stage == 0)
        for fixed in range(side):
            members = [(m * side + fixed if along_x else fixed * side + m) for m in range(side)]
            groups.append([m * owners + owner for m in members])
    return groups


def along(block, stage, distance):
    route = []
    for members in lines(stage):
        count = len(members)
        route += [(members[i], members[(i + distance) % count]) for i in range(count)]
    return lax.ppermute(block, ("seq", "exp"), route)


def passed_along(block, axis, distance):
    devices = range(lax.axis_size(axis))
    route = [(i - distance, i) for i in devices if i - distance in devices]
    return lax.ppermute(block, axis, route)


def conv_kernel(
    x_hbm,
    weight_hbm,
    bias_hbm,
    proj_hbm,
    rim_ref,
    mixed_ref,
    part_ref,
    x_ref,
    weight_ref,
    bias_ref,
    proj_ref,
    padded,
    sems,
):
    sources = (x_hbm, weight_hbm, bias_hbm, proj_hbm)
    targets = (x_ref, weight_ref, bias_ref, proj_ref)
    copies = [pltpu.make_async_copy(*pair, sems.at[k]) for k, pair in enumerate(zip(sources, targets))]
    for copy in copies:
        copy.start()
    length, channels = x_ref.shape
    steps = length // SEG
    head = 8
    for copy in copies[:3]:
        copy.wait()
    for lane in range(0, channels, LANES):
        block = padded.at[lane // LANES]
        block[head - (CONV - 1) : head, :] = rim_ref[:, lane : lane + LANES].astype(F32)
        block[head:, :] = x_ref[:, lane : lane + LANES].astype(F32)

    def step(i, carry):
        rows = pl.ds(pl.multiple_of(i * SEG, SEG), SEG)
        for lane in range(0, channels, LANES):
            lanes = pl.ds(lane, LANES)
            acc = jnp.broadcast_to(bias_ref[:, lanes], (SEG, LANES))
            for tap in range(CONV):
                taken = padded[
                    lane // LANES, pl.ds(i + head - (CONV - 1) + tap, SEG, stride=steps), :
                ]
                acc = acc + weight_ref[tap : tap + 1, lanes] * taken
            mixed_ref[rows, lanes] = (acc * jax.nn.sigmoid(acc)).astype(BF16).astype(F32)
        return carry

    lax.fori_loop(0, steps, step, 0)
    copies[3].wait()
    part_ref[...] = jnp.dot(
        mixed_ref[...].astype(BF16), proj_ref[...], preferred_element_type=F32
    )


def spread(target, packed_ref, first):
    packed = packed_ref[...].astype(F32)
    coef = packed[:, RANK : RANK + 2 * STATE] + packed[:, RANK + 2 * STATE :]
    for n in range(STATE):
        target[n] = jnp.broadcast_to(coef[:, first + n : first + n + 1], (coef.shape[0], LANES))


def scan_kernel(
    packed_ref,
    mixed_ref,
    rates_ref,
    proj_hbm,
    bias_hbm,
    y_ref,
    delta_ref,
    before_hbm,
    enter_hbm,
    msg_hbm,
    b_wide,
    c_wide,
    proj_ref,
    bias_ref,
    before_ref,
    enter_ref,
    msg_ref,
    in_sems,
    out_sems,
):
    length, channels = mixed_ref.shape
    steps = length // SEG
    copies = [
        pltpu.make_async_copy(proj_hbm, proj_ref, in_sems.at[0]),
        pltpu.make_async_copy(bias_hbm, bias_ref, in_sems.at[1]),
    ]
    for copy in copies:
        copy.start()
    spread(b_wide, packed_ref, 0)
    spread(c_wide, packed_ref, STATE)
    for copy in copies:
        copy.wait()
    copies = []
    raw = jnp.dot(packed_ref[:, :RANK], proj_ref[...], preferred_element_type=F32) + bias_ref[...]
    delta_ref[...] = jnp.maximum(raw, 0.0) + jnp.log1p(jnp.exp(-jnp.abs(raw)))
    row = lax.broadcasted_iota(jnp.int32, (SEG, LANES), 0)

    def shifted(value, by, fill):
        return jnp.where(row < by, fill, pltpu.roll(value, by, axis=0))

    for lane in range(0, channels, LANES):
        lanes = pl.ds(lane, LANES)
        rates = [
            jnp.broadcast_to(rates_ref[n : n + 1, lanes], (SEG, LANES)) for n in range(STATE)
        ]

        def step(i, carry):
            elapsed, states = carry
            rows = pl.ds(pl.multiple_of(i * SEG, SEG), SEG)
            delta = delta_ref[rows, lanes]
            drive = delta * mixed_ref[rows, lanes]
            fresh, terms = [], []
            for n in range(STATE):
                state = jnp.exp2(delta * rates[n]) * states[n] + drive * b_wide[n, rows, :]
                fresh.append(state)
                terms.append(state * c_wide[n, rows, :])
            while len(terms) > 1:
                terms = [a + b for a, b in zip(terms[::2], terms[1::2])]
            y_ref[rows, lanes] = terms[0]
            return elapsed + delta, tuple(fresh)

        zero = jnp.zeros((SEG, LANES), F32)
        elapsed, states = lax.fori_loop(0, steps, step, (zero, (zero,) * STATE), unroll=2)
        total = elapsed
        for by in (1, 2, 4):
            total = total + shifted(total, by, 0.0)
        before_ref[:, lanes] = shifted(total, 1, 0.0)
        last = total[SEG - 1 : SEG, :]
        for n in range(STATE):
            decay = jnp.exp2(elapsed * rates[n])
            state = states[n]
            for by in (1, 2, 4):
                state = decay * shifted(state, by, 0.0) + state
                decay = decay * shifted(decay, by, 1.0)
            enter_ref[n, :, lanes] = shifted(state, 1, 0.0)
            msg_ref[n, 0:1, lanes] = state[SEG - 1 : SEG, :]
            msg_ref[n, 1:2, lanes] = last
        block = lane // LANES
        fresh = [
            pltpu.make_async_copy(
                before_ref.at[:, lanes], before_hbm.at[:, lanes], out_sems.at[0, block]
            ),
            pltpu.make_async_copy(
                enter_ref.at[:, :, lanes], enter_hbm.at[:, :, lanes], out_sems.at[1, block]
            ),
            pltpu.make_async_copy(
                msg_ref.at[:, :, lanes], msg_hbm.at[:, :, lanes], out_sems.at[2, block]
            ),
        ]
        for copy in fresh:
            copy.start()
        copies += fresh
    for copy in copies:
        copy.wait()


def relay_kernel(place_ref, ends_ref, rates_ref, out_ref):
    rate = rates_ref[pl.ds(place_ref[0], 1), :]
    state = jnp.zeros_like(rate)
    for device in range(ends_ref.shape[0]):
        out_ref[device] = state
        state = jnp.exp2(ends_ref[device, 1:2, :] * rate) * state + ends_ref[device, 0:1, :]


def finish_kernel(
    order_ref,
    entering_ref,
    rates_ref,
    delta_ref,
    packed_ref,
    y_ref,
    mixed_ref,
    before_hbm,
    enter_hbm,
    skip_hbm,
    z_hbm,
    gated_ref,
    before_ref,
    enter_ref,
    skip_ref,
    z_ref,
    c_wide,
    z_wide,
    gated,
    sems,
):
    length, channels = mixed_ref.shape
    steps = length // SEG
    sources = (before_hbm, enter_hbm, skip_hbm, z_hbm)
    targets = (before_ref, enter_ref, skip_ref, z_ref)
    copies = [pltpu.make_async_copy(*pair, sems.at[k]) for k, pair in enumerate(zip(sources, targets))]
    for copy in copies:
        copy.start()
    spread(c_wide, packed_ref, STATE)
    for copy in copies:
        copy.wait()
    for lane in range(0, channels, LANES):
        z_wide[lane // LANES] = z_ref[:, lane : lane + LANES].astype(F32)

    for lane in range(0, channels, LANES):
        lanes = pl.ds(lane, LANES)
        rates = [
            jnp.broadcast_to(rates_ref[n : n + 1, lanes], (SEG, LANES)) for n in range(STATE)
        ]
        before = before_ref[:, lanes]
        held = [
            jnp.exp2(before * rates[n]) * entering_ref[n : n + 1, lanes] + enter_ref[n, :, lanes]
            for n in range(STATE)
        ]
        skip = skip_ref[:, lanes]

        def step(i, elapsed):
            rows = pl.ds(pl.multiple_of(i * SEG, SEG), SEG)
            apart = pl.ds(i, SEG, stride=steps)
            elapsed = elapsed + delta_ref[rows, lanes]
            terms = [
                jnp.exp2(elapsed * rates[n]) * held[n] * c_wide[n, rows, :] for n in range(STATE)
            ]
            while len(terms) > 1:
                terms = [a + b for a, b in zip(terms[::2], terms[1::2])]
            output = y_ref[rows, lanes] + terms[0] + skip * mixed_ref[rows, lanes]
            z = z_wide[lane // LANES, apart, :]
            gated[lane // LANES, apart, :] = output * (z * jax.nn.sigmoid(z))
            return elapsed

        lax.fori_loop(0, steps, step, jnp.zeros((SEG, LANES), F32), unroll=2)
    for place in range(SEG):
        rows = pl.ds(pl.multiple_of(order_ref[place] * steps, steps), steps)
        for lane in range(0, channels, LANES):
            gated_ref[place * steps : (place + 1) * steps, lane : lane + LANES] = gated[
                lane // LANES, rows, :
            ].astype(BF16)


def outward_kernel(gated_ref, proj_hbm, send_ref, keep_ref, proj, arrived):
    parts, _, width = proj_hbm.shape
    middle = send_ref.shape[0]
    for part in range(parts):
        pltpu.make_async_copy(proj_hbm.at[part], proj.at[part], arrived.at[part]).start()

    def product(part, carry):
        pltpu.make_async_copy(proj_hbm.at[part], proj.at[part], arrived.at[part]).wait()
        columns = pl.ds(pl.multiple_of(part * width, width), width)
        terms = jnp.dot(gated_ref[...], proj[part], preferred_element_type=F32)
        send_ref[:, columns] = terms[:middle].astype(BF16)
        keep_ref[:, columns] = terms[middle:]
        return carry

    lax.fori_loop(0, parts, product, 0)


def expert_kernel(rows_ref, gate_ref, up_ref, down_ref, out_ref, inner):
    tile = 256

    def widen(part, carry):
        columns = pl.ds(pl.multiple_of(part * tile, tile), tile)
        gate = jnp.dot(rows_ref[...], gate_ref[:, columns], preferred_element_type=F32)
        upper = jnp.dot(rows_ref[...], up_ref[:, columns], preferred_element_type=F32)
        inner[:, columns] = (gate * jax.nn.sigmoid(gate) * upper).astype(BF16)
        return carry

    lax.fori_loop(0, inner.shape[1] // tile, widen, 0)

    def narrow(part, carry):
        columns = pl.ds(pl.multiple_of(part * tile, tile), tile)
        piece = jnp.dot(inner[...], down_ref[:, columns], preferred_element_type=F32)
        out_ref[:, columns] = piece.astype(BF16)
        return carry

    lax.fori_loop(0, out_ref.shape[1] // tile, narrow, 0)


def expert(rows, gate, up, down):
    count, features = rows.shape
    hidden = gate.shape[1]
    return pl.pallas_call(
        expert_kernel,
        out_shape=jax.ShapeDtypeStruct((count, features), BF16),
        in_specs=[whole()] * 4,
        out_specs=whole(),
        scratch_shapes=[pltpu.VMEM((count, hidden), BF16)],
        compiler_params=params(12),
        cost_estimate=pl.CostEstimate(
            flops=6 * count * features * hidden,
            bytes_accessed=4 * count * features,
            transcendentals=count * hidden,
        ),
        name="expert",
    )(rows, gate, up, down)


def halves(block):
    middle = block.shape[0] // 2
    return block[:middle], block[middle:]


def added(*blocks):
    total = blocks[0].astype(F32)
    for block in blocks[1:]:
        total = total + block.astype(F32)
    return total.astype(BF16)


def experts_on_grid(rows, gate, up, down):
    run = functools.partial(expert, gate=gate, up=up, down=down)
    behind = along(rows, 0, 1)
    ahead = along(rows, 0, -1)
    across = along(rows, 0, 2)
    own = jnp.concatenate([rows, behind, ahead, across], axis=0)
    behind = along(own, 1, 1)
    ahead = along(own, 1, -1)
    own_out = run(own)
    behind, ahead, own_out = lax.optimization_barrier((behind, ahead, own_out))
    far_first = along(halves(behind)[0], 1, 1)
    far_second = along(halves(ahead)[1], 1, -1)
    behind_out = run(behind)
    far_first, far_second, behind_out = lax.optimization_barrier((far_first, far_second, behind_out))
    far_out = run(jnp.concatenate([far_first, far_second], axis=0))
    first, second = halves(far_out)
    from_behind = along(first, 1, 1)
    from_ahead = along(second, 1, -1)
    ahead_out = run(ahead)
    from_behind, from_ahead, ahead_out = lax.optimization_barrier(
        (from_behind, from_ahead, ahead_out)
    )
    ahead_first, ahead_second = halves(ahead_out)
    behind_first, behind_second = halves(behind_out)
    ahead_sum = jnp.concatenate([added(ahead_first, from_behind), ahead_second], axis=0)
    behind_sum = jnp.concatenate([behind_first, added(behind_second, from_ahead)], axis=0)
    ahead_sum, behind_sum = lax.optimization_barrier((ahead_sum, behind_sum))
    from_behind = along(ahead_sum, 1, 1)
    from_ahead = along(behind_sum, 1, -1)
    total = added(own_out, from_behind, from_ahead)
    kept, behind, ahead, across = jnp.split(total, 4, axis=0)
    return added(kept, along(behind, 0, -1), along(ahead, 0, 1), along(across, 0, 2))


def mixer(x_in, z_in, conv_weight, conv_bias, x_proj, dt_proj, dt_bias, a_log, d_skip, out_proj):
    length, channels = x_in.shape
    steps = length // SEG
    owners = lax.axis_size("exp")
    seqs = lax.axis_size("seq")
    columns = lax.all_gather(out_proj, "seq", axis=0)
    rates = (-jnp.exp(a_log) * LOG2E).T
    rim = passed_along(x_in[length - (CONV - 1) :], "seq", 1)
    mixed, partial = pl.pallas_call(
        conv_kernel,
        out_shape=(
            jax.ShapeDtypeStruct((length, channels), F32),
            jax.ShapeDtypeStruct((length, RANK + 2 * STATE), F32),
        ),
        in_specs=[far()] * 4 + [whole()],
        out_specs=[whole()] * 2,
        scratch_shapes=[
            pltpu.VMEM(x_in.shape, BF16),
            pltpu.VMEM(conv_weight.shape, F32),
            pltpu.VMEM((1, channels), F32),
            pltpu.VMEM(x_proj.shape, BF16),
            pltpu.VMEM((channels // LANES, length + 8, LANES), F32),
            pltpu.SemaphoreType.DMA((4,)),
        ],
        compiler_params=params(12),
        name="conv",
    )(x_in, conv_weight, conv_bias[None, :], x_proj, rim)
    share = lax.all_to_all(
        partial.reshape(owners, length // owners, -1), "exp", split_axis=0, concat_axis=0, tiled=True
    )
    summed = jnp.sum(share, axis=0)
    low = summed[:, :RANK].astype(BF16)
    coef = summed[:, RANK:]
    coef_high = coef.astype(BF16)
    coef_low = (coef - coef_high.astype(F32)).astype(BF16)
    packed = jnp.concatenate([low, coef_high, coef_low], axis=1)
    packed = lax.all_to_all(
        jnp.broadcast_to(packed[None], (owners,) + packed.shape),
        "exp",
        split_axis=0,
        concat_axis=0,
        tiled=True,
    ).reshape(length, -1)
    y_local, delta, before, enter, message = pl.pallas_call(
        scan_kernel,
        out_shape=(
            jax.ShapeDtypeStruct((length, channels), F32),
            jax.ShapeDtypeStruct((length, channels), F32),
            jax.ShapeDtypeStruct((SEG, channels), F32),
            jax.ShapeDtypeStruct((STATE, SEG, channels), F32),
            jax.ShapeDtypeStruct((STATE, 2, channels), F32),
        ),
        in_specs=[whole()] * 3 + [far()] * 2,
        out_specs=[whole()] * 2 + [far()] * 3,
        scratch_shapes=[
            pltpu.VMEM((STATE, length, LANES), F32),
            pltpu.VMEM((STATE, length, LANES), F32),
            pltpu.VMEM(dt_proj.shape, BF16),
            pltpu.VMEM((1, channels), F32),
            pltpu.VMEM((SEG, channels), F32),
            pltpu.VMEM((STATE, SEG, channels), F32),
            pltpu.VMEM((STATE, 2, channels), F32),
            pltpu.SemaphoreType.DMA((2,)),
            pltpu.SemaphoreType.DMA((3, channels // LANES)),
        ],
        compiler_params=params(14),
        name="scan",
    )(packed, mixed, rates, dt_proj, dt_bias[None, :])
    ends = lax.all_to_all(message, "seq", split_axis=0, concat_axis=0, tiled=True)
    place = lax.axis_index("seq").astype(jnp.int32).reshape(1)
    entering = pl.pallas_call(
        relay_kernel,
        out_shape=jax.ShapeDtypeStruct((seqs, 1, channels), F32),
        in_specs=[pl.BlockSpec(memory_space=pltpu.SMEM), whole(), whole()],
        out_specs=whole(),
        compiler_params=params(4),
        name="relay",
    )(place, ends, rates)
    entering = lax.all_to_all(entering, "seq", split_axis=0, concat_axis=0, tiled=True)
    side = owners // 2
    owner = lax.axis_index("exp").astype(jnp.int32)
    chips = (owner // 2 + jnp.arange(side, dtype=jnp.int32)) % side
    order = jnp.concatenate([chips * 2 + 1 - owner % 2, chips * 2 + owner % 2])
    gated = pl.pallas_call(
        finish_kernel,
        out_shape=jax.ShapeDtypeStruct((length, channels), BF16),
        in_specs=[pl.BlockSpec(memory_space=pltpu.SMEM)] + [whole()] * 6 + [far()] * 4,
        out_specs=whole(),
        scratch_shapes=[
            pltpu.VMEM((SEG, channels), F32),
            pltpu.VMEM((STATE, SEG, channels), F32),
            pltpu.VMEM((1, channels), F32),
            pltpu.VMEM((length, channels), BF16),
            pltpu.VMEM((STATE, length, LANES), F32),
            pltpu.VMEM((channels // LANES, length, LANES), F32),
            pltpu.VMEM((channels // LANES, length, LANES), F32),
            pltpu.SemaphoreType.DMA((4,)),
        ],
        compiler_params=params(14),
        name="finish",
    )(
        order,
        entering.reshape(STATE, channels),
        rates,
        delta,
        packed,
        y_local,
        mixed,
        before,
        enter,
        d_skip[None, :],
        z_in,
    )
    width = out_proj.shape[1]
    features = seqs * width
    send, keep = pl.pallas_call(
        outward_kernel,
        out_shape=(
            jax.ShapeDtypeStruct((length // 2, features), BF16),
            jax.ShapeDtypeStruct((length // 2, features), F32),
        ),
        in_specs=[whole(), far()],
        out_specs=[whole()] * 2,
        scratch_shapes=[
            pltpu.VMEM((seqs, channels, width), BF16),
            pltpu.SemaphoreType.DMA((seqs,)),
        ],
        compiler_params=params(14),
        name="outward",
    )(gated, columns)
    swap = [(e, e + 1 - 2 * (e % 2)) for e in range(owners)]
    sums = keep + lax.ppermute(send, "exp", swap).astype(F32)
    sums = sums.reshape(side, length // owners, features)
    total = sums[0]
    for hop in range(1, side):
        route = [(e, (e + 2 * hop) % owners) for e in range(owners)]
        total = total + lax.ppermute(sums[hop].astype(BF16), "exp", route).astype(F32)
    return total


def shards(
    x_in,
    z_in,
    conv_weight,
    conv_bias,
    x_proj,
    dt_proj,
    dt_bias,
    a_log,
    d_skip,
    out_proj,
    residual,
    expert_ids,
    gate_weights,
    w_gate,
    w_up,
    w_down,
):
    owners = lax.axis_size("exp")
    tok_rows = residual.shape[0]
    mixed = mixer(
        x_in, z_in, conv_weight, conv_bias, x_proj, dt_proj, dt_bias, a_log, d_skip, out_proj
    )
    hidden = residual.astype(jnp.float32) + mixed
    normed = (hidden * lax.rsqrt(jnp.mean(hidden * hidden, axis=-1, keepdims=True) + 1e-06)).astype(
        jnp.bfloat16
    )
    capacity = max(2, tok_rows // 4)
    slots = owners * capacity
    chosen_count = expert_ids.shape[1]
    flat_ids = expert_ids.reshape(-1)
    hits = (flat_ids[:, None] == jnp.arange(owners, dtype=jnp.int32)[None, :]).astype(jnp.int32)
    before = jnp.cumsum(hits, axis=0) - hits
    ranked = jnp.sum(before * hits, axis=1)
    valid = jnp.sum(hits, axis=1)
    target = flat_ids * capacity + ranked
    placed = (
        (target[:, None] == jnp.arange(slots, dtype=jnp.int32)[None, :]) & (valid[:, None] > 0)
    ).astype(jnp.float32)
    dispatch_table = jnp.sum(placed.reshape(tok_rows, chosen_count, slots), axis=1)
    combine_table = jnp.sum(
        (placed * gate_weights.reshape(-1)[:, None]).reshape(tok_rows, chosen_count, slots), axis=1
    )
    outgoing = jnp.einsum(
        "ts,td->sd", dispatch_table.astype(jnp.bfloat16), normed, preferred_element_type=jnp.float32
    )
    outgoing = outgoing.astype(jnp.bfloat16).reshape(owners, capacity, -1)
    arrived = lax.all_to_all(outgoing, "exp", split_axis=0, concat_axis=0, tiled=True)
    summed = experts_on_grid(arrived.reshape(slots, -1), w_gate[0], w_up[0], w_down[0])
    expert_out = summed.reshape(owners, capacity, -1)
    returned_rows = lax.all_to_all(
        expert_out, "exp", split_axis=0, concat_axis=0, tiled=True
    ).reshape(slots, -1)
    combined = jnp.dot(
        combine_table, returned_rows.astype(jnp.float32), precision=lax.Precision.HIGHEST
    )
    return hidden + combined


def solution(mesh):
    placed = (
        P("seq", "exp"),
        P("seq", "exp"),
        P(None, "exp"),
        P("exp"),
        P("exp", None),
        P(None, "exp"),
        P("exp"),
        P("exp", None),
        P("exp"),
        P("exp", "seq"),
        P(("seq", "exp"), None),
        P(("seq", "exp"), None),
        P(("seq", "exp"), None),
        P("exp", None, "seq"),
        P("exp", None, "seq"),
        P("exp", "seq", None),
    )
    return jax.shard_map(
        shards, mesh=mesh, in_specs=placed, out_specs=P(("seq", "exp"), None), check_vma=False
    )
```

profile of v0, /device:TPU:24, one launch (start us, length us, event | category | flops | bytes accessed | tf_op | source)
XLA Modules:
  0.0 297.2 jit_solution(12382502011799478205)
XLA Ops:
  6.5 0.7 all-gather.3.cloned.1.call-update
  7.3 0.7 slice.53
  8.0 3.2 %collective-permute-start = (bf16[3,1024]{1,0:T(4,128)(2,1)S(1)}, bf16[3,1024]{1,0:T(4,128)(2,1)S(1)}, u32[]{:S(2)}, u32[]{:S(2)}) collective-permute-start(bf16[3,1024]{1,0:T(4,128)(2,1)S(1)} %slice.53), channel_id=1, source_target_pairs={{0,8},{8,16},{16,24},{24,32},{32,40},{40,48},{48,56},{56,64},{64,7... | collective-permute-start | bytes 18440 | tf_op jit(solution)/shard_map/ppermute | solution.py:57
  11.2 1.4 copy.40.proj_hbm
  12.6 1.1 collective-permute-done.rim_ref
  13.7 0.7 copy-done.12
  14.4 0.7 copy-done.13
  15.1 3.7 %conv.1 = (f32[256,1024]{1,0:T(8,128)S(1)}, f32[256,288]{1,0:T(8,128)S(1)}) custom-call(bf16[256,1024]{1,0:T(8,128)(2,1)S(1)} %copy-done.9, f32[4,1024]{1,0:T(4,128)S(1)} %copy-done.12, f32[1,1024]{1,0:T(1,128)S(1)} %bitcast.46, bf16[1024,288]{1,0:T(8,128)(2,1)S(1)} %copy.40.proj_hbm, bf16[3,1024]{1,0:T(4,128)(2,1)S(1)} %collective-permute-done.rim_ref), custom_call_target="tpu_custom_call" | custom-call | tf_op jit(solution)/shard_map/conv/pallas_call | solution.py:403
  18.8 14.1 %all_to_all.30 = f32[8,32,288]{2,1,0:T(8,128)S(1)} all-to-all(f32[8,32,288]{2,1,0:T(8,128)S(1)} %bitcast.44), channel_id=1, replica_groups=mesh['seq'=16,'exp'=8] {'exp'}, dimensions={0} | all-to-all | bytes 589824 | tf_op jit(solution)/shard_map/all_to_all | solution.py:422
  33.0 0.7 broadcast_in_dim.9
  33.7 3.4 %all-to-all-start.1 = ((bf16[8,32,320]{2,1,0:T(8,128)(2,1)}), bf16[8,32,320]{2,1,0:T(8,128)(2,1)S(1)}, u32[]{:S(2)}, u32[]{:S(2)}) async-start(bf16[8,32,320]{2,1,0:T(8,128)(2,1)} %broadcast_in_dim.9), calls=%async_computation.1 | async-start | bytes 393216 | tf_op jit(solution)/shard_map/all_to_all | solution.py:431
  37.1 6.7 %all-to-all-done.1 = bf16[8,32,320]{2,1,0:T(8,128)(2,1)S(1)} async-done(((bf16[8,32,320]{2,1,0:T(8,128)(2,1)}), bf16[8,32,320]{2,1,0:T(8,128)(2,1)S(1)}, u32[]{:S(2)}, u32[]{:S(2)}) %all-to-all-start.1) | async-done | bytes 163872 | tf_op jit(solution)/shard_map/all_to_all | solution.py:431
  43.9 8.9 %scan.1 = (f32[256,1024]{1,0:T(8,128)S(1)}, f32[256,1024]{1,0:T(8,128)S(1)}, f32[8,1024]{1,0:T(8,128)S(1)}, f32[16,8,1024]{2,1,0:T(8,128)S(1)}, f32[16,2,1024]{2,1,0:T(2,128)}) custom-call(bf16[256,320]{1,0:T(8,128)(2,1)S(1)} %bitcast.42, f32[256,1024]{1,0:T(8,128)S(1)} %get-tuple-element.26.mixed_ref, f32[16,1024]{1,0:T(8,128)S(1)} %multiply_bitcast_fusion.rates_ref, ...), custom_call_target="tpu_custom_call" | custom-call | tf_op jit(solution)/shard_map/scan/pallas_call | solution.py:438
  52.8 1.0 copy-done.5
  53.7 1.0 copy-done.7
  54.7 7.2 %all-to-all-start.2 = ((f32[16,2,1024]{2,1,0:T(2,128)}), f32[16,2,1024]{2,1,0:T(2,128)S(1)}, u32[]{:S(2)}, u32[]{:S(2)}) async-start(f32[16,2,1024]{2,1,0:T(2,128)} %get-tuple-element.27), calls=%async_computation.2 | async-start | bytes 262144 | tf_op jit(solution)/shard_map/all_to_all | solution.py:463
  61.9 6.9 %all-to-all-done.2.ends_ref = f32[16,2,1024]{2,1,0:T(2,128)S(1)} async-done(((f32[16,2,1024]{2,1,0:T(2,128)}), f32[16,2,1024]{2,1,0:T(2,128)S(1)}, u32[]{:S(2)}, u32[]{:S(2)}) %all-to-all-start.2) | async-done | bytes 131104 | tf_op jit(solution)/shard_map/all_to_all | solution.py:463
  68.8 0.7 relay.1
  69.5 6.0 %all-to-all-start.3 = ((f32[16,1,1024]{2,1,0:T(1,128)}), f32[16,1,1024]{2,1,0:T(1,128)S(1)}, u32[]{:S(2)}, u32[]{:S(2)}) async-start(f32[16,1,1024]{2,1,0:T(1,128)} %relay.1), calls=%async_computation.3 | async-start | bytes 131072 | tf_op jit(solution)/shard_map/all_to_all | solution.py:473
  75.6 6.0 %all-to-all-done.3 = f32[16,1,1024]{2,1,0:T(1,128)S(1)} async-done(((f32[16,1,1024]{2,1,0:T(1,128)}), f32[16,1,1024]{2,1,0:T(1,128)S(1)}, u32[]{:S(2)}, u32[]{:S(2)}) %all-to-all-start.3) | async-done | bytes 65568 | tf_op jit(solution)/shard_map/all_to_all | solution.py:473
  81.6 1.2 copy-done.6
  82.9 1.2 copy-done.8
  84.1 7.0 %finish.1.gated_ref = bf16[256,1024]{1,0:T(8,128)(2,1)S(1)} custom-call(s32[8]{0:T(128)S(1)} %pad_add_fusion.order_ref, f32[16,1024]{1,0:T(8,128)S(1)} %bitcast.45, f32[16,1024]{1,0:T(8,128)S(1)} %multiply_bitcast_fusion.rates_ref, f32[256,1024]{1,0:T(8,128)S(1)} %copy-done.8, bf16[256,320]{1,0:T(8,128)(2,1)S(1)} %bitcast.43, f32[256,1024]{1,0:T(8,128)S(1)} %copy-done.6, ...), custom_call_target="tpu_custom_call" | custom-call | tf_op jit(solution)/shard_map/finish/pallas_call | solution.py:478
  91.1 3.4 %copy-done.1 = bf16[16384,256]{1,0:T(8,128)(2,1)S(1)} copy-done((bf16[16384,256]{1,0:T(8,128)(2,1)S(1)}, bf16[16384,256]{1,0:T(8,128)(2,1)}, u32[]{:S(2)}) %copy-start.1) | copy-done | bytes 8388632
  94.5 6.5 %outward.1 = (bf16[128,4096]{1,0:T(8,128)(2,1)}, f32[128,4096]{1,0:T(8,128)S(1)}) custom-call(bf16[256,1024]{1,0:T(8,128)(2,1)S(1)} %finish.1.gated_ref, bf16[16,1024,256]{2,1,0:T(8,128)(2,1)S(1)} %bitcast.41), custom_call_target="tpu_custom_call" | custom-call | tf_op jit(solution)/shard_map/outward/pallas_call | solution.py:510
  101.1 1.3 copy-done.4
  103.4 1.9 collective-permute-done.1
  105.3 2.1 fusion.14
  107.4 0.6 collective-permute-start.2
  108.0 2.0 collective-permute-start.3
  110.1 0.7 collective-permute-start.4
  110.9 11.7 %collective-permute-done.2 = bf16[32,4096]{1,0:T(8,128)(2,1)S(1)} collective-permute-done((bf16[32,4096]{1,0:T(8,128)(2,1)S(1)}, bf16[32,4096]{1,0:T(8,128)(2,1)S(1)}, u32[]{:S(2)}, u32[]{:S(2)}) %collective-permute-start.2) | collective-permute-done | bytes 262176 | tf_op jit(solution)/shard_map/ppermute | solution.py:531
  122.7 0.6 collective-permute-done.4
  123.6 0.4 fusion
  123.9 13.9 %all_to_all.31 = bf16[8,8,4096]{2,1,0:T(8,128)(2,1)S(1)} all-to-all(bf16[8,8,4096]{2,1,0:T(8,128)(2,1)S(1)} %fusion), channel_id=1, replica_groups=mesh['seq'=16,'exp'=8] {'exp'}, dimensions={0} | all-to-all | bytes 1048576 | tf_op jit(solution)/shard_map/all_to_all | solution.py:582
  137.8 0.4 collective-permute-start.5
  138.2 2.9 collective-permute-start.6
  141.1 12.8 %collective-permute-done.5 = bf16[64,4096]{1,0:T(8,128)(2,1)S(1)} collective-permute-done((bf16[64,4096]{1,0:T(8,128)(2,1)S(1)}, bf16[64,4096]{1,0:T(8,128)(2,1)S(1)}, u32[]{:S(2)}, u32[]{:S(2)}) %collective-permute-start.5) | collective-permute-done | bytes 524320 | tf_op jit(solution)/shard_map/ppermute | solution.py:51
  154.1 2.1 collective-permute-start.8
  156.2 2.8 copy-done
  159.0 8.4 %expert.4 = bf16[256,4096]{1,0:T(8,128)(2,1)S(1)} custom-call(bf16[256,4096]{1,0:T(8,128)(2,1)S(1)} %pad_maximum_fusion.rows_ref, bf16[4096,768]{1,0:T(8,128)(2,1)S(1)} %bitcast.27, bf16[4096,768]{1,0:T(8,128)(2,1)S(1)} %bitcast.33, bf16[768,4096]{1,0:T(8,128)(2,1)S(1)} %bitcast.37), custom_call_target="tpu_custom_call" | custom-call | flops 4831838208 | bytes 4194304 | tf_op jit(solution)/shard_map/expert/pallas_call | solution.py:333
  167.4 12.8 %collective-permute-done.8.rows_ref = bf16[256,4096]{1,0:T(8,128)(2,1)S(1)} collective-permute-done((bf16[256,4096]{1,0:T(8,128)(2,1)S(1)}, bf16[256,4096]{1,0:T(8,128)(2,1)S(1)}, u32[]{:S(2)}, u32[]{:S(2)}) %collective-permute-start.8) | collective-permute-done | bytes 2097184 | tf_op jit(solution)/shard_map/ppermute | solution.py:51
  180.2 3.2 %collective-permute-done.9.rows_ref = bf16[256,4096]{1,0:T(8,128)(2,1)S(1)} collective-permute-done((bf16[256,4096]{1,0:T(8,128)(2,1)S(1)}, bf16[256,4096]{1,0:T(8,128)(2,1)S(1)}, u32[]{:S(2)}, u32[]{:S(2)}) %collective-permute-start.9) | collective-permute-done | bytes 2097184 | tf_op jit(solution)/shard_map/ppermute | solution.py:51
  183.7 2.1 collective-permute-start.11
  185.8 8.4 %expert.5 = bf16[256,4096]{1,0:T(8,128)(2,1)S(1)} custom-call(bf16[256,4096]{1,0:T(8,128)(2,1)S(1)} %collective-permute-done.8.rows_ref, bf16[4096,768]{1,0:T(8,128)(2,1)S(1)} %bitcast.28, bf16[4096,768]{1,0:T(8,128)(2,1)S(1)} %bitcast.34, bf16[768,4096]{1,0:T(8,128)(2,1)S(1)} %bitcast.38), custom_call_target="tpu_custom_call" | custom-call | flops 4831838208 | bytes 4194304 | tf_op jit(solution)/shard_map/expert/pallas_call | solution.py:333
  194.2 4.2 %collective-permute-done.10 = bf16[128,4096]{1,0:T(8,128)(2,1)S(1)} collective-permute-done((bf16[128,4096]{1,0:T(8,128)(2,1)S(1)}, bf16[128,4096]{1,0:T(8,128)(2,1)S(1)}, u32[]{:S(2)}, u32[]{:S(2)}) %collective-permute-start.10) | collective-permute-done | bytes 1048608 | tf_op jit(solution)/shard_map/ppermute | solution.py:51
  198.4 1.4 collective-permute-done.11
  200.0 8.4 %expert.6 = bf16[256,4096]{1,0:T(8,128)(2,1)S(1)} custom-call(bf16[256,4096]{1,0:T(8,128)(2,1)S(1)} %pad_maximum_fusion.1.rows_ref, bf16[4096,768]{1,0:T(8,128)(2,1)S(1)} %bitcast.29, bf16[4096,768]{1,0:T(8,128)(2,1)S(1)} %bitcast.35, bf16[768,4096]{1,0:T(8,128)(2,1)S(1)} %bitcast.39), custom_call_target="tpu_custom_call" | custom-call | flops 4831838208 | bytes 4194304 | tf_op jit(solution)/shard_map/expert/pallas_call | solution.py:333
  208.7 2.0 collective-permute-start.13
  210.7 8.4 %expert.7 = bf16[256,4096]{1,0:T(8,128)(2,1)S(1)} custom-call(bf16[256,4096]{1,0:T(8,128)(2,1)S(1)} %collective-permute-done.9.rows_ref, bf16[4096,768]{1,0:T(8,128)(2,1)S(1)} %bitcast.30, bf16[4096,768]{1,0:T(8,128)(2,1)S(1)} %bitcast.36, bf16[768,4096]{1,0:T(8,128)(2,1)S(1)} %bitcast.40), custom_call_target="tpu_custom_call" | custom-call | flops 4831838208 | bytes 4194304 | tf_op jit(solution)/shard_map/expert/pallas_call | solution.py:333
  219.1 4.4 %collective-permute-done.12 = bf16[128,4096]{1,0:T(8,128)(2,1)S(1)} collective-permute-done((bf16[128,4096]{1,0:T(8,128)(2,1)S(1)}, bf16[128,4096]{1,0:T(8,128)(2,1)S(1)}, u32[]{:S(2)}, u32[]{:S(2)}) %collective-permute-start.12) | collective-permute-done | bytes 1048608 | tf_op jit(solution)/shard_map/ppermute | solution.py:51
  223.4 1.3 collective-permute-done.13
  225.3 1.0 slice-done.4
  226.4 1.0 slice-done.5
  227.9 1.9 collective-permute-start.15
  229.8 24.2 %collective-permute-done.14 = bf16[256,4096]{1,0:T(8,128)(2,1)S(1)} collective-permute-done((bf16[256,4096]{1,0:T(8,128)(2,1)S(1)}, bf16[256,4096]{1,0:T(8,128)(2,1)S(1)}, u32[]{:S(2)}, u32[]{:S(2)}) %collective-permute-start.14) | collective-permute-done | bytes 2097184 | tf_op jit(solution)/shard_map/ppermute | solution.py:51
  253.9 1.5 collective-permute-done.15
  255.5 1.0 add_convert_fusion
  256.6 3.5 %collective-permute-start.16 = (bf16[64,4096]{1,0:T(8,128)(2,1)S(1)}, bf16[64,4096]{1,0:T(8,128)(2,1)S(1)}, u32[]{:S(2)}, u32[]{:S(2)}) collective-permute-start(bf16[64,4096]{1,0:T(8,128)(2,1)S(1)} %get-tuple-element.55), channel_id=1, source_target_pairs={{0,96},{32,0},{64,32},{96,64},{8,104},{40,8},{72,40},{104,72},{16,... | collective-permute-start | bytes 1572872 | tf_op jit(solution)/shard_map/ppermute | solution.py:51
  260.1 1.5 collective-permute-start.18
  261.7 10.8 %collective-permute-done.16 = bf16[64,4096]{1,0:T(8,128)(2,1)S(1)} collective-permute-done((bf16[64,4096]{1,0:T(8,128)(2,1)S(1)}, bf16[64,4096]{1,0:T(8,128)(2,1)S(1)}, u32[]{:S(2)}, u32[]{:S(2)}) %collective-permute-start.16) | collective-permute-done | bytes 524320 | tf_op jit(solution)/shard_map/ppermute | solution.py:51
  272.4 3.7 %collective-permute-done.17 = bf16[64,4096]{1,0:T(8,128)(2,1)S(1)} collective-permute-done((bf16[64,4096]{1,0:T(8,128)(2,1)S(1)}, bf16[64,4096]{1,0:T(8,128)(2,1)S(1)}, u32[]{:S(2)}, u32[]{:S(2)}) %collective-permute-start.17) | collective-permute-done | bytes 524320 | tf_op jit(solution)/shard_map/ppermute | solution.py:51
  276.4 12.8 %all_to_all.32 = bf16[8,8,4096]{2,1,0:T(8,128)(2,1)S(1)} all-to-all(bf16[8,8,4096]{2,1,0:T(8,128)(2,1)S(1)} %fusion.1), channel_id=1, replica_groups=mesh['seq'=16,'exp'=8] {'exp'}, dimensions={0} | all-to-all | bytes 1048576 | tf_op jit(solution)/shard_map/all_to_all | solution.py:585
  289.2 1.2 convolution_add_fusion
  (90 shorter events, 4.2 us)
Async XLA Ops:
  6.5 7.2 %copy-start.9 = (bf16[256,1024]{1,0:T(8,128)(2,1)S(1)}, bf16[256,1024]{1,0:T(8,128)(2,1)}, u32[]{:S(2)}) copy-start(bf16[256,1024]{1,0:T(8,128)(2,1)} %x_hbm.1) | copy-start | bytes 1572868
  6.5 84.6 %all-gather.3.cloned.1.call-start = ((), (), s32[]{:S(2)}) async-start(), calls=%async_computation.6 | async-start | bytes 8912896 | tf_op jit(solution)/shard_map/all_gather | solution.py:400
  8.0 29.1 %copy-start.17 = (f32[1024,16]{0,1:T(8,128)S(1)}, f32[1024,16]{0,1:T(8,128)}, u32[]{:S(2)}) copy-start(f32[1024,16]{0,1:T(8,128)} %param.23) | copy-start | bytes 196612
  8.0 35.9 %copy-start.10 = (bf16[256,1024]{1,0:T(8,128)(2,1)S(1)}, bf16[256,1024]{1,0:T(8,128)(2,1)}, u32[]{:S(2)}) copy-start(bf16[256,1024]{1,0:T(8,128)(2,1)} %proj_hbm.2) | copy-start | bytes 1572868
  8.0 35.9 %copy-start.14 = (f32[1024]{0:T(1024)S(1)}, f32[1024]{0:T(1024)}, u32[]{:S(2)}) copy-start(f32[1024]{0:T(1024)} %param.22) | copy-start | bytes 12292
  8.0 5.7 %collective-permute-start = (bf16[3,1024]{1,0:T(4,128)(2,1)S(1)}, bf16[3,1024]{1,0:T(4,128)(2,1)S(1)}, u32[]{:S(2)}, u32[]{:S(2)}) collective-permute-start(bf16[3,1024]{1,0:T(4,128)(2,1)S(1)} %slice.53), channel_id=1, source_target_pairs={{0,8},{8,16},{16,24},{24,32},{32,40},{40,48},{48,56},{56,64},{64,7... | collective-permute-start | bytes 18440 | tf_op jit(solution)/shard_map/ppermute | solution.py:57
  13.7 0.7 copy-start.12
  14.4 0.7 copy-start.13
  32.9 48.8 %copy-start.11 = (bf16[256,1024]{1,0:T(8,128)(2,1)S(1)}, bf16[256,1024]{1,0:T(8,128)(2,1)}, u32[]{:S(2)}) copy-start(bf16[256,1024]{1,0:T(8,128)(2,1)} %z_hbm.1) | copy-start | bytes 1572868
  32.9 48.8 %copy-start.15 = (f32[1024]{0:T(1024)S(1)}, f32[1024]{0:T(1024)}, u32[]{:S(2)}) copy-start(f32[1024]{0:T(1024)} %param.24) | copy-start | bytes 12292
  33.7 10.2 %all-to-all-start.1 = ((bf16[8,32,320]{2,1,0:T(8,128)(2,1)}), bf16[8,32,320]{2,1,0:T(8,128)(2,1)S(1)}, u32[]{:S(2)}, u32[]{:S(2)}) async-start(bf16[8,32,320]{2,1,0:T(8,128)(2,1)} %broadcast_in_dim.9), calls=%async_computation.1 | async-start | bytes 393216 | tf_op jit(solution)/shard_map/all_to_all | solution.py:431
  52.8 1.0 copy-start.5
  53.7 1.0 copy-start.7
  54.7 14.1 %all-to-all-start.2 = ((f32[16,2,1024]{2,1,0:T(2,128)}), f32[16,2,1024]{2,1,0:T(2,128)S(1)}, u32[]{:S(2)}, u32[]{:S(2)}) async-start(f32[16,2,1024]{2,1,0:T(2,128)} %get-tuple-element.27), calls=%async_computation.2 | async-start | bytes 262144 | tf_op jit(solution)/shard_map/all_to_all | solution.py:463
  69.5 12.1 %all-to-all-start.3 = ((f32[16,1,1024]{2,1,0:T(1,128)}), f32[16,1,1024]{2,1,0:T(1,128)S(1)}, u32[]{:S(2)}, u32[]{:S(2)}) async-start(f32[16,1,1024]{2,1,0:T(1,128)} %relay.1), calls=%async_computation.3 | async-start | bytes 131072 | tf_op jit(solution)/shard_map/all_to_all | solution.py:473
  81.6 1.2 copy-start.6
  82.9 1.2 copy-start.8
  91.1 3.4 %copy-start.1 = (bf16[16384,256]{1,0:T(8,128)(2,1)S(1)}, bf16[16384,256]{1,0:T(8,128)(2,1)}, u32[]{:S(2)}) copy-start(bf16[16384,256]{1,0:T(8,128)(2,1)} %all-gather.3.cloned.1.call-done) | copy-start | bytes 25165828
  94.5 7.9 %copy-start.18 = (s32[32,2]{0,1:T(2,128)S(1)}, s32[32,2]{0,1:T(2,128)}, u32[]{:S(2)}) copy-start(s32[32,2]{0,1:T(2,128)} %param.27) | copy-start | bytes 772
  94.5 16.3 %copy-start.19 = (f32[32,2]{0,1:T(2,128)S(1)}, f32[32,2]{0,1:T(2,128)}, u32[]{:S(2)}) copy-start(f32[32,2]{0,1:T(2,128)} %param.28) | copy-start | bytes 772
  94.5 28.8 %copy-start.16 = (bf16[32,4096]{1,0:T(8,128)(2,1)S(1)}, bf16[32,4096]{1,0:T(8,128)(2,1)}, u32[]{:S(2)}) copy-start(bf16[32,4096]{1,0:T(8,128)(2,1)} %param.26) | copy-start | bytes 786436
  94.5 61.7 %slice-start.2 = ((s8[6291456]{0:T(1024)(128)(4,1)}), s8[2097152]{0:T(1024)(128)(4,1)S(1)}, s32[]{:S(2)}) async-start(s8[6291456]{0:T(1024)(128)(4,1)} %bitcast.31), calls=%async_computation.9 | async-start | bytes 4194304
  101.1 1.3 copy-start.4
  102.4 2.9 collective-permute-start.1
  105.3 50.9 %slice-start = ((s8[6291456]{0:T(1024)(128)(4,1)}), s8[4194304]{0:T(1024)(128)(4,1)S(1)}, s32[]{:S(2)}) async-start(s8[6291456]{0:T(1024)(128)(4,1)} %bitcast.25), calls=%async_computation.7 | async-start | bytes 8388608
  105.3 50.9 %slice-start.3 = ((s8[6291456]{0:T(1024)(128)(4,1)}), s8[4194304]{0:T(1024)(128)(4,1)S(1)}, s32[]{:S(2)}) async-start(s8[6291456]{0:T(1024)(128)(4,1)} %bitcast.31), calls=%async_computation.10 | async-start | bytes 8388608
  107.4 15.2 %collective-permute-start.2 = (bf16[32,4096]{1,0:T(8,128)(2,1)S(1)}, bf16[32,4096]{1,0:T(8,128)(2,1)S(1)}, u32[]{:S(2)}, u32[]{:S(2)}) collective-permute-start(bf16[32,4096]{1,0:T(8,128)(2,1)S(1)} %get-tuple-element.60), channel_id=1, source_target_pairs={{0,2},{1,3},{2,4},{3,5},{4,6},{5,7},{6,0},{7,1},{8,10},{9,11},{10,... | collective-permute-start | bytes 786440 | tf_op jit(solution)/shard_map/ppermute | solution.py:531
  108.0 14.6 %collective-permute-start.3 = (bf16[32,4096]{1,0:T(8,128)(2,1)S(1)}, bf16[32,4096]{1,0:T(8,128)(2,1)S(1)}, u32[]{:S(2)}, u32[]{:S(2)}) collective-permute-start(bf16[32,4096]{1,0:T(8,128)(2,1)S(1)} %get-tuple-element.62), channel_id=1, source_target_pairs={{0,4},{1,5},{2,6},{3,7},{4,0},{5,1},{6,2},{7,3},{8,12},{9,13},{10,... | collective-permute-start | bytes 786440 | tf_op jit(solution)/shard_map/ppermute | solution.py:531
  110.1 13.2 %collective-permute-start.4 = (bf16[32,4096]{1,0:T(8,128)(2,1)S(1)}, bf16[32,4096]{1,0:T(8,128)(2,1)S(1)}, u32[]{:S(2)}, u32[]{:S(2)}) collective-permute-start(bf16[32,4096]{1,0:T(8,128)(2,1)S(1)} %get-tuple-element.61), channel_id=1, source_target_pairs={{0,6},{1,7},{2,0},{3,1},{4,2},{5,3},{6,4},{7,5},{8,14},{9,15},{10,... | collective-permute-start | bytes 786440 | tf_op jit(solution)/shard_map/ppermute | solution.py:531
  123.3 32.9 %slice-start.1 = ((s8[6291456]{0:T(1024)(128)(4,1)}), s8[2097152]{0:T(1024)(128)(4,1)S(1)}, s32[]{:S(2)}) async-start(s8[6291456]{0:T(1024)(128)(4,1)} %bitcast.25), calls=%async_computation.8 | async-start | bytes 4194304
  137.8 16.0 %collective-permute-start.5 = (bf16[64,4096]{1,0:T(8,128)(2,1)S(1)}, bf16[64,4096]{1,0:T(8,128)(2,1)S(1)}, u32[]{:S(2)}, u32[]{:S(2)}) collective-permute-start(bf16[64,4096]{1,0:T(8,128)(2,1)S(1)} %bitcast.49), channel_id=1, source_target_pairs={{0,32},{32,64},{64,96},{96,0},{8,40},{40,72},{72,104},{104,8},{16,... | collective-permute-start | bytes 1572872 | tf_op jit(solution)/shard_map/ppermute | solution.py:51
  138.2 15.7 %collective-permute-start.6 = (bf16[64,4096]{1,0:T(8,128)(2,1)S(1)}, bf16[64,4096]{1,0:T(8,128)(2,1)S(1)}, u32[]{:S(2)}, u32[]{:S(2)}) collective-permute-start(bf16[64,4096]{1,0:T(8,128)(2,1)S(1)} %bitcast.50), channel_id=1, source_target_pairs={{0,96},{32,0},{64,32},{96,64},{8,104},{40,8},{72,40},{104,72},{16,... | collective-permute-start | bytes 1572872 | tf_op jit(solution)/shard_map/ppermute | solution.py:51
  141.1 12.8 %collective-permute-start.7 = (bf16[64,4096]{1,0:T(8,128)(2,1)S(1)}, bf16[64,4096]{1,0:T(8,128)(2,1)S(1)}, u32[]{:S(2)}, u32[]{:S(2)}) collective-permute-start(bf16[64,4096]{1,0:T(8,128)(2,1)S(1)} %bitcast.51), channel_id=1, source_target_pairs={{0,64},{32,96},{64,0},{96,32},{8,72},{40,104},{72,8},{104,40},{16,... | collective-permute-start | bytes 1572872 | tf_op jit(solution)/shard_map/ppermute | solution.py:51
  154.1 26.1 %collective-permute-start.8 = (bf16[256,4096]{1,0:T(8,128)(2,1)S(1)}, bf16[256,4096]{1,0:T(8,128)(2,1)S(1)}, u32[]{:S(2)}, u32[]{:S(2)}) collective-permute-start(bf16[256,4096]{1,0:T(8,128)(2,1)S(1)} %pad_maximum_fusion.rows_ref), channel_id=1, source_target_pairs={{0,8},{8,16},{16,24},{24,0},{32,40},{40,48},{48,56},{56,32},{64,72... | collective-permute-start | bytes 6291464 | tf_op jit(solution)/shard_map/ppermute | solution.py:51
  156.2 27.2 %collective-permute-start.9 = (bf16[256,4096]{1,0:T(8,128)(2,1)S(1)}, bf16[256,4096]{1,0:T(8,128)(2,1)S(1)}, u32[]{:S(2)}, u32[]{:S(2)}) collective-permute-start(bf16[256,4096]{1,0:T(8,128)(2,1)S(1)} %pad_maximum_fusion.rows_ref), channel_id=1, source_target_pairs={{0,24},{8,0},{16,8},{24,16},{32,56},{40,32},{48,40},{56,48},{64,88... | collective-permute-start | bytes 6291464 | tf_op jit(solution)/shard_map/ppermute | solution.py:51
  156.2 2.8 copy-start
  183.5 14.9 %collective-permute-start.10 = (bf16[128,4096]{1,0:T(8,128)(2,1)S(1)}, bf16[128,4096]{1,0:T(8,128)(2,1)S(1)}, u32[]{:S(2)}, u32[]{:S(2)}) collective-permute-start(bf16[128,4096]{1,0:T(8,128)(2,1)S(1)} %slice.60), channel_id=1, source_target_pairs={{0,8},{8,16},{16,24},{24,0},{32,40},{40,48},{48,56},{56,32},{64,72... | collective-permute-start | bytes 3145736 | tf_op jit(solution)/shard_map/ppermute | solution.py:51
  183.7 16.1 %collective-permute-start.11 = (bf16[128,4096]{1,0:T(8,128)(2,1)S(1)}, bf16[128,4096]{1,0:T(8,128)(2,1)S(1)}, u32[]{:S(2)}, u32[]{:S(2)}) collective-permute-start(bf16[128,4096]{1,0:T(8,128)(2,1)S(1)} %slice.61), channel_id=1, source_target_pairs={{0,24},{8,0},{16,8},{24,16},{32,56},{40,32},{48,40},{56,48},{64,88... | collective-permute-start | bytes 3145736 | tf_op jit(solution)/shard_map/ppermute | solution.py:51
  194.2 30.6 %copy-start.2 = (bf16[256,4096]{1,0:T(8,128)(2,1)}, bf16[256,4096]{1,0:T(8,128)(2,1)S(1)}, u32[]{:S(2)}) copy-start(bf16[256,4096]{1,0:T(8,128)(2,1)S(1)} %expert.5) | copy-start | bytes 6291460
  208.6 14.9 %collective-permute-start.12 = (bf16[128,4096]{1,0:T(8,128)(2,1)S(1)}, bf16[128,4096]{1,0:T(8,128)(2,1)S(1)}, u32[]{:S(2)}, u32[]{:S(2)}) collective-permute-start(bf16[128,4096]{1,0:T(8,128)(2,1)S(1)} %get-tuple-element.59), channel_id=1, source_target_pairs={{0,8},{8,16},{16,24},{24,0},{32,40},{40,48},{48,56},{56,32},{64,72... | collective-permute-start | bytes 3145736 | tf_op jit(solution)/shard_map/ppermute | solution.py:51
  208.7 16.1 %collective-permute-start.13 = (bf16[128,4096]{1,0:T(8,128)(2,1)S(1)}, bf16[128,4096]{1,0:T(8,128)(2,1)S(1)}, u32[]{:S(2)}, u32[]{:S(2)}) collective-permute-start(bf16[128,4096]{1,0:T(8,128)(2,1)S(1)} %get-tuple-element.58), channel_id=1, source_target_pairs={{0,24},{8,0},{16,8},{24,16},{32,56},{40,32},{48,40},{56,48},{64,88... | collective-permute-start | bytes 3145736 | tf_op jit(solution)/shard_map/ppermute | solution.py:51
  219.1 5.9 %copy-start.3 = (bf16[256,4096]{1,0:T(8,128)(2,1)}, bf16[256,4096]{1,0:T(8,128)(2,1)S(1)}, u32[]{:S(2)}) copy-start(bf16[256,4096]{1,0:T(8,128)(2,1)S(1)} %expert.7) | copy-start | bytes 6291460
  225.0 1.2 slice-start.4
  226.2 1.2 slice-start.5
  227.7 26.3 %collective-permute-start.14 = (bf16[256,4096]{1,0:T(8,128)(2,1)S(1)}, bf16[256,4096]{1,0:T(8,128)(2,1)S(1)}, u32[]{:S(2)}, u32[]{:S(2)}) collective-permute-start(bf16[256,4096]{1,0:T(8,128)(2,1)S(1)} %pad_maximum_fusion.2), channel_id=1, source_target_pairs={{0,8},{8,16},{16,24},{24,0},{32,40},{40,48},{48,56},{56,32},{64,72... | collective-permute-start | bytes 6291464 | tf_op jit(solution)/shard_map/ppermute | solution.py:51
  227.9 27.6 %collective-permute-start.15 = (bf16[256,4096]{1,0:T(8,128)(2,1)S(1)}, bf16[256,4096]{1,0:T(8,128)(2,1)S(1)}, u32[]{:S(2)}, u32[]{:S(2)}) collective-permute-start(bf16[256,4096]{1,0:T(8,128)(2,1)S(1)} %pad_maximum_fusion.3), channel_id=1, source_target_pairs={{0,24},{8,0},{16,8},{24,16},{32,56},{40,32},{48,40},{56,48},{64,88... | collective-permute-start | bytes 6291464 | tf_op jit(solution)/shard_map/ppermute | solution.py:51
  256.6 15.8 %collective-permute-start.16 = (bf16[64,4096]{1,0:T(8,128)(2,1)S(1)}, bf16[64,4096]{1,0:T(8,128)(2,1)S(1)}, u32[]{:S(2)}, u32[]{:S(2)}) collective-permute-start(bf16[64,4096]{1,0:T(8,128)(2,1)S(1)} %get-tuple-element.55), channel_id=1, source_target_pairs={{0,96},{32,0},{64,32},{96,64},{8,104},{40,8},{72,40},{104,72},{16,... | collective-permute-start | bytes 1572872 | tf_op jit(solution)/shard_map/ppermute | solution.py:51
  260.1 16.0 %collective-permute-start.17 = (bf16[64,4096]{1,0:T(8,128)(2,1)S(1)}, bf16[64,4096]{1,0:T(8,128)(2,1)S(1)}, u32[]{:S(2)}, u32[]{:S(2)}) collective-permute-start(bf16[64,4096]{1,0:T(8,128)(2,1)S(1)} %get-tuple-element.57), channel_id=1, source_target_pairs={{0,32},{32,64},{64,96},{96,0},{8,40},{40,72},{72,104},{104,8},{16,... | collective-permute-start | bytes 1572872 | tf_op jit(solution)/shard_map/ppermute | solution.py:51
  260.1 16.0 %collective-permute-start.18 = (bf16[64,4096]{1,0:T(8,128)(2,1)S(1)}, bf16[64,4096]{1,0:T(8,128)(2,1)S(1)}, u32[]{:S(2)}, u32[]{:S(2)}) collective-permute-start(bf16[64,4096]{1,0:T(8,128)(2,1)S(1)} %get-tuple-element.56), channel_id=1, source_target_pairs={{0,64},{32,96},{64,0},{96,32},{8,72},{40,104},{72,8},{104,40},{16,... | collective-permute-start | bytes 1572872 | tf_op jit(solution)/shard_map/ppermute | solution.py:51
Sparse Core Ops, SparseCore 0:
  9.5 74.7 all-gather.2
where the time goes:
time: 301 us; the launch traced here: 297 us
  waiting for transfers between devices  116 us (39%)
  Pallas kernels  60.3 us (20%)
  blocking collectives  40.8 us (14%)
  starting transfers between devices  39.9 us (13%)
  local copies, waits for them, and re-layouts  19.3 us (6%)
  between operations  13.9 us (5%)
  other arithmetic  5.64 us (2%)
    ppermute x14, waiting for transfers between devices, along(): return lax.ppermute(block, ('seq', 'exp'), route)  80.2 us
    pallas_call x4, Pallas kernels, expert(): pl.pallas_call(expert_kernel, out_shape=jax.ShapeDtypeStruct((count, feat...  33.5 us
    ppermute x14, starting transfers between devices, along(): return lax.ppermute(block, ('seq', 'exp'), route)  16.7 us
    unnamed x51, local copies, waits for them, and re-layouts  14.8 us
    all_to_all x1, blocking collectives, mixer(): lax.all_to_all(partial.reshape(owners, length // owners, -1), 'exp', spli...  14.1 us
    all_to_all x1, blocking collectives, shards(): lax.all_to_all(outgoing, 'exp', split_axis=0, concat_axis=0, tiled=True)  13.9 us
    all_to_all x1, blocking collectives, shards(): lax.all_to_all(expert_out, 'exp', split_axis=0, concat_axis=0, tiled=True)  12.8 us
    ppermute x3, waiting for transfers between devices, mixer(): lax.ppermute(sums[hop].astype(BF16), 'exp', route).astype(F32)  12.4 us
  transfers between devices with their start and end apart: 23, of which 18 were waited for; matrix products, arithmetic and copies ran while one was open for 1% of the time, Pallas kernels for 15%

commit v1 on v0

--- a/solution.py
+++ b/solution.py
@@ -102,8 +102,11 @@
 
     lax.fori_loop(0, steps, step, 0)
     copies[3].wait()
-    part_ref[...] = jnp.dot(
-        mixed_ref[...].astype(BF16), proj_ref[...], preferred_element_type=F32
+    part_ref[...] = lax.dot_general(
+        mixed_ref[...].astype(BF16),
+        proj_ref[...],
+        (((1,), (1,)), ((), ())),
+        preferred_element_type=F32,
     )
 
 
@@ -306,8 +309,9 @@
     lax.fori_loop(0, parts, product, 0)
 
 
-def expert_kernel(rows_ref, gate_ref, up_ref, down_ref, out_ref, inner):
+def expert_kernel(rows_ref, gate_ref, up_ref, down_ref, first_ref, second_ref, inner):
     tile = 256
+    middle = first_ref.shape[0]
 
     def widen(part, carry):
         columns = pl.ds(pl.multiple_of(part * tile, tile), tile)
@@ -321,10 +325,11 @@
     def narrow(part, carry):
         columns = pl.ds(pl.multiple_of(part * tile, tile), tile)
         piece = jnp.dot(inner[...], down_ref[:, columns], preferred_element_type=F32)
-        out_ref[:, columns] = piece.astype(BF16)
+        first_ref[:, columns] = piece[:middle].astype(BF16)
+        second_ref[:, columns] = piece[middle:].astype(BF16)
         return carry
 
-    lax.fori_loop(0, out_ref.shape[1] // tile, narrow, 0)
+    lax.fori_loop(0, first_ref.shape[1] // tile, narrow, 0)
 
 
 def expert(rows, gate, up, down):
@@ -332,9 +337,9 @@
     hidden = gate.shape[1]
     return pl.pallas_call(
         expert_kernel,
-        out_shape=jax.ShapeDtypeStruct((count, features), BF16),
+        out_shape=(jax.ShapeDtypeStruct((count // 2, features), BF16),) * 2,
         in_specs=[whole()] * 4,
-        out_specs=whole(),
+        out_specs=[whole()] * 2,
         scratch_shapes=[pltpu.VMEM((count, hidden), BF16)],
         compiler_params=params(12),
         cost_estimate=pl.CostEstimate(
@@ -370,25 +375,19 @@
     behind, ahead, own_out = lax.optimization_barrier((behind, ahead, own_out))
     far_first = along(halves(behind)[0], 1, 1)
     far_second = along(halves(ahead)[1], 1, -1)
-    behind_out = run(behind)
-    far_first, far_second, behind_out = lax.optimization_barrier((far_first, far_second, behind_out))
-    far_out = run(jnp.concatenate([far_first, far_second], axis=0))
-    first, second = halves(far_out)
-    from_behind = along(first, 1, 1)
-    from_ahead = along(second, 1, -1)
-    ahead_out = run(ahead)
-    from_behind, from_ahead, ahead_out = lax.optimization_barrier(
-        (from_behind, from_ahead, ahead_out)
-    )
-    ahead_first, ahead_second = halves(ahead_out)
-    behind_first, behind_second = halves(behind_out)
-    ahead_sum = jnp.concatenate([added(ahead_first, from_behind), ahead_second], axis=0)
-    behind_sum = jnp.concatenate([behind_first, added(behind_second, from_ahead)], axis=0)
-    ahead_sum, behind_sum = lax.optimization_barrier((ahead_sum, behind_sum))
-    from_behind = along(ahead_sum, 1, 1)
-    from_ahead = along(behind_sum, 1, -1)
-    total = added(own_out, from_behind, from_ahead)
-    kept, behind, ahead, across = jnp.split(total, 4, axis=0)
+    behind_first, behind_second = run(behind)
+    early_first = along(behind_first, 1, -1)
+    ahead_first, ahead_second = run(ahead)
+    early_second = along(ahead_second, 1, 1)
+    far_first, far_second, behind_second, ahead_first = lax.optimization_barrier(
+        (far_first, far_second, behind_second, ahead_first)
+    )
+    across_first, across_second = run(jnp.concatenate([far_first, far_second], axis=0))
+    late_first = along(added(ahead_first, along(across_first, 1, 1)), 1, 1)
+    late_second = along(added(behind_second, along(across_second, 1, -1)), 1, -1)
+    first = added(own_out[0], early_first, late_first)
+    second = added(own_out[1], early_second, late_second)
+    (kept, behind), (ahead, across) = halves(first), halves(second)
     return added(kept, along(behind, 0, -1), along(ahead, 0, 1), along(across, 0, 2))
 
 
@@ -412,13 +411,13 @@
             pltpu.VMEM(x_in.shape, BF16),
             pltpu.VMEM(conv_weight.shape, F32),
             pltpu.VMEM((1, channels), F32),
-            pltpu.VMEM(x_proj.shape, BF16),
+            pltpu.VMEM(x_proj.shape[::-1], BF16),
             pltpu.VMEM((channels // LANES, length + 8, LANES), F32),
             pltpu.SemaphoreType.DMA((4,)),
         ],
         compiler_params=params(12),
         name="conv",
-    )(x_in, conv_weight, conv_bias[None, :], x_proj, rim)
+    )(x_in, conv_weight, conv_bias[None, :], x_proj.T, rim)
     share = lax.all_to_all(
         partial.reshape(owners, length // owners, -1), "exp", split_axis=0, concat_axis=0, tiled=True
     )
@@ -519,7 +518,7 @@
             pltpu.VMEM((seqs, channels, width), BF16),
             pltpu.SemaphoreType.DMA((seqs,)),
         ],
-        compiler_params=params(14),
+        compiler_params=params(50),
         name="outward",
     )(gated, columns)
     swap = [(e, e + 1 - 2 * (e % 2)) for e in range(owners)]

time: 301 us -> 303 us (level)
  starting transfers between devices: 39.9 us -> 45.3 us
  local copies, waits for them, and re-layouts: 19.3 us -> 15.5 us
    ppermute x14 -> x16, starting transfers between devices: 16.7 us -> 22.3 us  [along(): return lax.ppermute(block, ('seq', 'exp'), route)]
    unnamed x51 -> x50, local copies, waits for them, and re-layouts: 14.8 us -> 13.2 us
    ppermute x14 -> x16, waiting for transfers between devices: 80.2 us -> 81.5 us  [along(): return lax.ppermute(block, ('seq', 'exp'), route)]
  transfers between devices with their start and end apart: 23 -> 25, of which waited for: 18 -> 17; matrix products, arithmetic and copies ran while one was open for 1% -> 1% of each run, Pallas kernels for 15% -> 15%
where the time goes in v1:
time: 303 us; the launch traced here: 302 us
  waiting for transfers between devices  119 us (39%)
  Pallas kernels  61 us (20%)
  starting transfers between devices  45.3 us (15%)
  blocking collectives  40.8 us (13%)
  local copies, waits for them, and re-layouts  15.5 us (5%)
  between operations  13.8 us (5%)
  other arithmetic  5.18 us (2%)
    ppermute x16, waiting for transfers between devices, along(): return lax.ppermute(block, ('seq', 'exp'), route)  81.5 us
    pallas_call x4, Pallas kernels, expert(): pl.pallas_call(expert_kernel, out_shape=(jax.ShapeDtypeStruct((count // 2...  33.5 us
    ppermute x16, starting transfers between devices, along(): return lax.ppermute(block, ('seq', 'exp'), route)  22.3 us
    all_to_all x1, blocking collectives, mixer(): lax.all_to_all(partial.reshape(owners, length // owners, -1), 'exp', spli...  14.1 us
    all_to_all x1, blocking collectives, shards(): lax.all_to_all(outgoing, 'exp', split_axis=0, concat_axis=0, tiled=True)  13.9 us
    unnamed x50, local copies, waits for them, and re-layouts  13.2 us
    all_to_all x1, blocking collectives, shards(): lax.all_to_all(expert_out, 'exp', split_axis=0, concat_axis=0, tiled=True)  12.8 us
    ppermute x3, waiting for transfers between devices, mixer(): lax.ppermute(sums[hop].astype(BF16), 'exp', route).astype(F32)  12.3 us
  transfers between devices with their start and end apart: 25, of which 17 were waited for; matrix products, arithmetic and copies ran while one was open for 1% of the time, Pallas kernels for 15%

profile of v1, /device:TPU:24, one launch (start us, length us, event | category | flops | bytes accessed | tf_op | source)
XLA Modules:
  0.0 301.7 jit_solution(8110405024999103955)
XLA Ops:
  6.5 0.7 all-gather.3.cloned.1.call-update
  7.3 0.7 slice.47
  8.0 3.0 %collective-permute-start = (bf16[3,1024]{1,0:T(4,128)(2,1)S(1)}, bf16[3,1024]{1,0:T(4,128)(2,1)S(1)}, u32[]{:S(2)}, u32[]{:S(2)}) collective-permute-start(bf16[3,1024]{1,0:T(4,128)(2,1)S(1)} %slice.47), channel_id=1, source_target_pairs={{0,8},{8,16},{16,24},{24,32},{32,40},{40,48},{48,56},{56,64},{64,7... | collective-permute-start | bytes 18440 | tf_op jit(solution)/shard_map/ppermute | solution.py:57
  11.0 2.5 collective-permute-done.rim_ref
  13.5 1.1 copy-done.6
  14.6 1.0 copy-done.7
  15.6 0.7 copy-done.12
  16.3 0.7 copy-done.13
  17.0 3.8 %conv.1 = (f32[256,1024]{1,0:T(8,128)S(1)}, f32[256,288]{1,0:T(8,128)S(1)}) custom-call(bf16[256,1024]{1,0:T(8,128)(2,1)S(1)} %copy-done.7, f32[4,1024]{1,0:T(4,128)S(1)} %copy-done.12, f32[1,1024]{1,0:T(1,128)S(1)} %bitcast.47, bf16[288,1024]{1,0:T(8,128)(2,1)S(1)} %bitcast.44, bf16[3,1024]{1,0:T(4,128)(2,1)S(1)} %collective-permute-done.rim_ref), custom_call_target="tpu_custom_call" | custom-call | tf_op jit(solution)/shard_map/conv/pallas_call | solution.py:402
  20.8 14.1 %all_to_all.30 = f32[8,32,288]{2,1,0:T(8,128)S(1)} all-to-all(f32[8,32,288]{2,1,0:T(8,128)S(1)} %bitcast.45), channel_id=1, replica_groups=mesh['seq'=16,'exp'=8] {'exp'}, dimensions={0} | all-to-all | bytes 589824 | tf_op jit(solution)/shard_map/all_to_all | solution.py:421
  35.0 0.7 broadcast_in_dim.9
  35.7 3.4 %all-to-all-start.1 = ((bf16[8,32,320]{2,1,0:T(8,128)(2,1)}), bf16[8,32,320]{2,1,0:T(8,128)(2,1)S(1)}, u32[]{:S(2)}, u32[]{:S(2)}) async-start(bf16[8,32,320]{2,1,0:T(8,128)(2,1)} %broadcast_in_dim.9), calls=%async_computation.1 | async-start | bytes 393216 | tf_op jit(solution)/shard_map/all_to_all | solution.py:430
  39.2 6.7 %all-to-all-done.1 = bf16[8,32,320]{2,1,0:T(8,128)(2,1)S(1)} async-done(((bf16[8,32,320]{2,1,0:T(8,128)(2,1)}), bf16[8,32,320]{2,1,0:T(8,128)(2,1)S(1)}, u32[]{:S(2)}, u32[]{:S(2)}) %all-to-all-start.1) | async-done | bytes 163872 | tf_op jit(solution)/shard_map/all_to_all | solution.py:430
  45.9 8.9 %scan.1 = (f32[256,1024]{1,0:T(8,128)S(1)}, f32[256,1024]{1,0:T(8,128)S(1)}, f32[8,1024]{1,0:T(8,128)S(1)}, f32[16,8,1024]{2,1,0:T(8,128)S(1)}, f32[16,2,1024]{2,1,0:T(2,128)}) custom-call(bf16[256,320]{1,0:T(8,128)(2,1)S(1)} %bitcast.42, f32[256,1024]{1,0:T(8,128)S(1)} %get-tuple-element.31.mixed_ref, f32[16,1024]{1,0:T(8,128)S(1)} %multiply_bitcast_fusion.rates_ref, ...), custom_call_target="tpu_custom_call" | custom-call | tf_op jit(solution)/shard_map/scan/pallas_call | solution.py:437
  54.8 1.0 copy-done.2
  55.8 1.0 copy-done.4
  56.7 7.2 %all-to-all-start.2 = ((f32[16,2,1024]{2,1,0:T(2,128)}), f32[16,2,1024]{2,1,0:T(2,128)S(1)}, u32[]{:S(2)}, u32[]{:S(2)}) async-start(f32[16,2,1024]{2,1,0:T(2,128)} %get-tuple-element.32), calls=%async_computation.2 | async-start | bytes 262144 | tf_op jit(solution)/shard_map/all_to_all | solution.py:462
  63.9 6.9 %all-to-all-done.2.ends_ref = f32[16,2,1024]{2,1,0:T(2,128)S(1)} async-done(((f32[16,2,1024]{2,1,0:T(2,128)}), f32[16,2,1024]{2,1,0:T(2,128)S(1)}, u32[]{:S(2)}, u32[]{:S(2)}) %all-to-all-start.2) | async-done | bytes 131104 | tf_op jit(solution)/shard_map/all_to_all | solution.py:462
  70.8 0.7 relay.1
  71.5 6.0 %all-to-all-start.3 = ((f32[16,1,1024]{2,1,0:T(1,128)}), f32[16,1,1024]{2,1,0:T(1,128)S(1)}, u32[]{:S(2)}, u32[]{:S(2)}) async-start(f32[16,1,1024]{2,1,0:T(1,128)} %relay.1), calls=%async_computation.3 | async-start | bytes 131072 | tf_op jit(solution)/shard_map/all_to_all | solution.py:472
  77.6 6.0 %all-to-all-done.3 = f32[16,1,1024]{2,1,0:T(1,128)S(1)} async-done(((f32[16,1,1024]{2,1,0:T(1,128)}), f32[16,1,1024]{2,1,0:T(1,128)S(1)}, u32[]{:S(2)}, u32[]{:S(2)}) %all-to-all-start.3) | async-done | bytes 65568 | tf_op jit(solution)/shard_map/all_to_all | solution.py:472
  83.7 1.2 copy-done.3
  84.9 1.2 copy-done.5
  86.1 1.0 copy-done.11
  87.1 7.0 %finish.1.gated_ref = bf16[256,1024]{1,0:T(8,128)(2,1)S(1)} custom-call(s32[8]{0:T(128)S(1)} %pad_add_fusion.order_ref, f32[16,1024]{1,0:T(8,128)S(1)} %bitcast.46, f32[16,1024]{1,0:T(8,128)S(1)} %multiply_bitcast_fusion.rates_ref, f32[256,1024]{1,0:T(8,128)S(1)} %copy-done.5, bf16[256,320]{1,0:T(8,128)(2,1)S(1)} %bitcast.43, f32[256,1024]{1,0:T(8,128)S(1)} %copy-done.3, ...), custom_call_target="tpu_custom_call" | custom-call | tf_op jit(solution)/shard_map/finish/pallas_call | solution.py:477
  94.2 7.1 %outward.1 = (bf16[128,4096]{1,0:T(8,128)(2,1)}, f32[128,4096]{1,0:T(8,128)S(1)}) custom-call(bf16[256,1024]{1,0:T(8,128)(2,1)S(1)} %finish.1.gated_ref, bf16[16,1024,256]{2,1,0:T(8,128)(2,1)} %bitcast.50), custom_call_target="tpu_custom_call" | custom-call | tf_op jit(solution)/shard_map/outward/pallas_call | solution.py:509
  101.4 1.3 copy-done.1
  103.7 1.9 collective-permute-done.1
  105.6 2.1 fusion.14
  107.7 0.6 collective-permute-start.2
  108.4 2.0 collective-permute-start.3
  110.4 0.7 collective-permute-start.4
  111.2 11.7 %collective-permute-done.2 = bf16[32,4096]{1,0:T(8,128)(2,1)S(1)} collective-permute-done((bf16[32,4096]{1,0:T(8,128)(2,1)S(1)}, bf16[32,4096]{1,0:T(8,128)(2,1)S(1)}, u32[]{:S(2)}, u32[]{:S(2)}) %collective-permute-start.2) | collective-permute-done | bytes 262176 | tf_op jit(solution)/shard_map/ppermute | solution.py:530
  123.0 0.6 collective-permute-done.4
  124.2 13.9 %all_to_all.31 = bf16[8,8,4096]{2,1,0:T(8,128)(2,1)S(1)} all-to-all(bf16[8,8,4096]{2,1,0:T(8,128)(2,1)S(1)} %fusion), channel_id=1, replica_groups=mesh['seq'=16,'exp'=8] {'exp'}, dimensions={0} | all-to-all | bytes 1048576 | tf_op jit(solution)/shard_map/all_to_all | solution.py:581
  138.5 2.9 collective-permute-start.6
  141.4 12.8 %collective-permute-done.5 = bf16[64,4096]{1,0:T(8,128)(2,1)S(1)} collective-permute-done((bf16[64,4096]{1,0:T(8,128)(2,1)S(1)}, bf16[64,4096]{1,0:T(8,128)(2,1)S(1)}, u32[]{:S(2)}, u32[]{:S(2)}) %collective-permute-start.5) | collective-permute-done | bytes 524320 | tf_op jit(solution)/shard_map/ppermute | solution.py:51
  154.4 2.1 collective-permute-start.8
  156.5 2.8 copy-done
  159.3 8.4 %expert.4 = (bf16[128,4096]{1,0:T(8,128)(2,1)S(1)}, bf16[128,4096]{1,0:T(8,128)(2,1)S(1)}) custom-call(bf16[256,4096]{1,0:T(8,128)(2,1)S(1)} %pad_maximum_fusion.rows_ref, bf16[4096,768]{1,0:T(8,128)(2,1)S(1)} %bitcast.28, bf16[4096,768]{1,0:T(8,128)(2,1)S(1)} %bitcast.34, bf16[768,4096]{1,0:T(8,128)(2,1)S(1)} %bitcast.38), custom_call_target="tpu_custom_call" | custom-call | flops 4831838208 | bytes 4194304 | tf_op jit(solution)/shard_map/expert/pallas_call | solution.py:338
  167.7 12.8 %collective-permute-done.8.rows_ref = bf16[256,4096]{1,0:T(8,128)(2,1)S(1)} collective-permute-done((bf16[256,4096]{1,0:T(8,128)(2,1)S(1)}, bf16[256,4096]{1,0:T(8,128)(2,1)S(1)}, u32[]{:S(2)}, u32[]{:S(2)}) %collective-permute-start.8) | collective-permute-done | bytes 2097184 | tf_op jit(solution)/shard_map/ppermute | solution.py:51
  180.5 3.2 %collective-permute-done.9.rows_ref = bf16[256,4096]{1,0:T(8,128)(2,1)S(1)} collective-permute-done((bf16[256,4096]{1,0:T(8,128)(2,1)S(1)}, bf16[256,4096]{1,0:T(8,128)(2,1)S(1)}, u32[]{:S(2)}, u32[]{:S(2)}) %collective-permute-start.9) | collective-permute-done | bytes 2097184 | tf_op jit(solution)/shard_map/ppermute | solution.py:51
  184.0 2.1 collective-permute-start.12
  186.1 8.4 %expert.5 = (bf16[128,4096]{1,0:T(8,128)(2,1)S(1)}, bf16[128,4096]{1,0:T(8,128)(2,1)S(1)}) custom-call(bf16[256,4096]{1,0:T(8,128)(2,1)S(1)} %collective-permute-done.8.rows_ref, bf16[4096,768]{1,0:T(8,128)(2,1)S(1)} %bitcast.29, bf16[4096,768]{1,0:T(8,128)(2,1)S(1)} %bitcast.35, bf16[768,4096]{1,0:T(8,128)(2,1)S(1)} %bitcast.39), custom_call_target="tpu_custom_call" | custom-call | flops 4831838208 | bytes 4194304 | tf_op jit(solution)/shard_map/expert/pallas_call | solution.py:338
  194.5 8.4 %expert.6 = (bf16[128,4096]{1,0:T(8,128)(2,1)S(1)}, bf16[128,4096]{1,0:T(8,128)(2,1)S(1)}) custom-call(bf16[256,4096]{1,0:T(8,128)(2,1)S(1)} %collective-permute-done.9.rows_ref, bf16[4096,768]{1,0:T(8,128)(2,1)S(1)} %bitcast.30, bf16[4096,768]{1,0:T(8,128)(2,1)S(1)} %bitcast.36, bf16[768,4096]{1,0:T(8,128)(2,1)S(1)} %bitcast.40), custom_call_target="tpu_custom_call" | custom-call | flops 4831838208 | bytes 4194304 | tf_op jit(solution)/shard_map/expert/pallas_call | solution.py:338
  203.1 8.4 %expert.7 = (bf16[128,4096]{1,0:T(8,128)(2,1)S(1)}, bf16[128,4096]{1,0:T(8,128)(2,1)S(1)}) custom-call(bf16[256,4096]{1,0:T(8,128)(2,1)S(1)} %pad_maximum_fusion.1.rows_ref, bf16[4096,768]{1,0:T(8,128)(2,1)S(1)} %bitcast.31, bf16[4096,768]{1,0:T(8,128)(2,1)S(1)} %bitcast.37, bf16[768,4096]{1,0:T(8,128)(2,1)S(1)} %bitcast.41), custom_call_target="tpu_custom_call" | custom-call | flops 4831838208 | bytes 4194304 | tf_op jit(solution)/shard_map/expert/pallas_call | solution.py:338
  211.5 1.3 collective-permute-start.13
  212.8 0.8 collective-permute-start.17
  213.6 12.7 %collective-permute-done.13 = bf16[128,4096]{1,0:T(8,128)(2,1)S(1)} collective-permute-done((bf16[128,4096]{1,0:T(8,128)(2,1)S(1)}, bf16[128,4096]{1,0:T(8,128)(2,1)S(1)}, u32[]{:S(2)}, u32[]{:S(2)}) %collective-permute-start.13) | collective-permute-done | bytes 1048608 | tf_op jit(solution)/shard_map/ppermute | solution.py:51
  226.6 2.5 collective-permute-start.14
  229.5 2.0 collective-permute-start.18
  231.5 8.6 %collective-permute-done.10 = bf16[128,4096]{1,0:T(8,128)(2,1)S(1)} collective-permute-done((bf16[128,4096]{1,0:T(8,128)(2,1)S(1)}, bf16[128,4096]{1,0:T(8,128)(2,1)S(1)}, u32[]{:S(2)}, u32[]{:S(2)}) %collective-permute-start.10) | collective-permute-done | bytes 1048608 | tf_op jit(solution)/shard_map/ppermute | solution.py:51
  240.1 1.4 collective-permute-done.14
  241.5 0.5 add_convert_fusion.2
  242.0 3.3 %collective-permute-start.15 = (bf16[64,4096]{1,0:T(8,128)(2,1)S(1)}, bf16[64,4096]{1,0:T(8,128)(2,1)S(1)}, u32[]{:S(2)}, u32[]{:S(2)}) collective-permute-start(bf16[64,4096]{1,0:T(8,128)(2,1)S(1)} %slice.67), channel_id=1, source_target_pairs={{0,96},{32,0},{64,32},{96,64},{8,104},{40,8},{72,40},{104,72},{16,... | collective-permute-start | bytes 1572872 | tf_op jit(solution)/shard_map/ppermute | solution.py:51
  245.3 7.4 %collective-permute-done.16 = bf16[128,4096]{1,0:T(8,128)(2,1)S(1)} collective-permute-done((bf16[128,4096]{1,0:T(8,128)(2,1)S(1)}, bf16[128,4096]{1,0:T(8,128)(2,1)S(1)}, u32[]{:S(2)}, u32[]{:S(2)}) %collective-permute-start.16) | collective-permute-done | bytes 1048608 | tf_op jit(solution)/shard_map/ppermute | solution.py:51
  252.7 9.8 %collective-permute-done.18 = bf16[128,4096]{1,0:T(8,128)(2,1)S(1)} collective-permute-done((bf16[128,4096]{1,0:T(8,128)(2,1)S(1)}, bf16[128,4096]{1,0:T(8,128)(2,1)S(1)}, u32[]{:S(2)}, u32[]{:S(2)}) %collective-permute-start.18) | collective-permute-done | bytes 1048608 | tf_op jit(solution)/shard_map/ppermute | solution.py:51
  262.5 0.5 add_convert_fusion
  263.1 0.9 collective-permute-start.19
  264.0 3.8 %collective-permute-start.20 = (bf16[64,4096]{1,0:T(8,128)(2,1)S(1)}, bf16[64,4096]{1,0:T(8,128)(2,1)S(1)}, u32[]{:S(2)}, u32[]{:S(2)}) collective-permute-start(bf16[64,4096]{1,0:T(8,128)(2,1)S(1)} %get-tuple-element.66), channel_id=1, source_target_pairs={{0,64},{32,96},{64,0},{96,32},{8,72},{40,104},{72,8},{104,40},{16,... | collective-permute-start | bytes 1572872 | tf_op jit(solution)/shard_map/ppermute | solution.py:51
  267.9 5.7 %collective-permute-done.19 = bf16[64,4096]{1,0:T(8,128)(2,1)S(1)} collective-permute-done((bf16[64,4096]{1,0:T(8,128)(2,1)S(1)}, bf16[64,4096]{1,0:T(8,128)(2,1)S(1)}, u32[]{:S(2)}, u32[]{:S(2)}) %collective-permute-start.19) | collective-permute-done | bytes 524320 | tf_op jit(solution)/shard_map/ppermute | solution.py:51
  273.6 7.1 %collective-permute-done.20 = bf16[64,4096]{1,0:T(8,128)(2,1)S(1)} collective-permute-done((bf16[64,4096]{1,0:T(8,128)(2,1)S(1)}, bf16[64,4096]{1,0:T(8,128)(2,1)S(1)}, u32[]{:S(2)}, u32[]{:S(2)}) %collective-permute-start.20) | collective-permute-done | bytes 524320 | tf_op jit(solution)/shard_map/ppermute | solution.py:51
  280.9 12.8 %all_to_all.32 = bf16[8,8,4096]{2,1,0:T(8,128)(2,1)S(1)} all-to-all(bf16[8,8,4096]{2,1,0:T(8,128)(2,1)S(1)} %fusion.1), channel_id=1, replica_groups=mesh['seq'=16,'exp'=8] {'exp'}, dimensions={0} | all-to-all | bytes 1048576 | tf_op jit(solution)/shard_map/all_to_all | solution.py:584
  293.7 1.2 convolution_add_fusion
  (88 shorter events, 4.2 us)
Async XLA Ops:
  6.5 39.4 %copy-start.14 = (f32[1024]{0:T(1024)S(1)}, f32[1024]{0:T(1024)}, u32[]{:S(2)}) copy-start(f32[1024]{0:T(1024)} %param.22) | copy-start | bytes 12292
  6.5 39.4 %copy-start.8 = (bf16[256,1024]{1,0:T(8,128)(2,1)S(1)}, bf16[256,1024]{1,0:T(8,128)(2,1)}, u32[]{:S(2)}) copy-start(bf16[256,1024]{1,0:T(8,128)(2,1)} %proj_hbm.1) | copy-start | bytes 1572868
  6.5 87.6 %all-gather.3.cloned.1.call-start = ((), (), s32[]{:S(2)}) async-start(), calls=%async_computation.6 | async-start | bytes 8912896 | tf_op jit(solution)/shard_map/all_gather | solution.py:399
  8.0 5.5 %collective-permute-start = (bf16[3,1024]{1,0:T(4,128)(2,1)S(1)}, bf16[3,1024]{1,0:T(4,128)(2,1)S(1)}, u32[]{:S(2)}, u32[]{:S(2)}) collective-permute-start(bf16[3,1024]{1,0:T(4,128)(2,1)S(1)} %slice.47), channel_id=1, source_target_pairs={{0,8},{8,16},{16,24},{24,32},{32,40},{40,48},{48,56},{56,64},{64,7... | collective-permute-start | bytes 18440 | tf_op jit(solution)/shard_map/ppermute | solution.py:57
  13.5 1.1 copy-start.6
  14.6 1.0 copy-start.7
  15.6 0.7 copy-start.12
  16.3 0.7 copy-start.13
  17.0 22.1 %copy-start.17 = (f32[1024,16]{0,1:T(8,128)S(1)}, f32[1024,16]{0,1:T(8,128)}, u32[]{:S(2)}) copy-start(f32[1024,16]{0,1:T(8,128)} %param.23) | copy-start | bytes 196612
  34.9 48.7 %copy-start.9 = (bf16[256,1024]{1,0:T(8,128)(2,1)S(1)}, bf16[256,1024]{1,0:T(8,128)(2,1)}, u32[]{:S(2)}) copy-start(bf16[256,1024]{1,0:T(8,128)(2,1)} %z_hbm.1) | copy-start | bytes 1572868
  34.9 48.7 %copy-start.15 = (f32[1024]{0:T(1024)S(1)}, f32[1024]{0:T(1024)}, u32[]{:S(2)}) copy-start(f32[1024]{0:T(1024)} %param.24) | copy-start | bytes 12292
  35.7 10.2 %all-to-all-start.1 = ((bf16[8,32,320]{2,1,0:T(8,128)(2,1)}), bf16[8,32,320]{2,1,0:T(8,128)(2,1)S(1)}, u32[]{:S(2)}, u32[]{:S(2)}) async-start(bf16[8,32,320]{2,1,0:T(8,128)(2,1)} %broadcast_in_dim.9), calls=%async_computation.1 | async-start | bytes 393216 | tf_op jit(solution)/shard_map/all_to_all | solution.py:430
  54.8 1.0 copy-start.2
  55.8 1.0 copy-start.4
  56.7 26.9 %copy-start.10 = (f32[16,8,1024]{2,1,0:T(8,128)}, f32[16,8,1024]{2,1,0:T(8,128)S(1)}, u32[]{:S(2)}) copy-start(f32[16,8,1024]{2,1,0:T(8,128)S(1)} %get-tuple-element.36.enter_hbm) | copy-start | bytes 1572868
  56.7 14.1 %all-to-all-start.2 = ((f32[16,2,1024]{2,1,0:T(2,128)}), f32[16,2,1024]{2,1,0:T(2,128)S(1)}, u32[]{:S(2)}, u32[]{:S(2)}) async-start(f32[16,2,1024]{2,1,0:T(2,128)} %get-tuple-element.32), calls=%async_computation.2 | async-start | bytes 262144 | tf_op jit(solution)/shard_map/all_to_all | solution.py:462
  71.5 12.1 %all-to-all-start.3 = ((f32[16,1,1024]{2,1,0:T(1,128)}), f32[16,1,1024]{2,1,0:T(1,128)S(1)}, u32[]{:S(2)}, u32[]{:S(2)}) async-start(f32[16,1,1024]{2,1,0:T(1,128)} %relay.1), calls=%async_computation.3 | async-start | bytes 131072 | tf_op jit(solution)/shard_map/all_to_all | solution.py:472
  83.7 1.2 copy-start.3
  84.9 1.2 copy-start.5
  86.1 1.0 copy-start.11
  94.2 8.5 %copy-start.18 = (s32[32,2]{0,1:T(2,128)S(1)}, s32[32,2]{0,1:T(2,128)}, u32[]{:S(2)}) copy-start(s32[32,2]{0,1:T(2,128)} %param.27) | copy-start | bytes 772
  94.2 17.0 %copy-start.19 = (f32[32,2]{0,1:T(2,128)S(1)}, f32[32,2]{0,1:T(2,128)}, u32[]{:S(2)}) copy-start(f32[32,2]{0,1:T(2,128)} %param.28) | copy-start | bytes 772
  94.2 29.4 %copy-start.16 = (bf16[32,4096]{1,0:T(8,128)(2,1)S(1)}, bf16[32,4096]{1,0:T(8,128)(2,1)}, u32[]{:S(2)}) copy-start(bf16[32,4096]{1,0:T(8,128)(2,1)} %param.26) | copy-start | bytes 786436
  94.2 62.3 %slice-start.2 = ((s8[6291456]{0:T(1024)(128)(4,1)}), s8[2097152]{0:T(1024)(128)(4,1)S(1)}, s32[]{:S(2)}) async-start(s8[6291456]{0:T(1024)(128)(4,1)} %bitcast.32), calls=%async_computation.9 | async-start | bytes 4194304
  101.4 1.3 copy-start.1
  102.7 2.9 collective-permute-start.1
  105.6 50.9 %slice-start = ((s8[6291456]{0:T(1024)(128)(4,1)}), s8[4194304]{0:T(1024)(128)(4,1)S(1)}, s32[]{:S(2)}) async-start(s8[6291456]{0:T(1024)(128)(4,1)} %bitcast.26), calls=%async_computation.7 | async-start | bytes 8388608
  105.6 50.9 %slice-start.3 = ((s8[6291456]{0:T(1024)(128)(4,1)}), s8[4194304]{0:T(1024)(128)(4,1)S(1)}, s32[]{:S(2)}) async-start(s8[6291456]{0:T(1024)(128)(4,1)} %bitcast.32), calls=%async_computation.10 | async-start | bytes 8388608
  107.7 15.2 %collective-permute-start.2 = (bf16[32,4096]{1,0:T(8,128)(2,1)S(1)}, bf16[32,4096]{1,0:T(8,128)(2,1)S(1)}, u32[]{:S(2)}, u32[]{:S(2)}) collective-permute-start(bf16[32,4096]{1,0:T(8,128)(2,1)S(1)} %get-tuple-element.67), channel_id=1, source_target_pairs={{0,2},{1,3},{2,4},{3,5},{4,6},{5,7},{6,0},{7,1},{8,10},{9,11},{10,... | collective-permute-start | bytes 786440 | tf_op jit(solution)/shard_map/ppermute | solution.py:530
  108.4 14.6 %collective-permute-start.3 = (bf16[32,4096]{1,0:T(8,128)(2,1)S(1)}, bf16[32,4096]{1,0:T(8,128)(2,1)S(1)}, u32[]{:S(2)}, u32[]{:S(2)}) collective-permute-start(bf16[32,4096]{1,0:T(8,128)(2,1)S(1)} %get-tuple-element.69), channel_id=1, source_target_pairs={{0,4},{1,5},{2,6},{3,7},{4,0},{5,1},{6,2},{7,3},{8,12},{9,13},{10,... | collective-permute-start | bytes 786440 | tf_op jit(solution)/shard_map/ppermute | solution.py:530
  110.4 13.2 %collective-permute-start.4 = (bf16[32,4096]{1,0:T(8,128)(2,1)S(1)}, bf16[32,4096]{1,0:T(8,128)(2,1)S(1)}, u32[]{:S(2)}, u32[]{:S(2)}) collective-permute-start(bf16[32,4096]{1,0:T(8,128)(2,1)S(1)} %get-tuple-element.68), channel_id=1, source_target_pairs={{0,6},{1,7},{2,0},{3,1},{4,2},{5,3},{6,4},{7,5},{8,14},{9,15},{10,... | collective-permute-start | bytes 786440 | tf_op jit(solution)/shard_map/ppermute | solution.py:530
  123.6 32.9 %slice-start.1 = ((s8[6291456]{0:T(1024)(128)(4,1)}), s8[2097152]{0:T(1024)(128)(4,1)S(1)}, s32[]{:S(2)}) async-start(s8[6291456]{0:T(1024)(128)(4,1)} %bitcast.26), calls=%async_computation.8 | async-start | bytes 4194304
  138.2 16.0 %collective-permute-start.5 = (bf16[64,4096]{1,0:T(8,128)(2,1)S(1)}, bf16[64,4096]{1,0:T(8,128)(2,1)S(1)}, u32[]{:S(2)}, u32[]{:S(2)}) collective-permute-start(bf16[64,4096]{1,0:T(8,128)(2,1)S(1)} %bitcast.51), channel_id=1, source_target_pairs={{0,32},{32,64},{64,96},{96,0},{8,40},{40,72},{72,104},{104,8},{16,... | collective-permute-start | bytes 1572872 | tf_op jit(solution)/shard_map/ppermute | solution.py:51
  138.5 15.6 %collective-permute-start.6 = (bf16[64,4096]{1,0:T(8,128)(2,1)S(1)}, bf16[64,4096]{1,0:T(8,128)(2,1)S(1)}, u32[]{:S(2)}, u32[]{:S(2)}) collective-permute-start(bf16[64,4096]{1,0:T(8,128)(2,1)S(1)} %bitcast.52), channel_id=1, source_target_pairs={{0,96},{32,0},{64,32},{96,64},{8,104},{40,8},{72,40},{104,72},{16,... | collective-permute-start | bytes 1572872 | tf_op jit(solution)/shard_map/ppermute | solution.py:51
  141.4 12.8 %collective-permute-start.7 = (bf16[64,4096]{1,0:T(8,128)(2,1)S(1)}, bf16[64,4096]{1,0:T(8,128)(2,1)S(1)}, u32[]{:S(2)}, u32[]{:S(2)}) collective-permute-start(bf16[64,4096]{1,0:T(8,128)(2,1)S(1)} %bitcast.53), channel_id=1, source_target_pairs={{0,64},{32,96},{64,0},{96,32},{8,72},{40,104},{72,8},{104,40},{16,... | collective-permute-start | bytes 1572872 | tf_op jit(solution)/shard_map/ppermute | solution.py:51
  154.4 26.1 %collective-permute-start.8 = (bf16[256,4096]{1,0:T(8,128)(2,1)S(1)}, bf16[256,4096]{1,0:T(8,128)(2,1)S(1)}, u32[]{:S(2)}, u32[]{:S(2)}) collective-permute-start(bf16[256,4096]{1,0:T(8,128)(2,1)S(1)} %pad_maximum_fusion.rows_ref), channel_id=1, source_target_pairs={{0,8},{8,16},{16,24},{24,0},{32,40},{40,48},{48,56},{56,32},{64,72... | collective-permute-start | bytes 6291464 | tf_op jit(solution)/shard_map/ppermute | solution.py:51
  156.5 27.2 %collective-permute-start.9 = (bf16[256,4096]{1,0:T(8,128)(2,1)S(1)}, bf16[256,4096]{1,0:T(8,128)(2,1)S(1)}, u32[]{:S(2)}, u32[]{:S(2)}) collective-permute-start(bf16[256,4096]{1,0:T(8,128)(2,1)S(1)} %pad_maximum_fusion.rows_ref), channel_id=1, source_target_pairs={{0,24},{8,0},{16,8},{24,16},{32,56},{40,32},{48,40},{56,48},{64,88... | collective-permute-start | bytes 6291464 | tf_op jit(solution)/shard_map/ppermute | solution.py:51
  156.5 2.8 copy-start
  183.8 19.1 %collective-permute-start.11 = (bf16[128,4096]{1,0:T(8,128)(2,1)S(1)}, bf16[128,4096]{1,0:T(8,128)(2,1)S(1)}, u32[]{:S(2)}, u32[]{:S(2)}) collective-permute-start(bf16[128,4096]{1,0:T(8,128)(2,1)S(1)} %slice.54), channel_id=1, source_target_pairs={{0,8},{8,16},{16,24},{24,0},{32,40},{40,48},{48,56},{56,32},{64,72... | collective-permute-start | bytes 3145736 | tf_op jit(solution)/shard_map/ppermute | solution.py:51
  184.0 18.9 %collective-permute-start.12 = (bf16[128,4096]{1,0:T(8,128)(2,1)S(1)}, bf16[128,4096]{1,0:T(8,128)(2,1)S(1)}, u32[]{:S(2)}, u32[]{:S(2)}) collective-permute-start(bf16[128,4096]{1,0:T(8,128)(2,1)S(1)} %slice.55), channel_id=1, source_target_pairs={{0,24},{8,0},{16,8},{24,16},{32,56},{40,32},{48,40},{56,48},{64,88... | collective-permute-start | bytes 3145736 | tf_op jit(solution)/shard_map/ppermute | solution.py:51
  211.5 14.9 %collective-permute-start.13 = (bf16[128,4096]{1,0:T(8,128)(2,1)S(1)}, bf16[128,4096]{1,0:T(8,128)(2,1)S(1)}, u32[]{:S(2)}, u32[]{:S(2)}) collective-permute-start(bf16[128,4096]{1,0:T(8,128)(2,1)S(1)} %get-tuple-element.50), channel_id=1, source_target_pairs={{0,8},{8,16},{16,24},{24,0},{32,40},{40,48},{48,56},{56,32},{64,72... | collective-permute-start | bytes 3145736 | tf_op jit(solution)/shard_map/ppermute | solution.py:51
  212.8 16.4 %collective-permute-start.17 = (bf16[128,4096]{1,0:T(8,128)(2,1)S(1)}, bf16[128,4096]{1,0:T(8,128)(2,1)S(1)}, u32[]{:S(2)}, u32[]{:S(2)}) collective-permute-start(bf16[128,4096]{1,0:T(8,128)(2,1)S(1)} %get-tuple-element.54), channel_id=1, source_target_pairs={{0,24},{8,0},{16,8},{24,16},{32,56},{40,32},{48,40},{56,48},{64,88... | collective-permute-start | bytes 3145736 | tf_op jit(solution)/shard_map/ppermute | solution.py:51
  213.6 26.4 %collective-permute-start.10 = (bf16[128,4096]{1,0:T(8,128)(2,1)S(1)}, bf16[128,4096]{1,0:T(8,128)(2,1)S(1)}, u32[]{:S(2)}, u32[]{:S(2)}) collective-permute-start(bf16[128,4096]{1,0:T(8,128)(2,1)S(1)} %get-tuple-element.43), channel_id=1, source_target_pairs={{0,24},{8,0},{16,8},{24,16},{32,56},{40,32},{48,40},{56,48},{64,88... | collective-permute-start | bytes 3145736 | tf_op jit(solution)/shard_map/ppermute | solution.py:51
  226.6 14.9 %collective-permute-start.14 = (bf16[128,4096]{1,0:T(8,128)(2,1)S(1)}, bf16[128,4096]{1,0:T(8,128)(2,1)S(1)}, u32[]{:S(2)}, u32[]{:S(2)}) collective-permute-start(bf16[128,4096]{1,0:T(8,128)(2,1)S(1)} %add_convert_fusion.3), channel_id=1, source_target_pairs={{0,8},{8,16},{16,24},{24,0},{32,40},{40,48},{48,56},{56,32},{64,72... | collective-permute-start | bytes 3145736 | tf_op jit(solution)/shard_map/ppermute | solution.py:51
  229.1 23.6 %collective-permute-start.16 = (bf16[128,4096]{1,0:T(8,128)(2,1)S(1)}, bf16[128,4096]{1,0:T(8,128)(2,1)S(1)}, u32[]{:S(2)}, u32[]{:S(2)}) collective-permute-start(bf16[128,4096]{1,0:T(8,128)(2,1)S(1)} %get-tuple-element.52), channel_id=1, source_target_pairs={{0,8},{8,16},{16,24},{24,0},{32,40},{40,48},{48,56},{56,32},{64,72... | collective-permute-start | bytes 3145736 | tf_op jit(solution)/shard_map/ppermute | solution.py:51
  229.5 33.0 %collective-permute-start.18 = (bf16[128,4096]{1,0:T(8,128)(2,1)S(1)}, bf16[128,4096]{1,0:T(8,128)(2,1)S(1)}, u32[]{:S(2)}, u32[]{:S(2)}) collective-permute-start(bf16[128,4096]{1,0:T(8,128)(2,1)S(1)} %add_convert_fusion.1), channel_id=1, source_target_pairs={{0,24},{8,0},{16,8},{24,16},{32,56},{40,32},{48,40},{56,48},{64,88... | collective-permute-start | bytes 3145736 | tf_op jit(solution)/shard_map/ppermute | solution.py:51
  242.0 25.8 %collective-permute-start.15 = (bf16[64,4096]{1,0:T(8,128)(2,1)S(1)}, bf16[64,4096]{1,0:T(8,128)(2,1)S(1)}, u32[]{:S(2)}, u32[]{:S(2)}) collective-permute-start(bf16[64,4096]{1,0:T(8,128)(2,1)S(1)} %slice.67), channel_id=1, source_target_pairs={{0,96},{32,0},{64,32},{96,64},{8,104},{40,8},{72,40},{104,72},{16,... | collective-permute-start | bytes 1572872 | tf_op jit(solution)/shard_map/ppermute | solution.py:51
  263.1 10.5 %collective-permute-start.19 = (bf16[64,4096]{1,0:T(8,128)(2,1)S(1)}, bf16[64,4096]{1,0:T(8,128)(2,1)S(1)}, u32[]{:S(2)}, u32[]{:S(2)}) collective-permute-start(bf16[64,4096]{1,0:T(8,128)(2,1)S(1)} %get-tuple-element.65), channel_id=1, source_target_pairs={{0,32},{32,64},{64,96},{96,0},{8,40},{40,72},{72,104},{104,8},{16,... | collective-permute-start | bytes 1572872 | tf_op jit(solution)/shard_map/ppermute | solution.py:51
  264.0 16.6 %collective-permute-start.20 = (bf16[64,4096]{1,0:T(8,128)(2,1)S(1)}, bf16[64,4096]{1,0:T(8,128)(2,1)S(1)}, u32[]{:S(2)}, u32[]{:S(2)}) collective-permute-start(bf16[64,4096]{1,0:T(8,128)(2,1)S(1)} %get-tuple-element.66), channel_id=1, source_target_pairs={{0,64},{32,96},{64,0},{96,32},{8,72},{40,104},{72,8},{104,40},{16,... | collective-permute-start | bytes 1572872 | tf_op jit(solution)/shard_map/ppermute | solution.py:51
Sparse Core Ops, SparseCore 0:
  9.5 74.7 all-gather.2

commit v2 on v1

--- a/solution.py
+++ b/solution.py
@@ -383,6 +383,9 @@
         (far_first, far_second, behind_second, ahead_first)
     )
     across_first, across_second = run(jnp.concatenate([far_first, far_second], axis=0))
+    across_first, across_second, early_first, early_second = lax.optimization_barrier(
+        (across_first, across_second, early_first, early_second)
+    )
     late_first = along(added(ahead_first, along(across_first, 1, 1)), 1, 1)
     late_second = along(added(behind_second, along(across_second, 1, -1)), 1, -1)
     first = added(own_out[0], early_first, late_first)

time: 303 us -> 306 us (level)
  starting transfers between devices: 45.3 us -> 59.5 us
  waiting for transfers between devices: 119 us -> 108 us
    ppermute x16, starting transfers between devices: 22.3 us -> 36.5 us  [along(): return lax.ppermute(block, ('seq', 'exp'), route)]
    ppermute x16, waiting for transfers between devices: 81.5 us -> 71 us  [along(): return lax.ppermute(block, ('seq', 'exp'), route)]
  transfers between devices with their start and end apart: 25 -> 25, of which waited for: 17 -> 16; matrix products, arithmetic and copies ran while one was open for 1% -> 1% of each run, Pallas kernels for 15% -> 18%
where the time goes in v2:
time: 306 us; the launch traced here: 305 us
  waiting for transfers between devices  108 us (35%)
  Pallas kernels  61 us (20%)
  starting transfers between devices  59.5 us (19%)
  blocking collectives  40.8 us (13%)
  local copies, waits for them, and re-layouts  15.4 us (5%)
  between operations  13.8 us (5%)
  other arithmetic  5.17 us (2%)
    ppermute x16, waiting for transfers between devices, along(): return lax.ppermute(block, ('seq', 'exp'), route)  71 us
    ppermute x16, starting transfers between devices, along(): return lax.ppermute(block, ('seq', 'exp'), route)  36.5 us
    pallas_call x4, Pallas kernels, expert(): pl.pallas_call(expert_kernel, out_shape=(jax.ShapeDtypeStruct((count // 2...  33.5 us
    all_to_all x1, blocking collectives, mixer(): lax.all_to_all(partial.reshape(owners, length // owners, -1), 'exp', spli...  14.1 us
    all_to_all x1, blocking collectives, shards(): lax.all_to_all(outgoing, 'exp', split_axis=0, concat_axis=0, tiled=True)  13.9 us
    unnamed x50, local copies, waits for them, and re-layouts  13.2 us
    all_to_all x1, blocking collectives, shards(): lax.all_to_all(expert_out, 'exp', split_axis=0, concat_axis=0, tiled=True)  12.8 us
    ppermute x3, waiting for transfers between devices, mixer(): lax.ppermute(sums[hop].astype(BF16), 'exp', route).astype(F32)  12.3 us
  transfers between devices with their start and end apart: 25, of which 16 were waited for; matrix products, arithmetic and copies ran while one was open for 1% of the time, Pallas kernels for 18%

profile of v2, /device:TPU:24, one launch (start us, length us, event | category | flops | bytes accessed | tf_op | source)
XLA Modules:
  0.0 305.4 jit_solution(16280661603397310694)
XLA Ops:
  6.5 0.7 all-gather.3.cloned.1.call-update
  7.3 0.7 slice.47
  8.0 3.0 collective-permute-start
  11.0 2.5 collective-permute-done.rim_ref
  13.5 1.1 copy-done.6
  14.6 1.0 copy-done.7
  15.6 0.7 copy-done.12
  16.3 0.7 copy-done.13
  17.0 3.8 %conv.1 = (f32[256,1024]{1,0:T(8,128)S(1)}, f32[256,288]{1,0:T(8,128)S(1)}) custom-call(bf16[256,1024]{1,0:T(8,128)(2,1)S(1)} %copy-done.7, f32[4,1024]{1,0:T(4,128)S(1)} %copy-done.12, f32[1,1024]{1,0:T(1,128)S(1)} %bitcast.47, bf16[288,1024]{1,0:T(8,128)(2,1)S(1)} %bitcast.44, bf16[3,1024]{1,0:T(4,128)(2,1)S(1)} %collective-permute-done.rim_ref), custom_call_target="tpu_custom_call" | custom-call | tf_op jit(solution)/shard_map/conv/pallas_call | solution.py:405
  20.8 14.1 %all_to_all.30 = f32[8,32,288]{2,1,0:T(8,128)S(1)} all-to-all(f32[8,32,288]{2,1,0:T(8,128)S(1)} %bitcast.45), channel_id=1, replica_groups=mesh['seq'=16,'exp'=8] {'exp'}, dimensions={0} | all-to-all | bytes 589824 | tf_op jit(solution)/shard_map/all_to_all | solution.py:424
  35.0 0.7 broadcast_in_dim.9
  35.7 3.4 %all-to-all-start.1 = ((bf16[8,32,320]{2,1,0:T(8,128)(2,1)}), bf16[8,32,320]{2,1,0:T(8,128)(2,1)S(1)}, u32[]{:S(2)}, u32[]{:S(2)}) async-start(bf16[8,32,320]{2,1,0:T(8,128)(2,1)} %broadcast_in_dim.9), calls=%async_computation.1 | async-start | bytes 393216 | tf_op jit(solution)/shard_map/all_to_all | solution.py:433
  39.2 6.7 %all-to-all-done.1 = bf16[8,32,320]{2,1,0:T(8,128)(2,1)S(1)} async-done(((bf16[8,32,320]{2,1,0:T(8,128)(2,1)}), bf16[8,32,320]{2,1,0:T(8,128)(2,1)S(1)}, u32[]{:S(2)}, u32[]{:S(2)}) %all-to-all-start.1) | async-done | bytes 163872 | tf_op jit(solution)/shard_map/all_to_all | solution.py:433
  45.9 8.9 %scan.1 = (f32[256,1024]{1,0:T(8,128)S(1)}, f32[256,1024]{1,0:T(8,128)S(1)}, f32[8,1024]{1,0:T(8,128)S(1)}, f32[16,8,1024]{2,1,0:T(8,128)S(1)}, f32[16,2,1024]{2,1,0:T(2,128)}) custom-call(bf16[256,320]{1,0:T(8,128)(2,1)S(1)} %bitcast.42, f32[256,1024]{1,0:T(8,128)S(1)} %get-tuple-element.35.mixed_ref, f32[16,1024]{1,0:T(8,128)S(1)} %multiply_bitcast_fusion.rates_ref, ...), custom_call_target="tpu_custom_call" | custom-call | tf_op jit(solution)/shard_map/scan/pallas_call | solution.py:440
  54.8 1.0 copy-done.2
  55.8 1.0 copy-done.4
  56.7 7.2 %all-to-all-start.2 = ((f32[16,2,1024]{2,1,0:T(2,128)}), f32[16,2,1024]{2,1,0:T(2,128)S(1)}, u32[]{:S(2)}, u32[]{:S(2)}) async-start(f32[16,2,1024]{2,1,0:T(2,128)} %get-tuple-element.36), calls=%async_computation.2 | async-start | bytes 262144 | tf_op jit(solution)/shard_map/all_to_all | solution.py:465
  63.9 6.9 %all-to-all-done.2.ends_ref = f32[16,2,1024]{2,1,0:T(2,128)S(1)} async-done(((f32[16,2,1024]{2,1,0:T(2,128)}), f32[16,2,1024]{2,1,0:T(2,128)S(1)}, u32[]{:S(2)}, u32[]{:S(2)}) %all-to-all-start.2) | async-done | bytes 131104 | tf_op jit(solution)/shard_map/all_to_all | solution.py:465
  70.8 0.7 relay.1
  71.5 6.0 %all-to-all-start.3 = ((f32[16,1,1024]{2,1,0:T(1,128)}), f32[16,1,1024]{2,1,0:T(1,128)S(1)}, u32[]{:S(2)}, u32[]{:S(2)}) async-start(f32[16,1,1024]{2,1,0:T(1,128)} %relay.1), calls=%async_computation.3 | async-start | bytes 131072 | tf_op jit(solution)/shard_map/all_to_all | solution.py:475
  77.6 6.0 %all-to-all-done.3 = f32[16,1,1024]{2,1,0:T(1,128)S(1)} async-done(((f32[16,1,1024]{2,1,0:T(1,128)}), f32[16,1,1024]{2,1,0:T(1,128)S(1)}, u32[]{:S(2)}, u32[]{:S(2)}) %all-to-all-start.3) | async-done | bytes 65568 | tf_op jit(solution)/shard_map/all_to_all | solution.py:475
  83.7 1.2 copy-done.3
  84.9 1.2 copy-done.5
  86.1 1.0 copy-done.11
  87.1 7.0 %finish.1.gated_ref = bf16[256,1024]{1,0:T(8,128)(2,1)S(1)} custom-call(s32[8]{0:T(128)S(1)} %pad_add_fusion.order_ref, f32[16,1024]{1,0:T(8,128)S(1)} %bitcast.46, f32[16,1024]{1,0:T(8,128)S(1)} %multiply_bitcast_fusion.rates_ref, f32[256,1024]{1,0:T(8,128)S(1)} %copy-done.5, bf16[256,320]{1,0:T(8,128)(2,1)S(1)} %bitcast.43, f32[256,1024]{1,0:T(8,128)S(1)} %copy-done.3, ...), custom_call_target="tpu_custom_call" | custom-call | tf_op jit(solution)/shard_map/finish/pallas_call | solution.py:480
  94.2 7.1 %outward.1 = (bf16[128,4096]{1,0:T(8,128)(2,1)}, f32[128,4096]{1,0:T(8,128)S(1)}) custom-call(bf16[256,1024]{1,0:T(8,128)(2,1)S(1)} %finish.1.gated_ref, bf16[16,1024,256]{2,1,0:T(8,128)(2,1)} %bitcast.50), custom_call_target="tpu_custom_call" | custom-call | tf_op jit(solution)/shard_map/outward/pallas_call | solution.py:512
  101.4 1.3 copy-done.1
  103.7 1.9 collective-permute-done.1
  105.6 2.1 fusion.14
  107.7 0.6 collective-permute-start.2
  108.4 2.0 collective-permute-start.3
  110.4 0.7 collective-permute-start.4
  111.2 11.7 %collective-permute-done.2 = bf16[32,4096]{1,0:T(8,128)(2,1)S(1)} collective-permute-done((bf16[32,4096]{1,0:T(8,128)(2,1)S(1)}, bf16[32,4096]{1,0:T(8,128)(2,1)S(1)}, u32[]{:S(2)}, u32[]{:S(2)}) %collective-permute-start.2) | collective-permute-done | bytes 262176 | tf_op jit(solution)/shard_map/ppermute | solution.py:533
  123.0 0.6 collective-permute-done.4
  123.9 0.3 fusion
  124.2 13.9 %all_to_all.31 = bf16[8,8,4096]{2,1,0:T(8,128)(2,1)S(1)} all-to-all(bf16[8,8,4096]{2,1,0:T(8,128)(2,1)S(1)} %fusion), channel_id=1, replica_groups=mesh['seq'=16,'exp'=8] {'exp'}, dimensions={0} | all-to-all | bytes 1048576 | tf_op jit(solution)/shard_map/all_to_all | solution.py:584
  138.2 0.4 collective-permute-start.5
  138.5 2.9 collective-permute-start.6
  141.4 12.8 %collective-permute-done.5 = bf16[64,4096]{1,0:T(8,128)(2,1)S(1)} collective-permute-done((bf16[64,4096]{1,0:T(8,128)(2,1)S(1)}, bf16[64,4096]{1,0:T(8,128)(2,1)S(1)}, u32[]{:S(2)}, u32[]{:S(2)}) %collective-permute-start.5) | collective-permute-done | bytes 524320 | tf_op jit(solution)/shard_map/ppermute | solution.py:51
  154.4 2.1 collective-permute-start.8
  156.5 2.8 copy-done
  159.3 8.4 %expert.4 = (bf16[128,4096]{1,0:T(8,128)(2,1)S(1)}, bf16[128,4096]{1,0:T(8,128)(2,1)S(1)}) custom-call(bf16[256,4096]{1,0:T(8,128)(2,1)S(1)} %pad_maximum_fusion.rows_ref, bf16[4096,768]{1,0:T(8,128)(2,1)S(1)} %bitcast.28, bf16[4096,768]{1,0:T(8,128)(2,1)S(1)} %bitcast.34, bf16[768,4096]{1,0:T(8,128)(2,1)S(1)} %bitcast.38), custom_call_target="tpu_custom_call" | custom-call | flops 4831838208 | bytes 4194304 | tf_op jit(solution)/shard_map/expert/pallas_call | solution.py:338
  167.7 12.8 %collective-permute-done.8.rows_ref = bf16[256,4096]{1,0:T(8,128)(2,1)S(1)} collective-permute-done((bf16[256,4096]{1,0:T(8,128)(2,1)S(1)}, bf16[256,4096]{1,0:T(8,128)(2,1)S(1)}, u32[]{:S(2)}, u32[]{:S(2)}) %collective-permute-start.8) | collective-permute-done | bytes 2097184 | tf_op jit(solution)/shard_map/ppermute | solution.py:51
  180.5 3.2 %collective-permute-done.9.rows_ref = bf16[256,4096]{1,0:T(8,128)(2,1)S(1)} collective-permute-done((bf16[256,4096]{1,0:T(8,128)(2,1)S(1)}, bf16[256,4096]{1,0:T(8,128)(2,1)S(1)}, u32[]{:S(2)}, u32[]{:S(2)}) %collective-permute-start.9) | collective-permute-done | bytes 2097184 | tf_op jit(solution)/shard_map/ppermute | solution.py:51
  184.0 2.1 collective-permute-start.11
  186.1 8.4 %expert.5 = (bf16[128,4096]{1,0:T(8,128)(2,1)S(1)}, bf16[128,4096]{1,0:T(8,128)(2,1)S(1)}) custom-call(bf16[256,4096]{1,0:T(8,128)(2,1)S(1)} %collective-permute-done.8.rows_ref, bf16[4096,768]{1,0:T(8,128)(2,1)S(1)} %bitcast.29, bf16[4096,768]{1,0:T(8,128)(2,1)S(1)} %bitcast.35, bf16[768,4096]{1,0:T(8,128)(2,1)S(1)} %bitcast.39), custom_call_target="tpu_custom_call" | custom-call | flops 4831838208 | bytes 4194304 | tf_op jit(solution)/shard_map/expert/pallas_call | solution.py:338
  194.6 8.4 %expert.6 = (bf16[128,4096]{1,0:T(8,128)(2,1)S(1)}, bf16[128,4096]{1,0:T(8,128)(2,1)S(1)}) custom-call(bf16[256,4096]{1,0:T(8,128)(2,1)S(1)} %collective-permute-done.9.rows_ref, bf16[4096,768]{1,0:T(8,128)(2,1)S(1)} %bitcast.30, bf16[4096,768]{1,0:T(8,128)(2,1)S(1)} %bitcast.36, bf16[768,4096]{1,0:T(8,128)(2,1)S(1)} %bitcast.40), custom_call_target="tpu_custom_call" | custom-call | flops 4831838208 | bytes 4194304 | tf_op jit(solution)/shard_map/expert/pallas_call | solution.py:338
  203.0 3.3 %collective-permute-start.13 = (bf16[128,4096]{1,0:T(8,128)(2,1)S(1)}, bf16[128,4096]{1,0:T(8,128)(2,1)S(1)}, u32[]{:S(2)}, u32[]{:S(2)}) collective-permute-start(bf16[128,4096]{1,0:T(8,128)(2,1)S(1)} %get-tuple-element.55), channel_id=1, source_target_pairs={{0,8},{8,16},{16,24},{24,0},{32,40},{40,48},{48,56},{56,32},{64,72... | collective-permute-start | bytes 3145736 | tf_op jit(solution)/shard_map/ppermute | solution.py:51
  206.5 8.4 %expert.7 = (bf16[128,4096]{1,0:T(8,128)(2,1)S(1)}, bf16[128,4096]{1,0:T(8,128)(2,1)S(1)}) custom-call(bf16[256,4096]{1,0:T(8,128)(2,1)S(1)} %pad_maximum_fusion.1.rows_ref, bf16[4096,768]{1,0:T(8,128)(2,1)S(1)} %bitcast.31, bf16[4096,768]{1,0:T(8,128)(2,1)S(1)} %bitcast.37, bf16[768,4096]{1,0:T(8,128)(2,1)S(1)} %bitcast.41), custom_call_target="tpu_custom_call" | custom-call | flops 4831838208 | bytes 4194304 | tf_op jit(solution)/shard_map/expert/pallas_call | solution.py:338
  214.9 3.7 %collective-permute-done.13 = bf16[128,4096]{1,0:T(8,128)(2,1)S(1)} collective-permute-done((bf16[128,4096]{1,0:T(8,128)(2,1)S(1)}, bf16[128,4096]{1,0:T(8,128)(2,1)S(1)}, u32[]{:S(2)}, u32[]{:S(2)}) %collective-permute-start.13) | collective-permute-done | bytes 1048608 | tf_op jit(solution)/shard_map/ppermute | solution.py:51
  218.6 3.7 %collective-permute-start.14 = (bf16[128,4096]{1,0:T(8,128)(2,1)S(1)}, bf16[128,4096]{1,0:T(8,128)(2,1)S(1)}, u32[]{:S(2)}, u32[]{:S(2)}) collective-permute-start(bf16[128,4096]{1,0:T(8,128)(2,1)S(1)} %get-tuple-element.58), channel_id=1, source_target_pairs={{0,8},{8,16},{16,24},{24,0},{32,40},{40,48},{48,56},{56,32},{64,72... | collective-permute-start | bytes 3145736 | tf_op jit(solution)/shard_map/ppermute | solution.py:51
  222.3 12.3 %collective-permute-done.14 = bf16[128,4096]{1,0:T(8,128)(2,1)S(1)} collective-permute-done((bf16[128,4096]{1,0:T(8,128)(2,1)S(1)}, bf16[128,4096]{1,0:T(8,128)(2,1)S(1)}, u32[]{:S(2)}, u32[]{:S(2)}) %collective-permute-start.14) | collective-permute-done | bytes 1048608 | tf_op jit(solution)/shard_map/ppermute | solution.py:51
  234.9 3.8 %collective-permute-start.15 = (bf16[128,4096]{1,0:T(8,128)(2,1)S(1)}, bf16[128,4096]{1,0:T(8,128)(2,1)S(1)}, u32[]{:S(2)}, u32[]{:S(2)}) collective-permute-start(bf16[128,4096]{1,0:T(8,128)(2,1)S(1)} %add_convert_fusion.3), channel_id=1, source_target_pairs={{0,8},{8,16},{16,24},{24,0},{32,40},{40,48},{48,56},{56,32},{64,72... | collective-permute-start | bytes 3145736 | tf_op jit(solution)/shard_map/ppermute | solution.py:51
  239.0 12.0 %collective-permute-done.15 = bf16[128,4096]{1,0:T(8,128)(2,1)S(1)} collective-permute-done((bf16[128,4096]{1,0:T(8,128)(2,1)S(1)}, bf16[128,4096]{1,0:T(8,128)(2,1)S(1)}, u32[]{:S(2)}, u32[]{:S(2)}) %collective-permute-start.15) | collective-permute-done | bytes 1048608 | tf_op jit(solution)/shard_map/ppermute | solution.py:51
  250.9 0.5 add_convert_fusion.2
  251.5 4.7 %collective-permute-start.16 = (bf16[64,4096]{1,0:T(8,128)(2,1)S(1)}, bf16[64,4096]{1,0:T(8,128)(2,1)S(1)}, u32[]{:S(2)}, u32[]{:S(2)}) collective-permute-start(bf16[64,4096]{1,0:T(8,128)(2,1)S(1)} %slice.67), channel_id=1, source_target_pairs={{0,96},{32,0},{64,32},{96,64},{8,104},{40,8},{72,40},{104,72},{16,... | collective-permute-start | bytes 1572872 | tf_op jit(solution)/shard_map/ppermute | solution.py:51
  256.1 1.4 collective-permute-done.18
  257.6 0.5 add_convert_fusion
  258.1 8.3 %collective-permute-start.19 = (bf16[64,4096]{1,0:T(8,128)(2,1)S(1)}, bf16[64,4096]{1,0:T(8,128)(2,1)S(1)}, u32[]{:S(2)}, u32[]{:S(2)}) collective-permute-start(bf16[64,4096]{1,0:T(8,128)(2,1)S(1)} %get-tuple-element.73), channel_id=1, source_target_pairs={{0,32},{32,64},{64,96},{96,0},{8,40},{40,72},{72,104},{104,8},{16,... | collective-permute-start | bytes 1572872 | tf_op jit(solution)/shard_map/ppermute | solution.py:51
  266.4 5.1 %collective-permute-start.20 = (bf16[64,4096]{1,0:T(8,128)(2,1)S(1)}, bf16[64,4096]{1,0:T(8,128)(2,1)S(1)}, u32[]{:S(2)}, u32[]{:S(2)}) collective-permute-start(bf16[64,4096]{1,0:T(8,128)(2,1)S(1)} %get-tuple-element.74), channel_id=1, source_target_pairs={{0,64},{32,96},{64,0},{96,32},{8,72},{40,104},{72,8},{104,40},{16,... | collective-permute-start | bytes 1572872 | tf_op jit(solution)/shard_map/ppermute | solution.py:51
  271.5 5.7 %collective-permute-done.19 = bf16[64,4096]{1,0:T(8,128)(2,1)S(1)} collective-permute-done((bf16[64,4096]{1,0:T(8,128)(2,1)S(1)}, bf16[64,4096]{1,0:T(8,128)(2,1)S(1)}, u32[]{:S(2)}, u32[]{:S(2)}) %collective-permute-start.19) | collective-permute-done | bytes 524320 | tf_op jit(solution)/shard_map/ppermute | solution.py:51
  277.2 7.1 %collective-permute-done.20 = bf16[64,4096]{1,0:T(8,128)(2,1)S(1)} collective-permute-done((bf16[64,4096]{1,0:T(8,128)(2,1)S(1)}, bf16[64,4096]{1,0:T(8,128)(2,1)S(1)}, u32[]{:S(2)}, u32[]{:S(2)}) %collective-permute-start.20) | collective-permute-done | bytes 524320 | tf_op jit(solution)/shard_map/ppermute | solution.py:51
  284.6 12.8 %all_to_all.32 = bf16[8,8,4096]{2,1,0:T(8,128)(2,1)S(1)} all-to-all(bf16[8,8,4096]{2,1,0:T(8,128)(2,1)S(1)} %fusion.1), channel_id=1, replica_groups=mesh['seq'=16,'exp'=8] {'exp'}, dimensions={0} | all-to-all | bytes 1048576 | tf_op jit(solution)/shard_map/all_to_all | solution.py:587
  297.4 1.2 convolution_add_fusion
  (88 shorter events, 3.5 us)
Async XLA Ops:
  6.5 39.4 %copy-start.14 = (f32[1024]{0:T(1024)S(1)}, f32[1024]{0:T(1024)}, u32[]{:S(2)}) copy-start(f32[1024]{0:T(1024)} %param.22) | copy-start | bytes 12292
  6.5 39.4 %copy-start.8 = (bf16[256,1024]{1,0:T(8,128)(2,1)S(1)}, bf16[256,1024]{1,0:T(8,128)(2,1)}, u32[]{:S(2)}) copy-start(bf16[256,1024]{1,0:T(8,128)(2,1)} %proj_hbm.1) | copy-start | bytes 1572868
  6.5 87.6 %all-gather.3.cloned.1.call-start = ((), (), s32[]{:S(2)}) async-start(), calls=%async_computation.6 | async-start | bytes 8912896 | tf_op jit(solution)/shard_map/all_gather | solution.py:402
  8.0 5.5 %collective-permute-start = (bf16[3,1024]{1,0:T(4,128)(2,1)S(1)}, bf16[3,1024]{1,0:T(4,128)(2,1)S(1)}, u32[]{:S(2)}, u32[]{:S(2)}) collective-permute-start(bf16[3,1024]{1,0:T(4,128)(2,1)S(1)} %slice.47), channel_id=1, source_target_pairs={{0,8},{8,16},{16,24},{24,32},{32,40},{40,48},{48,56},{56,64},{64,7... | collective-permute-start | bytes 18440 | tf_op jit(solution)/shard_map/ppermute | solution.py:57
  13.5 1.1 copy-start.6
  14.6 1.0 copy-start.7
  15.6 0.7 copy-start.12
  16.3 0.7 copy-start.13
  17.0 22.1 %copy-start.17 = (f32[1024,16]{0,1:T(8,128)S(1)}, f32[1024,16]{0,1:T(8,128)}, u32[]{:S(2)}) copy-start(f32[1024,16]{0,1:T(8,128)} %param.23) | copy-start | bytes 196612
  34.9 48.7 %copy-start.9 = (bf16[256,1024]{1,0:T(8,128)(2,1)S(1)}, bf16[256,1024]{1,0:T(8,128)(2,1)}, u32[]{:S(2)}) copy-start(bf16[256,1024]{1,0:T(8,128)(2,1)} %z_hbm.1) | copy-start | bytes 1572868
  34.9 48.7 %copy-start.15 = (f32[1024]{0:T(1024)S(1)}, f32[1024]{0:T(1024)}, u32[]{:S(2)}) copy-start(f32[1024]{0:T(1024)} %param.24) | copy-start | bytes 12292
  35.7 10.2 %all-to-all-start.1 = ((bf16[8,32,320]{2,1,0:T(8,128)(2,1)}), bf16[8,32,320]{2,1,0:T(8,128)(2,1)S(1)}, u32[]{:S(2)}, u32[]{:S(2)}) async-start(bf16[8,32,320]{2,1,0:T(8,128)(2,1)} %broadcast_in_dim.9), calls=%async_computation.1 | async-start | bytes 393216 | tf_op jit(solution)/shard_map/all_to_all | solution.py:433
  54.8 1.0 copy-start.2
  55.8 1.0 copy-start.4
  56.7 26.9 %copy-start.10 = (f32[16,8,1024]{2,1,0:T(8,128)}, f32[16,8,1024]{2,1,0:T(8,128)S(1)}, u32[]{:S(2)}) copy-start(f32[16,8,1024]{2,1,0:T(8,128)S(1)} %get-tuple-element.40.enter_hbm) | copy-start | bytes 1572868
  56.7 14.1 %all-to-all-start.2 = ((f32[16,2,1024]{2,1,0:T(2,128)}), f32[16,2,1024]{2,1,0:T(2,128)S(1)}, u32[]{:S(2)}, u32[]{:S(2)}) async-start(f32[16,2,1024]{2,1,0:T(2,128)} %get-tuple-element.36), calls=%async_computation.2 | async-start | bytes 262144 | tf_op jit(solution)/shard_map/all_to_all | solution.py:465
  71.5 12.1 %all-to-all-start.3 = ((f32[16,1,1024]{2,1,0:T(1,128)}), f32[16,1,1024]{2,1,0:T(1,128)S(1)}, u32[]{:S(2)}, u32[]{:S(2)}) async-start(f32[16,1,1024]{2,1,0:T(1,128)} %relay.1), calls=%async_computation.3 | async-start | bytes 131072 | tf_op jit(solution)/shard_map/all_to_all | solution.py:475
  83.7 1.2 copy-start.3
  84.9 1.2 copy-start.5
  86.1 1.0 copy-start.11
  94.2 8.5 %copy-start.18 = (s32[32,2]{0,1:T(2,128)S(1)}, s32[32,2]{0,1:T(2,128)}, u32[]{:S(2)}) copy-start(s32[32,2]{0,1:T(2,128)} %param.27) | copy-start | bytes 772
  94.2 17.0 %copy-start.19 = (f32[32,2]{0,1:T(2,128)S(1)}, f32[32,2]{0,1:T(2,128)}, u32[]{:S(2)}) copy-start(f32[32,2]{0,1:T(2,128)} %param.28) | copy-start | bytes 772
  94.2 29.4 %copy-start.16 = (bf16[32,4096]{1,0:T(8,128)(2,1)S(1)}, bf16[32,4096]{1,0:T(8,128)(2,1)}, u32[]{:S(2)}) copy-start(bf16[32,4096]{1,0:T(8,128)(2,1)} %param.26) | copy-start | bytes 786436
  94.2 62.3 %slice-start.2 = ((s8[6291456]{0:T(1024)(128)(4,1)}), s8[2097152]{0:T(1024)(128)(4,1)S(1)}, s32[]{:S(2)}) async-start(s8[6291456]{0:T(1024)(128)(4,1)} %bitcast.32), calls=%async_computation.9 | async-start | bytes 4194304
  101.4 1.3 copy-start.1
  102.7 2.9 collective-permute-start.1
  105.6 50.9 %slice-start = ((s8[6291456]{0:T(1024)(128)(4,1)}), s8[4194304]{0:T(1024)(128)(4,1)S(1)}, s32[]{:S(2)}) async-start(s8[6291456]{0:T(1024)(128)(4,1)} %bitcast.26), calls=%async_computation.7 | async-start | bytes 8388608
  105.6 50.9 %slice-start.3 = ((s8[6291456]{0:T(1024)(128)(4,1)}), s8[4194304]{0:T(1024)(128)(4,1)S(1)}, s32[]{:S(2)}) async-start(s8[6291456]{0:T(1024)(128)(4,1)} %bitcast.32), calls=%async_computation.10 | async-start | bytes 8388608
  107.7 15.2 %collective-permute-start.2 = (bf16[32,4096]{1,0:T(8,128)(2,1)S(1)}, bf16[32,4096]{1,0:T(8,128)(2,1)S(1)}, u32[]{:S(2)}, u32[]{:S(2)}) collective-permute-start(bf16[32,4096]{1,0:T(8,128)(2,1)S(1)} %get-tuple-element.75), channel_id=1, source_target_pairs={{0,2},{1,3},{2,4},{3,5},{4,6},{5,7},{6,0},{7,1},{8,10},{9,11},{10,... | collective-permute-start | bytes 786440 | tf_op jit(solution)/shard_map/ppermute | solution.py:533
  108.4 14.6 %collective-permute-start.3 = (bf16[32,4096]{1,0:T(8,128)(2,1)S(1)}, bf16[32,4096]{1,0:T(8,128)(2,1)S(1)}, u32[]{:S(2)}, u32[]{:S(2)}) collective-permute-start(bf16[32,4096]{1,0:T(8,128)(2,1)S(1)} %get-tuple-element.77), channel_id=1, source_target_pairs={{0,4},{1,5},{2,6},{3,7},{4,0},{5,1},{6,2},{7,3},{8,12},{9,13},{10,... | collective-permute-start | bytes 786440 | tf_op jit(solution)/shard_map/ppermute | solution.py:533
  110.4 13.2 %collective-permute-start.4 = (bf16[32,4096]{1,0:T(8,128)(2,1)S(1)}, bf16[32,4096]{1,0:T(8,128)(2,1)S(1)}, u32[]{:S(2)}, u32[]{:S(2)}) collective-permute-start(bf16[32,4096]{1,0:T(8,128)(2,1)S(1)} %get-tuple-element.76), channel_id=1, source_target_pairs={{0,6},{1,7},{2,0},{3,1},{4,2},{5,3},{6,4},{7,5},{8,14},{9,15},{10,... | collective-permute-start | bytes 786440 | tf_op jit(solution)/shard_map/ppermute | solution.py:533
  123.6 32.9 %slice-start.1 = ((s8[6291456]{0:T(1024)(128)(4,1)}), s8[2097152]{0:T(1024)(128)(4,1)S(1)}, s32[]{:S(2)}) async-start(s8[6291456]{0:T(1024)(128)(4,1)} %bitcast.26), calls=%async_computation.8 | async-start | bytes 4194304
  138.2 16.0 %collective-permute-start.5 = (bf16[64,4096]{1,0:T(8,128)(2,1)S(1)}, bf16[64,4096]{1,0:T(8,128)(2,1)S(1)}, u32[]{:S(2)}, u32[]{:S(2)}) collective-permute-start(bf16[64,4096]{1,0:T(8,128)(2,1)S(1)} %bitcast.51), channel_id=1, source_target_pairs={{0,32},{32,64},{64,96},{96,0},{8,40},{40,72},{72,104},{104,8},{16,... | collective-permute-start | bytes 1572872 | tf_op jit(solution)/shard_map/ppermute | solution.py:51
  138.5 15.6 %collective-permute-start.6 = (bf16[64,4096]{1,0:T(8,128)(2,1)S(1)}, bf16[64,4096]{1,0:T(8,128)(2,1)S(1)}, u32[]{:S(2)}, u32[]{:S(2)}) collective-permute-start(bf16[64,4096]{1,0:T(8,128)(2,1)S(1)} %bitcast.52), channel_id=1, source_target_pairs={{0,96},{32,0},{64,32},{96,64},{8,104},{40,8},{72,40},{104,72},{16,... | collective-permute-start | bytes 1572872 | tf_op jit(solution)/shard_map/ppermute | solution.py:51
  141.4 12.8 %collective-permute-start.7 = (bf16[64,4096]{1,0:T(8,128)(2,1)S(1)}, bf16[64,4096]{1,0:T(8,128)(2,1)S(1)}, u32[]{:S(2)}, u32[]{:S(2)}) collective-permute-start(bf16[64,4096]{1,0:T(8,128)(2,1)S(1)} %bitcast.53), channel_id=1, source_target_pairs={{0,64},{32,96},{64,0},{96,32},{8,72},{40,104},{72,8},{104,40},{16,... | collective-permute-start | bytes 1572872 | tf_op jit(solution)/shard_map/ppermute | solution.py:51
  154.4 26.1 %collective-permute-start.8 = (bf16[256,4096]{1,0:T(8,128)(2,1)S(1)}, bf16[256,4096]{1,0:T(8,128)(2,1)S(1)}, u32[]{:S(2)}, u32[]{:S(2)}) collective-permute-start(bf16[256,4096]{1,0:T(8,128)(2,1)S(1)} %pad_maximum_fusion.rows_ref), channel_id=1, source_target_pairs={{0,8},{8,16},{16,24},{24,0},{32,40},{40,48},{48,56},{56,32},{64,72... | collective-permute-start | bytes 6291464 | tf_op jit(solution)/shard_map/ppermute | solution.py:51
  156.5 27.2 %collective-permute-start.9 = (bf16[256,4096]{1,0:T(8,128)(2,1)S(1)}, bf16[256,4096]{1,0:T(8,128)(2,1)S(1)}, u32[]{:S(2)}, u32[]{:S(2)}) collective-permute-start(bf16[256,4096]{1,0:T(8,128)(2,1)S(1)} %pad_maximum_fusion.rows_ref), channel_id=1, source_target_pairs={{0,24},{8,0},{16,8},{24,16},{32,56},{40,32},{48,40},{56,48},{64,88... | collective-permute-start | bytes 6291464 | tf_op jit(solution)/shard_map/ppermute | solution.py:51
  156.5 2.8 copy-start
  183.8 22.4 %collective-permute-start.10 = (bf16[128,4096]{1,0:T(8,128)(2,1)S(1)}, bf16[128,4096]{1,0:T(8,128)(2,1)S(1)}, u32[]{:S(2)}, u32[]{:S(2)}) collective-permute-start(bf16[128,4096]{1,0:T(8,128)(2,1)S(1)} %slice.54), channel_id=1, source_target_pairs={{0,8},{8,16},{16,24},{24,0},{32,40},{40,48},{48,56},{56,32},{64,72... | collective-permute-start | bytes 3145736 | tf_op jit(solution)/shard_map/ppermute | solution.py:51
  184.0 22.2 %collective-permute-start.11 = (bf16[128,4096]{1,0:T(8,128)(2,1)S(1)}, bf16[128,4096]{1,0:T(8,128)(2,1)S(1)}, u32[]{:S(2)}, u32[]{:S(2)}) collective-permute-start(bf16[128,4096]{1,0:T(8,128)(2,1)S(1)} %slice.55), channel_id=1, source_target_pairs={{0,24},{8,0},{16,8},{24,16},{32,56},{40,32},{48,40},{56,48},{64,88... | collective-permute-start | bytes 3145736 | tf_op jit(solution)/shard_map/ppermute | solution.py:51
  194.5 20.4 %collective-permute-start.12 = (bf16[128,4096]{1,0:T(8,128)(2,1)S(1)}, bf16[128,4096]{1,0:T(8,128)(2,1)S(1)}, u32[]{:S(2)}, u32[]{:S(2)}) collective-permute-start(bf16[128,4096]{1,0:T(8,128)(2,1)S(1)} %get-tuple-element.54), channel_id=1, source_target_pairs={{0,24},{8,0},{16,8},{24,16},{32,56},{40,32},{48,40},{56,48},{64,88... | collective-permute-start | bytes 3145736 | tf_op jit(solution)/shard_map/ppermute | solution.py:51
  203.0 15.6 %collective-permute-start.13 = (bf16[128,4096]{1,0:T(8,128)(2,1)S(1)}, bf16[128,4096]{1,0:T(8,128)(2,1)S(1)}, u32[]{:S(2)}, u32[]{:S(2)}) collective-permute-start(bf16[128,4096]{1,0:T(8,128)(2,1)S(1)} %get-tuple-element.55), channel_id=1, source_target_pairs={{0,8},{8,16},{16,24},{24,0},{32,40},{40,48},{48,56},{56,32},{64,72... | collective-permute-start | bytes 3145736 | tf_op jit(solution)/shard_map/ppermute | solution.py:51
  218.6 16.0 %collective-permute-start.14 = (bf16[128,4096]{1,0:T(8,128)(2,1)S(1)}, bf16[128,4096]{1,0:T(8,128)(2,1)S(1)}, u32[]{:S(2)}, u32[]{:S(2)}) collective-permute-start(bf16[128,4096]{1,0:T(8,128)(2,1)S(1)} %get-tuple-element.58), channel_id=1, source_target_pairs={{0,8},{8,16},{16,24},{24,0},{32,40},{40,48},{48,56},{56,32},{64,72... | collective-permute-start | bytes 3145736 | tf_op jit(solution)/shard_map/ppermute | solution.py:51
  222.3 16.3 %collective-permute-start.17 = (bf16[128,4096]{1,0:T(8,128)(2,1)S(1)}, bf16[128,4096]{1,0:T(8,128)(2,1)S(1)}, u32[]{:S(2)}, u32[]{:S(2)}) collective-permute-start(bf16[128,4096]{1,0:T(8,128)(2,1)S(1)} %get-tuple-element.62), channel_id=1, source_target_pairs={{0,24},{8,0},{16,8},{24,16},{32,56},{40,32},{48,40},{56,48},{64,88... | collective-permute-start | bytes 3145736 | tf_op jit(solution)/shard_map/ppermute | solution.py:51
  234.9 16.1 %collective-permute-start.15 = (bf16[128,4096]{1,0:T(8,128)(2,1)S(1)}, bf16[128,4096]{1,0:T(8,128)(2,1)S(1)}, u32[]{:S(2)}, u32[]{:S(2)}) collective-permute-start(bf16[128,4096]{1,0:T(8,128)(2,1)S(1)} %add_convert_fusion.3), channel_id=1, source_target_pairs={{0,8},{8,16},{16,24},{24,0},{32,40},{40,48},{48,56},{56,32},{64,72... | collective-permute-start | bytes 3145736 | tf_op jit(solution)/shard_map/ppermute | solution.py:51
  238.9 18.7 %collective-permute-start.18 = (bf16[128,4096]{1,0:T(8,128)(2,1)S(1)}, bf16[128,4096]{1,0:T(8,128)(2,1)S(1)}, u32[]{:S(2)}, u32[]{:S(2)}) collective-permute-start(bf16[128,4096]{1,0:T(8,128)(2,1)S(1)} %add_convert_fusion.1), channel_id=1, source_target_pairs={{0,24},{8,0},{16,8},{24,16},{32,56},{40,32},{48,40},{56,48},{64,88... | collective-permute-start | bytes 3145736 | tf_op jit(solution)/shard_map/ppermute | solution.py:51
  251.5 20.1 %collective-permute-start.16 = (bf16[64,4096]{1,0:T(8,128)(2,1)S(1)}, bf16[64,4096]{1,0:T(8,128)(2,1)S(1)}, u32[]{:S(2)}, u32[]{:S(2)}) collective-permute-start(bf16[64,4096]{1,0:T(8,128)(2,1)S(1)} %slice.67), channel_id=1, source_target_pairs={{0,96},{32,0},{64,32},{96,64},{8,104},{40,8},{72,40},{104,72},{16,... | collective-permute-start | bytes 1572872 | tf_op jit(solution)/shard_map/ppermute | solution.py:51
  258.1 19.1 %collective-permute-start.19 = (bf16[64,4096]{1,0:T(8,128)(2,1)S(1)}, bf16[64,4096]{1,0:T(8,128)(2,1)S(1)}, u32[]{:S(2)}, u32[]{:S(2)}) collective-permute-start(bf16[64,4096]{1,0:T(8,128)(2,1)S(1)} %get-tuple-element.73), channel_id=1, source_target_pairs={{0,32},{32,64},{64,96},{96,0},{8,40},{40,72},{72,104},{104,8},{16,... | collective-permute-start | bytes 1572872 | tf_op jit(solution)/shard_map/ppermute | solution.py:51
  266.4 17.8 %collective-permute-start.20 = (bf16[64,4096]{1,0:T(8,128)(2,1)S(1)}, bf16[64,4096]{1,0:T(8,128)(2,1)S(1)}, u32[]{:S(2)}, u32[]{:S(2)}) collective-permute-start(bf16[64,4096]{1,0:T(8,128)(2,1)S(1)} %get-tuple-element.74), channel_id=1, source_target_pairs={{0,64},{32,96},{64,0},{96,32},{8,72},{40,104},{72,8},{104,40},{16,... | collective-permute-start | bytes 1572872 | tf_op jit(solution)/shard_map/ppermute | solution.py:51
Sparse Core Ops, SparseCore 0:
  9.5 74.7 all-gather.2

commit v3 on v1

--- a/solution.py
+++ b/solution.py
@@ -58,18 +58,21 @@
 
 
 def conv_kernel(
+    order_ref,
     x_hbm,
     weight_hbm,
     bias_hbm,
     proj_hbm,
     rim_ref,
     mixed_ref,
-    part_ref,
+    send_ref,
+    keep_ref,
     x_ref,
     weight_ref,
     bias_ref,
     proj_ref,
     padded,
+    part_ref,
     sems,
 ):
     sources = (x_hbm, weight_hbm, bias_hbm, proj_hbm)
@@ -108,6 +111,12 @@
         (((1,), (1,)), ((), ())),
         preferred_element_type=F32,
     )
+    half = SEG // 2
+    for place in range(SEG):
+        rows = pl.ds(pl.multiple_of(order_ref[place] * steps, steps), steps)
+        target = send_ref if place < half else keep_ref
+        first = place % half * steps
+        target[first : first + steps, :] = part_ref[rows, :]
 
 
 def spread(target, packed_ref, first):
@@ -118,23 +127,25 @@
 
 
 def scan_kernel(
-    packed_ref,
+    order_ref,
+    near_ref,
+    other_ref,
     mixed_ref,
     rates_ref,
     proj_hbm,
     bias_hbm,
+    packed_ref,
     y_ref,
     delta_ref,
+    msg_ref,
     before_hbm,
     enter_hbm,
-    msg_hbm,
     b_wide,
     c_wide,
     proj_ref,
     bias_ref,
     before_ref,
     enter_ref,
-    msg_ref,
     in_sems,
     out_sems,
 ):
@@ -146,6 +157,12 @@
     ]
     for copy in copies:
         copy.start()
+    half = SEG // 2
+    for place in range(half):
+        taken = slice(place * steps, (place + 1) * steps)
+        for source, slot in ((near_ref, place), (other_ref, place + half)):
+            rows = pl.ds(pl.multiple_of(order_ref[slot] * steps, steps), steps)
+            packed_ref[rows, :] = source[taken, :]
     spread(b_wide, packed_ref, 0)
     spread(c_wide, packed_ref, STATE)
     for copy in copies:
@@ -193,8 +210,8 @@
                 state = decay * shifted(state, by, 0.0) + state
                 decay = decay * shifted(decay, by, 1.0)
             enter_ref[n, :, lanes] = shifted(state, 1, 0.0)
-            msg_ref[n, 0:1, lanes] = state[SEG - 1 : SEG, :]
-            msg_ref[n, 1:2, lanes] = last
+            msg_ref[n : n + 1, lanes] = state[SEG - 1 : SEG, :]
+        msg_ref[STATE : STATE + 1, lanes] = last
         block = lane // LANES
         fresh = [
             pltpu.make_async_copy(
@@ -203,9 +220,6 @@
             pltpu.make_async_copy(
                 enter_ref.at[:, :, lanes], enter_hbm.at[:, :, lanes], out_sems.at[1, block]
             ),
-            pltpu.make_async_copy(
-                msg_ref.at[:, :, lanes], msg_hbm.at[:, :, lanes], out_sems.at[2, block]
-            ),
         ]
         for copy in fresh:
             copy.start()
@@ -214,12 +228,49 @@
         copy.wait()
 
 
-def relay_kernel(place_ref, ends_ref, rates_ref, out_ref):
-    rate = rates_ref[pl.ds(place_ref[0], 1), :]
-    state = jnp.zeros_like(rate)
-    for device in range(ends_ref.shape[0]):
-        out_ref[device] = state
-        state = jnp.exp2(ends_ref[device, 1:2, :] * rate) * state + ends_ref[device, 0:1, :]
+def meet_kernel(before_ref, own_ref, got_ref, prefix_ref, rates_ref, total_ref, next_ref):
+    partner_first = before_ref[0] > 0
+    rates = rates_ref[...]
+    own, got = own_ref[:STATE, :], got_ref[:STATE, :]
+    own_delta, got_delta = own_ref[STATE : STATE + 1, :], got_ref[STATE : STATE + 1, :]
+    prefix, prefix_delta = prefix_ref[:STATE, :], prefix_ref[STATE : STATE + 1, :]
+    late_delta = jnp.where(partner_first, own_delta, got_delta)
+    early = jnp.where(partner_first, got, own)
+    late = jnp.where(partner_first, own, got)
+    total_ref[:STATE, :] = jnp.exp2(late_delta * rates) * early + late
+    total_ref[STATE : STATE + 1, :] = own_delta + got_delta
+    joined = jnp.exp2(prefix_delta * rates) * got + prefix
+    next_ref[:STATE, :] = jnp.where(partner_first, joined, prefix)
+    next_ref[STATE : STATE + 1, :] = jnp.where(partner_first, prefix_delta + got_delta, prefix_delta)
+
+
+def entering_state(message, rates):
+    seqs = lax.axis_size("seq")
+    side = math.isqrt(seqs)
+    place = lax.axis_index("seq").astype(jnp.int32)
+    shape = jax.ShapeDtypeStruct(message.shape, F32)
+    prefix = jnp.zeros(message.shape, F32)
+
+    def flipped(index, axis, far_step):
+        x, y = index // side, index % side
+        value = x if axis == "x" else y
+        value = side - 1 - value if far_step else value + 1 - 2 * (value % 2)
+        return value * side + y if axis == "x" else x * side + value
+
+    for axis in ("y", "x"):
+        for far_step in (False, True):
+            route = [(i, flipped(i, axis, far_step)) for i in range(seqs)]
+            got = lax.ppermute(message, "seq", route)
+            before = (flipped(place, axis, far_step) < place).astype(jnp.int32).reshape(1)
+            message, prefix = pl.pallas_call(
+                meet_kernel,
+                out_shape=(shape, shape),
+                in_specs=[pl.BlockSpec(memory_space=pltpu.SMEM)] + [whole()] * 4,
+                out_specs=[whole()] * 2,
+                compiler_params=params(4),
+                name="meet",
+            )(before, message, got, prefix, rates)
+    return prefix
 
 
 def finish_kernel(
@@ -292,7 +343,7 @@
             ].astype(BF16)
 
 
-def outward_kernel(gated_ref, proj_hbm, send_ref, keep_ref, proj, arrived):
+def outward_kernel(order_ref, gated_ref, proj_hbm, send_ref, keep_ref, proj, arrived):
     parts, _, width = proj_hbm.shape
     middle = send_ref.shape[0]
     for part in range(parts):
@@ -300,7 +351,7 @@
 
     def product(part, carry):
         pltpu.make_async_copy(proj_hbm.at[part], proj.at[part], arrived.at[part]).wait()
-        columns = pl.ds(pl.multiple_of(part * width, width), width)
+        columns = pl.ds(pl.multiple_of(order_ref[part] * width, width), width)
         terms = jnp.dot(gated_ref[...], proj[part], preferred_element_type=F32)
         send_ref[:, columns] = terms[:middle].astype(BF16)
         keep_ref[:, columns] = terms[middle:]
@@ -377,14 +428,22 @@
     far_second = along(halves(ahead)[1], 1, -1)
     behind_first, behind_second = run(behind)
     early_first = along(behind_first, 1, -1)
+    far_first, far_second, behind_second = lax.optimization_barrier(
+        (far_first, far_second, behind_second)
+    )
+    across_first, across_second = run(jnp.concatenate([far_first, far_second], axis=0))
+    across_first, across_second, early_first = lax.optimization_barrier(
+        (across_first, across_second, early_first)
+    )
+    from_behind = along(across_first, 1, 1)
+    from_ahead = along(across_second, 1, -1)
     ahead_first, ahead_second = run(ahead)
     early_second = along(ahead_second, 1, 1)
-    far_first, far_second, behind_second, ahead_first = lax.optimization_barrier(
-        (far_first, far_second, behind_second, ahead_first)
-    )
-    across_first, across_second = run(jnp.concatenate([far_first, far_second], axis=0))
-    late_first = along(added(ahead_first, along(across_first, 1, 1)), 1, 1)
-    late_second = along(added(behind_second, along(across_second, 1, -1)), 1, -1)
+    from_behind, from_ahead, ahead_first = lax.optimization_barrier(
+        (from_behind, from_ahead, ahead_first)
+    )
+    late_first = along(added(ahead_first, from_behind), 1, 1)
+    late_second = along(added(behind_second, from_ahead), 1, -1)
     first = added(own_out[0], early_first, late_first)
     second = added(own_out[1], early_second, late_second)
     (kept, behind), (ahead, across) = halves(first), halves(second)
@@ -396,55 +455,77 @@
     steps = length // SEG
     owners = lax.axis_size("exp")
     seqs = lax.axis_size("seq")
-    columns = lax.all_gather(out_proj, "seq", axis=0)
+    side = owners // 2
+    owner = lax.axis_index("exp").astype(jnp.int32)
+    place = lax.axis_index("seq").astype(jnp.int32)
+    chip, core = owner // 2, owner % 2
+    swap = [(e, e + 1 - 2 * (e % 2)) for e in range(owners)]
+
+    def along_z(block, hop):
+        return lax.ppermute(block, "exp", [(e, (e + 2 * hop) % owners) for e in range(owners)])
+
+    hops = jnp.arange(side, dtype=jnp.int32)
+    onward, back = (chip + hops) % side, (chip - hops) % side
+    order = jnp.concatenate([onward * 2 + 1 - core, onward * 2 + core])
+    arrival = jnp.concatenate([back * 2 + core, back * 2 + 1 - core])
+
     rates = (-jnp.exp(a_log) * LOG2E).T
     rim = passed_along(x_in[length - (CONV - 1) :], "seq", 1)
-    mixed, partial = pl.pallas_call(
+    block = out_proj[None]
+    own_line = jnp.concatenate([block] + [along(block, 0, d) for d in (1, -1, 2)], axis=0)
+    columns = lax.all_gather(
+        own_line, ("seq", "exp"), axis_index_groups=lines(1), axis=0, tiled=True
+    )
+    grid_x, grid_y = place // side, place % side
+    shift = jnp.array([0, -1, 1, 2], dtype=jnp.int32)
+    fixed = jnp.arange(side, dtype=jnp.int32)[:, None]
+    by_x = ((grid_x + shift) % side)[None, :] * side + fixed
+    by_y = fixed * side + ((grid_y + shift) % side)[None, :]
+    column_order = jnp.where(core == 0, by_x, by_y).reshape(-1)
+
+    mixed, send, keep = pl.pallas_call(
         conv_kernel,
         out_shape=(
             jax.ShapeDtypeStruct((length, channels), F32),
-            jax.ShapeDtypeStruct((length, RANK + 2 * STATE), F32),
+            jax.ShapeDtypeStruct((length // 2, RANK + 2 * STATE), F32),
+            jax.ShapeDtypeStruct((length // 2, RANK + 2 * STATE), F32),
         ),
-        in_specs=[far()] * 4 + [whole()],
-        out_specs=[whole()] * 2,
+        in_specs=[pl.BlockSpec(memory_space=pltpu.SMEM)] + [far()] * 4 + [whole()],
+        out_specs=[whole()] * 3,
         scratch_shapes=[
             pltpu.VMEM(x_in.shape, BF16),
             pltpu.VMEM(conv_weight.shape, F32),
             pltpu.VMEM((1, channels), F32),
             pltpu.VMEM(x_proj.shape[::-1], BF16),
             pltpu.VMEM((channels // LANES, length + 8, LANES), F32),
+            pltpu.VMEM((length, RANK + 2 * STATE), F32),
             pltpu.SemaphoreType.DMA((4,)),
         ],
         compiler_params=params(12),
         name="conv",
-    )(x_in, conv_weight, conv_bias[None, :], x_proj.T, rim)
-    share = lax.all_to_all(
-        partial.reshape(owners, length // owners, -1), "exp", split_axis=0, concat_axis=0, tiled=True
-    )
-    summed = jnp.sum(share, axis=0)
-    low = summed[:, :RANK].astype(BF16)
+    )(order, x_in, conv_weight, conv_bias[None, :], x_proj.T, rim)
+    sums = (keep + lax.ppermute(send, "exp", swap)).reshape(side, length // owners, -1)
+    summed = sums[0]
+    for hop in range(1, side):
+        summed = summed + along_z(sums[hop], hop)
     coef = summed[:, RANK:]
     coef_high = coef.astype(BF16)
     coef_low = (coef - coef_high.astype(F32)).astype(BF16)
-    packed = jnp.concatenate([low, coef_high, coef_low], axis=1)
-    packed = lax.all_to_all(
-        jnp.broadcast_to(packed[None], (owners,) + packed.shape),
-        "exp",
-        split_axis=0,
-        concat_axis=0,
-        tiled=True,
-    ).reshape(length, -1)
-    y_local, delta, before, enter, message = pl.pallas_call(
+    near = jnp.concatenate([summed[:, :RANK].astype(BF16), coef_high, coef_low], axis=1)
+    near = jnp.concatenate([near] + [along_z(near, hop) for hop in range(1, side)], axis=0)
+    other = lax.ppermute(near, "exp", swap)
+    packed, y_local, delta, message, before, enter = pl.pallas_call(
         scan_kernel,
         out_shape=(
+            jax.ShapeDtypeStruct((length, RANK + 4 * STATE), BF16),
             jax.ShapeDtypeStruct((length, channels), F32),
             jax.ShapeDtypeStruct((length, channels), F32),
+            jax.ShapeDtypeStruct((STATE + 1, channels), F32),
             jax.ShapeDtypeStruct((SEG, channels), F32),
             jax.ShapeDtypeStruct((STATE, SEG, channels), F32),
-            jax.ShapeDtypeStruct((STATE, 2, channels), F32),
         ),
-        in_specs=[whole()] * 3 + [far()] * 2,
-        out_specs=[whole()] * 2 + [far()] * 3,
+        in_specs=[pl.BlockSpec(memory_space=pltpu.SMEM)] + [whole()] * 4 + [far()] * 2,
+        out_specs=[whole()] * 4 + [far()] * 2,
         scratch_shapes=[
             pltpu.VMEM((STATE, length, LANES), F32),
             pltpu.VMEM((STATE, length, LANES), F32),
@@ -452,28 +533,13 @@
             pltpu.VMEM((1, channels), F32),
             pltpu.VMEM((SEG, channels), F32),
             pltpu.VMEM((STATE, SEG, channels), F32),
-            pltpu.VMEM((STATE, 2, channels), F32),
             pltpu.SemaphoreType.DMA((2,)),
-            pltpu.SemaphoreType.DMA((3, channels // LANES)),
+            pltpu.SemaphoreType.DMA((2, channels // LANES)),
         ],
         compiler_params=params(14),
         name="scan",
-    )(packed, mixed, rates, dt_proj, dt_bias[None, :])
-    ends = lax.all_to_all(message, "seq", split_axis=0, concat_axis=0, tiled=True)
-    place = lax.axis_index("seq").astype(jnp.int32).reshape(1)
-    entering = pl.pallas_call(
-        relay_kernel,
-        out_shape=jax.ShapeDtypeStruct((seqs, 1, channels), F32),
-        in_specs=[pl.BlockSpec(memory_space=pltpu.SMEM), whole(), whole()],
-        out_specs=whole(),
-        compiler_params=params(4),
-        name="relay",
-    )(place, ends, rates)
-    entering = lax.all_to_all(entering, "seq", split_axis=0, concat_axis=0, tiled=True)
-    side = owners // 2
-    owner = lax.axis_index("exp").astype(jnp.int32)
-    chips = (owner // 2 + jnp.arange(side, dtype=jnp.int32)) % side
-    order = jnp.concatenate([chips * 2 + 1 - owner % 2, chips * 2 + owner % 2])
+    )(arrival, near, other, mixed, rates, dt_proj, dt_bias[None, :])
+    entering = entering_state(message, rates)
     gated = pl.pallas_call(
         finish_kernel,
         out_shape=jax.ShapeDtypeStruct((length, channels), BF16),
@@ -493,7 +559,7 @@
         name="finish",
     )(
         order,
-        entering.reshape(STATE, channels),
+        entering,
         rates,
         delta,
         packed,
@@ -512,7 +578,7 @@
             jax.ShapeDtypeStruct((length // 2, features), BF16),
             jax.ShapeDtypeStruct((length // 2, features), F32),
         ),
-        in_specs=[whole(), far()],
+        in_specs=[pl.BlockSpec(memory_space=pltpu.SMEM), whole(), far()],
         out_specs=[whole()] * 2,
         scratch_shapes=[
             pltpu.VMEM((seqs, channels, width), BF16),
@@ -520,14 +586,12 @@
         ],
         compiler_params=params(50),
         name="outward",
-    )(gated, columns)
-    swap = [(e, e + 1 - 2 * (e % 2)) for e in range(owners)]
+    )(column_order, gated, columns)
     sums = keep + lax.ppermute(send, "exp", swap).astype(F32)
     sums = sums.reshape(side, length // owners, features)
     total = sums[0]
     for hop in range(1, side):
-        route = [(e, (e + 2 * hop) % owners) for e in range(owners)]
-        total = total + lax.ppermute(sums[hop].astype(BF16), "exp", route).astype(F32)
+        total = total + along_z(sums[hop].astype(BF16), hop).astype(F32)
     return total
 
 

time: 303 us -> 307 us (1.013)
  waiting for transfers between devices: 119 us -> 133 us
  blocking collectives: 40.8 us -> 26.9 us
  local copies, waits for them, and re-layouts: 15.5 us -> 11.7 us
    ppermute x3 -> x15, waiting for transfers between devices: 12.3 us -> 38.5 us  [the longest x9 17.9 us: along_z(): lax.ppermute(block, 'exp', [(e, (e + 2 * hop) % owners) for e in range(ow...]
    all_to_all x3 -> x0, waiting for transfers between devices: 19.7 us -> none  [the longest x1 6.94 us: mixer(): lax.all_to_all(message, 'seq', split_axis=0, concat_axis=0, tiled=True)]
    all_to_all x3 -> x0, starting transfers between devices: 16.6 us -> none  [the longest x1 7.17 us: mixer(): lax.all_to_all(message, 'seq', split_axis=0, concat_axis=0, tiled=True)]
    ppermute x3 -> x15, starting transfers between devices: 3.41 us -> 19.9 us  [the longest x9 15.1 us: along_z(): lax.ppermute(block, 'exp', [(e, (e + 2 * hop) % owners) for e in range(ow...]
    all_to_all x1 -> x0, blocking collectives: 14.1 us -> none  [mixer(): lax.all_to_all(partial.reshape(owners, length // owners, -1), 'exp', spli...]
    ppermute x16 -> x19, waiting for transfers between devices: 81.5 us -> 89.9 us  [along(): return lax.ppermute(block, ('seq', 'exp'), route)]
    unnamed x50 -> x47, local copies, waits for them, and re-layouts: 13.2 us -> 10.8 us
    ppermute x16 -> x19, starting transfers between devices: 22.3 us -> 24.1 us  [along(): return lax.ppermute(block, ('seq', 'exp'), route)]
  transfers between devices with their start and end apart: 25 -> 37, of which waited for: 17 -> 32; matrix products, arithmetic and copies ran while one was open for 1% -> 1% of each run, Pallas kernels for 15% -> 18%
where the time goes in v3:
time: 307 us; the launch traced here: 304 us
  waiting for transfers between devices  133 us (43%)
  Pallas kernels  62.2 us (20%)
  starting transfers between devices  47 us (15%)
  blocking collectives  26.9 us (9%)
  between operations  13.9 us (5%)
  local copies, waits for them, and re-layouts  11.7 us (4%)
  other arithmetic  8.05 us (3%)
    ppermute x19, waiting for transfers between devices, along(): return lax.ppermute(block, ('seq', 'exp'), route)  89.9 us
    pallas_call x4, Pallas kernels, expert(): pl.pallas_call(expert_kernel, out_shape=(jax.ShapeDtypeStruct((count // 2...  33.5 us
    ppermute x19, starting transfers between devices, along(): return lax.ppermute(block, ('seq', 'exp'), route)  24.1 us
    ppermute x9, waiting for transfers between devices, along_z(): lax.ppermute(block, 'exp', [(e, (e + 2 * hop) % owners) for e in range(ow...  17.9 us
    ppermute x4, waiting for transfers between devices, entering_state(): got = lax.ppermute(message, 'seq', route)  17.9 us
    ppermute x9, starting transfers between devices, along_z(): lax.ppermute(block, 'exp', [(e, (e + 2 * hop) % owners) for e in range(ow...  15.1 us
    all_to_all x1, blocking collectives, shards(): lax.all_to_all(outgoing, 'exp', split_axis=0, concat_axis=0, tiled=True)  14.1 us
    all_to_all x1, blocking collectives, shards(): lax.all_to_all(expert_out, 'exp', split_axis=0, concat_axis=0, tiled=True)  12.8 us
  transfers between devices with their start and end apart: 37, of which 32 were waited for; matrix products, arithmetic and copies ran while one was open for 1% of the time, Pallas kernels for 18%

profile of v3, /device:TPU:24, one launch (start us, length us, event | category | flops | bytes accessed | tf_op | source)
XLA Modules:
  0.0 304.1 jit_solution(10327953987706066358)
XLA Ops:
  6.5 1.5 collective-permute-start.13
  8.0 1.7 collective-permute-start.14
  9.8 1.8 collective-permute-start.15
  11.6 5.6 %collective-permute-done.13 = bf16[1,1024,256]{2,1,0:T(8,128)(2,1)S(1)} collective-permute-done((bf16[1,1024,256]{2,1,0:T(8,128)(2,1)}, bf16[1,1024,256]{2,1,0:T(8,128)(2,1)S(1)}, u32[]{:S(2)}, u32[]{:S(2)}) %collective-permute-start.13) | collective-permute-done | bytes 524320 | tf_op jit(solution)/shard_map/ppermute | solution.py:51
  17.1 5.3 %collective-permute-done.14 = bf16[1,1024,256]{2,1,0:T(8,128)(2,1)S(1)} collective-permute-done((bf16[1,1024,256]{2,1,0:T(8,128)(2,1)}, bf16[1,1024,256]{2,1,0:T(8,128)(2,1)S(1)}, u32[]{:S(2)}, u32[]{:S(2)}) %collective-permute-start.14) | collective-permute-done | bytes 524320 | tf_op jit(solution)/shard_map/ppermute | solution.py:51
  22.4 1.3 collective-permute-done.15
  23.7 2.6 pad_maximum_fusion
  27.4 3.0 collective-permute-start
  30.5 2.4 collective-permute-done.rim_ref
  33.0 4.4 %conv.1 = (f32[256,1024]{1,0:T(8,128)S(1)}, f32[128,288]{1,0:T(8,128)S(1)}, f32[128,288]{1,0:T(8,128)S(1)}) custom-call(s32[8]{0:T(128)S(1)} %pad_add_fusion.order_ref, bf16[256,1024]{1,0:T(8,128)(2,1)S(1)} %copy-done.7, f32[4,1024]{1,0:T(4,128)S(1)} %copy-done.10, f32[1,1024]{1,0:T(1,128)S(1)} %bitcast.41, bf16[288,1024]{1,0:T(8,128)(2,1)S(1)} %bitcast.40, ...), custom_call_target="tpu_custom_call" | custom-call | tf_op jit(solution)/shard_map/conv/pallas_call | solution.py:486
  37.4 1.4 collective-permute-done.1
  38.9 2.0 collective-permute-start.2
  40.9 3.6 %collective-permute-start.3 = (f32[32,288]{1,0:T(8,128)S(1)}, f32[32,288]{1,0:T(8,128)S(1)}, u32[]{:S(2)}, u32[]{:S(2)}) collective-permute-start(f32[32,288]{1,0:T(8,128)S(1)} %get-tuple-element.100), channel_id=1, source_target_pairs={{0,4},{1,5},{2,6},{3,7},{4,0},{5,1},{6,2},{7,3},{8,12},{9,13},{10,... | collective-permute-start | bytes 110600 | tf_op jit(solution)/shard_map/ppermute | solution.py:465
  45.6 1.7 collective-permute-done.3
  47.3 1.3 collective-permute-done.4
  48.7 3.7 %collective-permute-start.6 = (bf16[32,320]{1,0:T(8,128)(2,1)S(1)}, bf16[32,320]{1,0:T(8,128)(2,1)S(1)}, u32[]{:S(2)}, u32[]{:S(2)}) collective-permute-start(bf16[32,320]{1,0:T(8,128)(2,1)S(1)} %pad_maximum_fusion.4), channel_id=1, source_target_pairs={{0,4},{1,5},{2,6},{3,7},{4,0},{5,1},{6,2},{7,3},{8,12},{9,13},{10,... | collective-permute-start | bytes 61448 | tf_op jit(solution)/shard_map/ppermute | solution.py:465
  54.5 1.8 collective-permute-done.7
  56.4 1.2 collective-permute-done.8.other_ref
  57.6 1.1 copy-done.9
  58.7 8.8 %scan.1 = (bf16[256,320]{1,0:T(8,128)(2,1)S(1)}, f32[256,1024]{1,0:T(8,128)S(1)}, f32[256,1024]{1,0:T(8,128)S(1)}, f32[17,1024]{1,0:T(8,128)S(1)}, f32[8,1024]{1,0:T(8,128)S(1)}, /*index=5*/f32[16,8,1024]{2,1,0:T(8,128)S(1)}) custom-call(s32[8]{0:T(128)S(1)} %pad_add_fusion.1.order_ref, bf16[128,320]{1,0:T(8,128)(2,1)S(1)} %pad_maximum_fusion.3.near_ref, ...), custom_call_target="tpu_custom_call" | custom-call | tf_op jit(solution)/shard_map/scan/pallas_call | solution.py:517
  70.3 5.5 %collective-permute-done.9.got_ref = f32[17,1024]{1,0:T(8,128)S(1)} collective-permute-done((f32[17,1024]{1,0:T(8,128)S(1)}, f32[17,1024]{1,0:T(8,128)S(1)}, u32[]{:S(2)}, u32[]{:S(2)}) %collective-permute-start.9) | collective-permute-done | bytes 69664 | tf_op jit(solution)/shard_map/ppermute | solution.py:263
  76.0 5.8 %collective-permute-done.10.got_ref = f32[17,1024]{1,0:T(8,128)S(1)} collective-permute-done((f32[17,1024]{1,0:T(8,128)S(1)}, f32[17,1024]{1,0:T(8,128)S(1)}, u32[]{:S(2)}, u32[]{:S(2)}) %collective-permute-start.10) | collective-permute-done | bytes 69664 | tf_op jit(solution)/shard_map/ppermute | solution.py:263
  81.8 1.5 collective-permute-start.11
  83.4 3.1 %collective-permute-done.11.got_ref = f32[17,1024]{1,0:T(8,128)S(1)} collective-permute-done((f32[17,1024]{1,0:T(8,128)S(1)}, f32[17,1024]{1,0:T(8,128)S(1)}, u32[]{:S(2)}, u32[]{:S(2)}) %collective-permute-start.11) | collective-permute-done | bytes 69664 | tf_op jit(solution)/shard_map/ppermute | solution.py:263
  86.5 2.3 collective-permute-start.12
  89.0 3.4 %collective-permute-done.12.got_ref = f32[17,1024]{1,0:T(8,128)S(1)} collective-permute-done((f32[17,1024]{1,0:T(8,128)S(1)}, f32[17,1024]{1,0:T(8,128)S(1)}, u32[]{:S(2)}, u32[]{:S(2)}) %collective-permute-start.12) | collective-permute-done | bytes 69664 | tf_op jit(solution)/shard_map/ppermute | solution.py:263
  93.1 1.2 copy-done.3
  94.4 1.2 copy-done.5
  95.6 7.0 %finish.1.gated_ref = bf16[256,1024]{1,0:T(8,128)(2,1)S(1)} custom-call(s32[8]{0:T(128)S(1)} %pad_add_fusion.order_ref, f32[17,1024]{1,0:T(8,128)S(1)} %get-tuple-element.54.entering_ref, f32[16,1024]{1,0:T(8,128)S(1)} %multiply_bitcast_fusion.rates_ref, f32[256,1024]{1,0:T(8,128)S(1)} %copy-done.5, bf16[256,320]{1,0:T(8,128)(2,1)S(1)} %get-tuple-element.56.packed_ref, ...), custom_call_target="tpu_custom_call" | custom-call | tf_op jit(solution)/shard_map/finish/pallas_call | solution.py:543
  102.7 7.8 %outward.1 = (bf16[128,4096]{1,0:T(8,128)(2,1)}, f32[128,4096]{1,0:T(8,128)S(1)}) custom-call(s32[16]{0:T(128)S(1)} %select_n.75.order_ref, bf16[256,1024]{1,0:T(8,128)(2,1)S(1)} %finish.1.gated_ref, bf16[16,1024,256]{2,1,0:T(8,128)(2,1)} %all-gather.2.cloned.1.call-done.proj_hbm), custom_call_target="tpu_custom_call" | custom-call | tf_op jit(solution)/shard_map/outward/pallas_call | solution.py:575
  110.4 1.3 copy-done.1
  112.7 1.9 collective-permute-done.16
  114.6 2.1 fusion.21
  117.4 2.7 collective-permute-start.18
  121.3 10.9 %collective-permute-done.17 = bf16[32,4096]{1,0:T(8,128)(2,1)S(1)} collective-permute-done((bf16[32,4096]{1,0:T(8,128)(2,1)S(1)}, bf16[32,4096]{1,0:T(8,128)(2,1)S(1)}, u32[]{:S(2)}, u32[]{:S(2)}) %collective-permute-start.17) | collective-permute-done | bytes 262176 | tf_op jit(solution)/shard_map/ppermute | solution.py:465
  133.5 14.1 %all_to_all.10 = bf16[8,8,4096]{2,1,0:T(8,128)(2,1)S(1)} all-to-all(bf16[8,8,4096]{2,1,0:T(8,128)(2,1)S(1)} %fusion), channel_id=1, replica_groups=mesh['seq'=16,'exp'=8] {'exp'}, dimensions={0} | all-to-all | bytes 1048576 | tf_op jit(solution)/shard_map/all_to_all | solution.py:645
  147.8 3.0 collective-permute-start.21
  151.3 6.7 %collective-permute-done.20 = bf16[64,4096]{1,0:T(8,128)(2,1)S(1)} collective-permute-done((bf16[64,4096]{1,0:T(8,128)(2,1)S(1)}, bf16[64,4096]{1,0:T(8,128)(2,1)S(1)}, u32[]{:S(2)}, u32[]{:S(2)}) %collective-permute-start.20) | collective-permute-done | bytes 524320 | tf_op jit(solution)/shard_map/ppermute | solution.py:51
  158.0 5.2 %collective-permute-done.21 = bf16[64,4096]{1,0:T(8,128)(2,1)S(1)} collective-permute-done((bf16[64,4096]{1,0:T(8,128)(2,1)S(1)}, bf16[64,4096]{1,0:T(8,128)(2,1)S(1)}, u32[]{:S(2)}, u32[]{:S(2)}) %collective-permute-start.21) | collective-permute-done | bytes 524320 | tf_op jit(solution)/shard_map/ppermute | solution.py:51
  164.3 2.4 collective-permute-start.23
  166.7 2.8 copy-done
  169.5 8.4 %expert.4 = (bf16[128,4096]{1,0:T(8,128)(2,1)S(1)}, bf16[128,4096]{1,0:T(8,128)(2,1)S(1)}) custom-call(bf16[256,4096]{1,0:T(8,128)(2,1)S(1)} %pad_maximum_fusion.1.rows_ref, bf16[4096,768]{1,0:T(8,128)(2,1)S(1)} %bitcast.26, bf16[4096,768]{1,0:T(8,128)(2,1)S(1)} %bitcast.32, bf16[768,4096]{1,0:T(8,128)(2,1)S(1)} %bitcast.36), custom_call_target="tpu_custom_call" | custom-call | flops 4831838208 | bytes 4194304 | tf_op jit(solution)/shard_map/expert/pallas_call | solution.py:389
  177.9 12.5 %collective-permute-done.23.rows_ref = bf16[256,4096]{1,0:T(8,128)(2,1)S(1)} collective-permute-done((bf16[256,4096]{1,0:T(8,128)(2,1)S(1)}, bf16[256,4096]{1,0:T(8,128)(2,1)S(1)}, u32[]{:S(2)}, u32[]{:S(2)}) %collective-permute-start.23) | collective-permute-done | bytes 2097184 | tf_op jit(solution)/shard_map/ppermute | solution.py:51
  190.4 3.5 %collective-permute-done.24.rows_ref = bf16[256,4096]{1,0:T(8,128)(2,1)S(1)} collective-permute-done((bf16[256,4096]{1,0:T(8,128)(2,1)S(1)}, bf16[256,4096]{1,0:T(8,128)(2,1)S(1)}, u32[]{:S(2)}, u32[]{:S(2)}) %collective-permute-start.24) | collective-permute-done | bytes 2097184 | tf_op jit(solution)/shard_map/ppermute | solution.py:51
  194.2 2.1 collective-permute-start.26
  196.3 8.4 %expert.5 = (bf16[128,4096]{1,0:T(8,128)(2,1)S(1)}, bf16[128,4096]{1,0:T(8,128)(2,1)S(1)}) custom-call(bf16[256,4096]{1,0:T(8,128)(2,1)S(1)} %collective-permute-done.23.rows_ref, bf16[4096,768]{1,0:T(8,128)(2,1)S(1)} %bitcast.27, bf16[4096,768]{1,0:T(8,128)(2,1)S(1)} %bitcast.33, bf16[768,4096]{1,0:T(8,128)(2,1)S(1)} %bitcast.37), custom_call_target="tpu_custom_call" | custom-call | flops 4831838208 | bytes 4194304 | tf_op jit(solution)/shard_map/expert/pallas_call | solution.py:389
  204.8 4.1 %collective-permute-done.25 = bf16[128,4096]{1,0:T(8,128)(2,1)S(1)} collective-permute-done((bf16[128,4096]{1,0:T(8,128)(2,1)S(1)}, bf16[128,4096]{1,0:T(8,128)(2,1)S(1)}, u32[]{:S(2)}, u32[]{:S(2)}) %collective-permute-start.25) | collective-permute-done | bytes 1048608 | tf_op jit(solution)/shard_map/ppermute | solution.py:51
  208.9 1.4 collective-permute-done.26
  210.5 8.4 %expert.6 = (bf16[128,4096]{1,0:T(8,128)(2,1)S(1)}, bf16[128,4096]{1,0:T(8,128)(2,1)S(1)}) custom-call(bf16[256,4096]{1,0:T(8,128)(2,1)S(1)} %pad_maximum_fusion.2.rows_ref, bf16[4096,768]{1,0:T(8,128)(2,1)S(1)} %bitcast.28, bf16[4096,768]{1,0:T(8,128)(2,1)S(1)} %bitcast.34, bf16[768,4096]{1,0:T(8,128)(2,1)S(1)} %bitcast.38), custom_call_target="tpu_custom_call" | custom-call | flops 4831838208 | bytes 4194304 | tf_op jit(solution)/shard_map/expert/pallas_call | solution.py:389
  218.9 2.6 collective-permute-done.27
  221.5 2.0 collective-permute-start.29
  223.5 8.4 %expert.7 = (bf16[128,4096]{1,0:T(8,128)(2,1)S(1)}, bf16[128,4096]{1,0:T(8,128)(2,1)S(1)}) custom-call(bf16[256,4096]{1,0:T(8,128)(2,1)S(1)} %collective-permute-done.24.rows_ref, bf16[4096,768]{1,0:T(8,128)(2,1)S(1)} %bitcast.29, bf16[4096,768]{1,0:T(8,128)(2,1)S(1)} %bitcast.35, bf16[768,4096]{1,0:T(8,128)(2,1)S(1)} %bitcast.39), custom_call_target="tpu_custom_call" | custom-call | flops 4831838208 | bytes 4194304 | tf_op jit(solution)/shard_map/expert/pallas_call | solution.py:389
  231.9 4.4 %collective-permute-done.28 = bf16[128,4096]{1,0:T(8,128)(2,1)S(1)} collective-permute-done((bf16[128,4096]{1,0:T(8,128)(2,1)S(1)}, bf16[128,4096]{1,0:T(8,128)(2,1)S(1)}, u32[]{:S(2)}, u32[]{:S(2)}) %collective-permute-start.28) | collective-permute-done | bytes 1048608 | tf_op jit(solution)/shard_map/ppermute | solution.py:51
  236.3 1.2 collective-permute-done.29
  238.1 2.0 collective-permute-start.32
  240.4 12.2 %collective-permute-done.30 = bf16[128,4096]{1,0:T(8,128)(2,1)S(1)} collective-permute-done((bf16[128,4096]{1,0:T(8,128)(2,1)S(1)}, bf16[128,4096]{1,0:T(8,128)(2,1)S(1)}, u32[]{:S(2)}, u32[]{:S(2)}) %collective-permute-start.30) | collective-permute-done | bytes 1048608 | tf_op jit(solution)/shard_map/ppermute | solution.py:51
  253.2 2.2 collective-permute-start.31
  255.4 10.2 %collective-permute-done.32 = bf16[128,4096]{1,0:T(8,128)(2,1)S(1)} collective-permute-done((bf16[128,4096]{1,0:T(8,128)(2,1)S(1)}, bf16[128,4096]{1,0:T(8,128)(2,1)S(1)}, u32[]{:S(2)}, u32[]{:S(2)}) %collective-permute-start.32) | collective-permute-done | bytes 1048608 | tf_op jit(solution)/shard_map/ppermute | solution.py:51
  266.1 2.7 collective-permute-start.34
  268.9 1.3 collective-permute-start.35
  270.2 6.4 %collective-permute-done.34 = bf16[64,4096]{1,0:T(8,128)(2,1)S(1)} collective-permute-done((bf16[64,4096]{1,0:T(8,128)(2,1)S(1)}, bf16[64,4096]{1,0:T(8,128)(2,1)S(1)}, u32[]{:S(2)}, u32[]{:S(2)}) %collective-permute-start.34) | collective-permute-done | bytes 524320 | tf_op jit(solution)/shard_map/ppermute | solution.py:51
  276.6 6.4 %collective-permute-done.35 = bf16[64,4096]{1,0:T(8,128)(2,1)S(1)} collective-permute-done((bf16[64,4096]{1,0:T(8,128)(2,1)S(1)}, bf16[64,4096]{1,0:T(8,128)(2,1)S(1)}, u32[]{:S(2)}, u32[]{:S(2)}) %collective-permute-start.35) | collective-permute-done | bytes 524320 | tf_op jit(solution)/shard_map/ppermute | solution.py:51
  283.3 12.8 %all_to_all.11 = bf16[8,8,4096]{2,1,0:T(8,128)(2,1)S(1)} all-to-all(bf16[8,8,4096]{2,1,0:T(8,128)(2,1)S(1)} %fusion.1), channel_id=1, replica_groups=mesh['seq'=16,'exp'=8] {'exp'}, dimensions={0} | all-to-all | bytes 1048576 | tf_op jit(solution)/shard_map/all_to_all | solution.py:648
  296.1 1.2 convolution_add_fusion
  (120 shorter events, 17.2 us)
Async XLA Ops:
  6.5 96.1 %all-gather.2.cloned.1.call-start = ((), (), s32[]{:S(2)}) async-start(), calls=%async_computation.2 | async-start | bytes 10485760 | tf_op jit(solution)/shard_map/all_gather | solution.py:476
  6.5 10.6 %collective-permute-start.13 = (bf16[1,1024,256]{2,1,0:T(8,128)(2,1)}, bf16[1,1024,256]{2,1,0:T(8,128)(2,1)S(1)}, u32[]{:S(2)}, u32[]{:S(2)}) collective-permute-start(bf16[1,1024,256]{2,1,0:T(8,128)(2,1)} %bitcast.48), channel_id=1, source_target_pairs={{0,32},{32,64},{64,96},{96,0},{8,40},{40,72},{72,104},{104,8},{16,... | collective-permute-start | bytes 1572872 | tf_op jit(solution)/shard_map/ppermute | solution.py:51
  8.0 14.4 %collective-permute-start.14 = (bf16[1,1024,256]{2,1,0:T(8,128)(2,1)}, bf16[1,1024,256]{2,1,0:T(8,128)(2,1)S(1)}, u32[]{:S(2)}, u32[]{:S(2)}) collective-permute-start(bf16[1,1024,256]{2,1,0:T(8,128)(2,1)} %bitcast.49), channel_id=1, source_target_pairs={{0,96},{32,0},{64,32},{96,64},{8,104},{40,8},{72,40},{104,72},{16,... | collective-permute-start | bytes 1572872 | tf_op jit(solution)/shard_map/ppermute | solution.py:51
  9.8 14.0 %collective-permute-start.15 = (bf16[1,1024,256]{2,1,0:T(8,128)(2,1)}, bf16[1,1024,256]{2,1,0:T(8,128)(2,1)S(1)}, u32[]{:S(2)}, u32[]{:S(2)}) collective-permute-start(bf16[1,1024,256]{2,1,0:T(8,128)(2,1)} %bitcast.50), channel_id=1, source_target_pairs={{0,64},{32,96},{64,0},{96,32},{8,72},{40,104},{72,8},{104,40},{16,... | collective-permute-start | bytes 1572872 | tf_op jit(solution)/shard_map/ppermute | solution.py:51
  26.4 1.0 copy-start.7
  26.4 6.6 %copy-start.6 = (bf16[1024,288]{0,1:T(8,128)(2,1)S(1)}, bf16[1024,288]{0,1:T(8,128)(2,1)}, u32[]{:S(2)}) copy-start(bf16[1024,288]{0,1:T(8,128)(2,1)} %param.21) | copy-start | bytes 1769476
  26.4 6.6 %copy-start.10 = (f32[4,1024]{1,0:T(4,128)S(1)}, f32[4,1024]{1,0:T(4,128)}, u32[]{:S(2)}) copy-start(f32[4,1024]{1,0:T(4,128)} %weight_hbm.1) | copy-start | bytes 49156
  26.4 6.6 %copy-start.11 = (f32[1024]{0:T(1024)S(1)}, f32[1024]{0:T(1024)}, u32[]{:S(2)}) copy-start(f32[1024]{0:T(1024)} %param.20) | copy-start | bytes 12292
  26.4 19.1 %copy-start.15 = (f32[1024,16]{0,1:T(8,128)S(1)}, f32[1024,16]{0,1:T(8,128)}, u32[]{:S(2)}) copy-start(f32[1024,16]{0,1:T(8,128)} %param.24) | copy-start | bytes 196612
  26.4 31.3 %copy-start.12 = (f32[1024]{0:T(1024)S(1)}, f32[1024]{0:T(1024)}, u32[]{:S(2)}) copy-start(f32[1024]{0:T(1024)} %param.23) | copy-start | bytes 12292
  27.4 5.5 %collective-permute-start = (bf16[3,1024]{1,0:T(4,128)(2,1)S(1)}, bf16[3,1024]{1,0:T(4,128)(2,1)S(1)}, u32[]{:S(2)}, u32[]{:S(2)}) collective-permute-start(bf16[3,1024]{1,0:T(4,128)(2,1)S(1)} %slice.63), channel_id=1, source_target_pairs={{0,8},{8,16},{16,24},{24,32},{32,40},{40,48},{48,56},{56,64},{64,7... | collective-permute-start | bytes 18440 | tf_op jit(solution)/shard_map/ppermute | solution.py:57
  37.4 1.5 collective-permute-start.1
  38.9 44.4 %copy-start.18 = (s32[4]{0:T(128)S(1)}, s32[4]{0:T(128)}, u32[]{:S(2)}) copy-start(s32[4]{0:T(128)} %constant.125.clone) | copy-start | bytes 52
  38.9 6.6 %collective-permute-start.2 = (f32[32,288]{1,0:T(8,128)S(1)}, f32[32,288]{1,0:T(8,128)S(1)}, u32[]{:S(2)}, u32[]{:S(2)}) collective-permute-start(f32[32,288]{1,0:T(8,128)S(1)} %get-tuple-element.98), channel_id=1, source_target_pairs={{0,2},{1,3},{2,4},{3,5},{4,6},{5,7},{6,0},{7,1},{8,10},{9,11},{10,... | collective-permute-start | bytes 110600 | tf_op jit(solution)/shard_map/ppermute | solution.py:465
  40.9 6.4 %collective-permute-start.3 = (f32[32,288]{1,0:T(8,128)S(1)}, f32[32,288]{1,0:T(8,128)S(1)}, u32[]{:S(2)}, u32[]{:S(2)}) collective-permute-start(f32[32,288]{1,0:T(8,128)S(1)} %get-tuple-element.100), channel_id=1, source_target_pairs={{0,4},{1,5},{2,6},{3,7},{4,0},{5,1},{6,2},{7,3},{8,12},{9,13},{10,... | collective-permute-start | bytes 110600 | tf_op jit(solution)/shard_map/ppermute | solution.py:465
  44.5 4.1 %collective-permute-start.4 = (f32[32,288]{1,0:T(8,128)S(1)}, f32[32,288]{1,0:T(8,128)S(1)}, u32[]{:S(2)}, u32[]{:S(2)}) collective-permute-start(f32[32,288]{1,0:T(8,128)S(1)} %get-tuple-element.99), channel_id=1, source_target_pairs={{0,6},{1,7},{2,0},{3,1},{4,2},{5,3},{6,4},{7,5},{8,14},{9,15},{10,... | collective-permute-start | bytes 110600 | tf_op jit(solution)/shard_map/ppermute | solution.py:465
  45.5 47.6 %copy-start.8 = (bf16[256,1024]{1,0:T(8,128)(2,1)S(1)}, bf16[256,1024]{1,0:T(8,128)(2,1)}, u32[]{:S(2)}) copy-start(bf16[256,1024]{1,0:T(8,128)(2,1)} %z_hbm.1) | copy-start | bytes 1572868
  45.5 47.6 %copy-start.13 = (f32[1024]{0:T(1024)S(1)}, f32[1024]{0:T(1024)}, u32[]{:S(2)}) copy-start(f32[1024]{0:T(1024)} %param.25) | copy-start | bytes 12292
  48.7 5.0 %collective-permute-start.5 = (bf16[32,320]{1,0:T(8,128)(2,1)S(1)}, bf16[32,320]{1,0:T(8,128)(2,1)S(1)}, u32[]{:S(2)}, u32[]{:S(2)}) collective-permute-start(bf16[32,320]{1,0:T(8,128)(2,1)S(1)} %pad_maximum_fusion.4), channel_id=1, source_target_pairs={{0,2},{1,3},{2,4},{3,5},{4,6},{5,7},{6,0},{7,1},{8,10},{9,11},{10,... | collective-permute-start | bytes 61448 | tf_op jit(solution)/shard_map/ppermute | solution.py:465
  48.7 5.7 %collective-permute-start.6 = (bf16[32,320]{1,0:T(8,128)(2,1)S(1)}, bf16[32,320]{1,0:T(8,128)(2,1)S(1)}, u32[]{:S(2)}, u32[]{:S(2)}) collective-permute-start(bf16[32,320]{1,0:T(8,128)(2,1)S(1)} %pad_maximum_fusion.4), channel_id=1, source_target_pairs={{0,4},{1,5},{2,6},{3,7},{4,0},{5,1},{6,2},{7,3},{8,12},{9,13},{10,... | collective-permute-start | bytes 61448 | tf_op jit(solution)/shard_map/ppermute | solution.py:465
  52.4 3.8 %collective-permute-start.7 = (bf16[32,320]{1,0:T(8,128)(2,1)S(1)}, bf16[32,320]{1,0:T(8,128)(2,1)S(1)}, u32[]{:S(2)}, u32[]{:S(2)}) collective-permute-start(bf16[32,320]{1,0:T(8,128)(2,1)S(1)} %pad_maximum_fusion.4), channel_id=1, source_target_pairs={{0,6},{1,7},{2,0},{3,1},{4,2},{5,3},{6,4},{7,5},{8,14},{9,15},{10,... | collective-permute-start | bytes 61448 | tf_op jit(solution)/shard_map/ppermute | solution.py:465
  56.3 1.3 collective-permute-start.8
  57.6 1.1 copy-start.9
  67.5 1.0 copy-start.2
  68.5 1.0 copy-start.4
  69.5 6.3 %collective-permute-start.9 = (f32[17,1024]{1,0:T(8,128)S(1)}, f32[17,1024]{1,0:T(8,128)S(1)}, u32[]{:S(2)}, u32[]{:S(2)}) collective-permute-start(f32[17,1024]{1,0:T(8,128)S(1)} %get-tuple-element.47.own_ref), channel_id=1, source_target_pairs={{0,8},{8,0},{16,24},{24,16},{32,40},{40,32},{48,56},{56,48},{64,72... | collective-permute-start | bytes 208904 | tf_op jit(solution)/shard_map/ppermute | solution.py:263
  75.9 5.9 %collective-permute-start.10 = (f32[17,1024]{1,0:T(8,128)S(1)}, f32[17,1024]{1,0:T(8,128)S(1)}, u32[]{:S(2)}, u32[]{:S(2)}) collective-permute-start(f32[17,1024]{1,0:T(8,128)S(1)} %get-tuple-element.48.own_ref), channel_id=1, source_target_pairs={{0,24},{8,16},{16,8},{24,0},{32,56},{40,48},{48,40},{56,32},{64,88... | collective-permute-start | bytes 208904 | tf_op jit(solution)/shard_map/ppermute | solution.py:263
  81.8 4.7 %collective-permute-start.11 = (f32[17,1024]{1,0:T(8,128)S(1)}, f32[17,1024]{1,0:T(8,128)S(1)}, u32[]{:S(2)}, u32[]{:S(2)}) collective-permute-start(f32[17,1024]{1,0:T(8,128)S(1)} %get-tuple-element.50.own_ref), channel_id=1, source_target_pairs={{0,32},{8,40},{16,48},{24,56},{32,0},{40,8},{48,16},{56,24},{64,96... | collective-permute-start | bytes 208904 | tf_op jit(solution)/shard_map/ppermute | solution.py:263
  86.5 5.9 %collective-permute-start.12 = (f32[17,1024]{1,0:T(8,128)S(1)}, f32[17,1024]{1,0:T(8,128)S(1)}, u32[]{:S(2)}, u32[]{:S(2)}) collective-permute-start(f32[17,1024]{1,0:T(8,128)S(1)} %get-tuple-element.52.own_ref), channel_id=1, source_target_pairs={{0,96},{8,104},{16,112},{24,120},{32,64},{40,72},{48,80},{56,88},{... | collective-permute-start | bytes 208904 | tf_op jit(solution)/shard_map/ppermute | solution.py:263
  93.1 1.2 copy-start.3
  94.4 1.2 copy-start.5
  102.6 9.2 %copy-start.16 = (s32[32,2]{0,1:T(2,128)S(1)}, s32[32,2]{0,1:T(2,128)}, u32[]{:S(2)}) copy-start(s32[32,2]{0,1:T(2,128)} %param.28) | copy-start | bytes 772
  102.6 18.5 %copy-start.17 = (f32[32,2]{0,1:T(2,128)S(1)}, f32[32,2]{0,1:T(2,128)}, u32[]{:S(2)}) copy-start(f32[32,2]{0,1:T(2,128)} %param.29) | copy-start | bytes 772
  102.6 30.2 %copy-start.14 = (bf16[32,4096]{1,0:T(8,128)(2,1)S(1)}, bf16[32,4096]{1,0:T(8,128)(2,1)}, u32[]{:S(2)}) copy-start(bf16[32,4096]{1,0:T(8,128)(2,1)} %param.27) | copy-start | bytes 786436
  102.6 64.1 %slice-start.2 = ((s8[6291456]{0:T(1024)(128)(4,1)}), s8[2097152]{0:T(1024)(128)(4,1)S(1)}, s32[]{:S(2)}) async-start(s8[6291456]{0:T(1024)(128)(4,1)} %bitcast.30), calls=%async_computation.5 | async-start | bytes 4194304
  110.4 1.3 copy-start.1
  111.8 2.9 collective-permute-start.16
  114.6 52.1 %slice-start = ((s8[6291456]{0:T(1024)(128)(4,1)}), s8[4194304]{0:T(1024)(128)(4,1)S(1)}, s32[]{:S(2)}) async-start(s8[6291456]{0:T(1024)(128)(4,1)} %bitcast.24), calls=%async_computation.3 | async-start | bytes 8388608
  114.6 52.1 %slice-start.3 = ((s8[6291456]{0:T(1024)(128)(4,1)}), s8[4194304]{0:T(1024)(128)(4,1)S(1)}, s32[]{:S(2)}) async-start(s8[6291456]{0:T(1024)(128)(4,1)} %bitcast.30), calls=%async_computation.6 | async-start | bytes 8388608
  116.8 15.4 %collective-permute-start.17 = (bf16[32,4096]{1,0:T(8,128)(2,1)S(1)}, bf16[32,4096]{1,0:T(8,128)(2,1)S(1)}, u32[]{:S(2)}, u32[]{:S(2)}) collective-permute-start(bf16[32,4096]{1,0:T(8,128)(2,1)S(1)} %get-tuple-element.95), channel_id=1, source_target_pairs={{0,2},{1,3},{2,4},{3,5},{4,6},{5,7},{6,0},{7,1},{8,10},{9,11},{10,... | collective-permute-start | bytes 786440 | tf_op jit(solution)/shard_map/ppermute | solution.py:465
  117.4 14.8 %collective-permute-start.18 = (bf16[32,4096]{1,0:T(8,128)(2,1)S(1)}, bf16[32,4096]{1,0:T(8,128)(2,1)S(1)}, u32[]{:S(2)}, u32[]{:S(2)}) collective-permute-start(bf16[32,4096]{1,0:T(8,128)(2,1)S(1)} %get-tuple-element.97), channel_id=1, source_target_pairs={{0,4},{1,5},{2,6},{3,7},{4,0},{5,1},{6,2},{7,3},{8,12},{9,13},{10,... | collective-permute-start | bytes 786440 | tf_op jit(solution)/shard_map/ppermute | solution.py:465
  120.2 12.7 %collective-permute-start.19 = (bf16[32,4096]{1,0:T(8,128)(2,1)S(1)}, bf16[32,4096]{1,0:T(8,128)(2,1)S(1)}, u32[]{:S(2)}, u32[]{:S(2)}) collective-permute-start(bf16[32,4096]{1,0:T(8,128)(2,1)S(1)} %get-tuple-element.96), channel_id=1, source_target_pairs={{0,6},{1,7},{2,0},{3,1},{4,2},{5,3},{6,4},{7,5},{8,14},{9,15},{10,... | collective-permute-start | bytes 786440 | tf_op jit(solution)/shard_map/ppermute | solution.py:465
  132.8 33.9 %slice-start.1 = ((s8[6291456]{0:T(1024)(128)(4,1)}), s8[2097152]{0:T(1024)(128)(4,1)S(1)}, s32[]{:S(2)}) async-start(s8[6291456]{0:T(1024)(128)(4,1)} %bitcast.24), calls=%async_computation.4 | async-start | bytes 4194304
  147.6 10.4 %collective-permute-start.20 = (bf16[64,4096]{1,0:T(8,128)(2,1)S(1)}, bf16[64,4096]{1,0:T(8,128)(2,1)S(1)}, u32[]{:S(2)}, u32[]{:S(2)}) collective-permute-start(bf16[64,4096]{1,0:T(8,128)(2,1)S(1)} %bitcast.44), channel_id=1, source_target_pairs={{0,32},{32,64},{64,96},{96,0},{8,40},{40,72},{72,104},{104,8},{16,... | collective-permute-start | bytes 1572872 | tf_op jit(solution)/shard_map/ppermute | solution.py:51
  147.8 15.3 %collective-permute-start.21 = (bf16[64,4096]{1,0:T(8,128)(2,1)S(1)}, bf16[64,4096]{1,0:T(8,128)(2,1)S(1)}, u32[]{:S(2)}, u32[]{:S(2)}) collective-permute-start(bf16[64,4096]{1,0:T(8,128)(2,1)S(1)} %bitcast.45), channel_id=1, source_target_pairs={{0,96},{32,0},{64,32},{96,64},{8,104},{40,8},{72,40},{104,72},{16,... | collective-permute-start | bytes 1572872 | tf_op jit(solution)/shard_map/ppermute | solution.py:51
  150.8 13.3 %collective-permute-start.22 = (bf16[64,4096]{1,0:T(8,128)(2,1)S(1)}, bf16[64,4096]{1,0:T(8,128)(2,1)S(1)}, u32[]{:S(2)}, u32[]{:S(2)}) collective-permute-start(bf16[64,4096]{1,0:T(8,128)(2,1)S(1)} %bitcast.46), channel_id=1, source_target_pairs={{0,64},{32,96},{64,0},{96,32},{8,72},{40,104},{72,8},{104,40},{16,... | collective-permute-start | bytes 1572872 | tf_op jit(solution)/shard_map/ppermute | solution.py:51
  164.3 26.1 %collective-permute-start.23 = (bf16[256,4096]{1,0:T(8,128)(2,1)S(1)}, bf16[256,4096]{1,0:T(8,128)(2,1)S(1)}, u32[]{:S(2)}, u32[]{:S(2)}) collective-permute-start(bf16[256,4096]{1,0:T(8,128)(2,1)S(1)} %pad_maximum_fusion.1.rows_ref), channel_id=1, source_target_pairs={{0,8},{8,16},{16,24},{24,0},{32,40},{40,48},{48,56},{56,32},{64,72... | collective-permute-start | bytes 6291464 | tf_op jit(solution)/shard_map/ppermute | solution.py:51
  166.7 27.2 %collective-permute-start.24 = (bf16[256,4096]{1,0:T(8,128)(2,1)S(1)}, bf16[256,4096]{1,0:T(8,128)(2,1)S(1)}, u32[]{:S(2)}, u32[]{:S(2)}) collective-permute-start(bf16[256,4096]{1,0:T(8,128)(2,1)S(1)} %pad_maximum_fusion.1.rows_ref), channel_id=1, source_target_pairs={{0,24},{8,0},{16,8},{24,16},{32,56},{40,32},{48,40},{56,48},{64,88... | collective-permute-start | bytes 6291464 | tf_op jit(solution)/shard_map/ppermute | solution.py:51
  166.7 2.8 copy-start
  194.0 14.9 %collective-permute-start.25 = (bf16[128,4096]{1,0:T(8,128)(2,1)S(1)}, bf16[128,4096]{1,0:T(8,128)(2,1)S(1)}, u32[]{:S(2)}, u32[]{:S(2)}) collective-permute-start(bf16[128,4096]{1,0:T(8,128)(2,1)S(1)} %slice.74), channel_id=1, source_target_pairs={{0,8},{8,16},{16,24},{24,0},{32,40},{40,48},{48,56},{56,32},{64,72... | collective-permute-start | bytes 3145736 | tf_op jit(solution)/shard_map/ppermute | solution.py:51
  194.2 16.1 %collective-permute-start.26 = (bf16[128,4096]{1,0:T(8,128)(2,1)S(1)}, bf16[128,4096]{1,0:T(8,128)(2,1)S(1)}, u32[]{:S(2)}, u32[]{:S(2)}) collective-permute-start(bf16[128,4096]{1,0:T(8,128)(2,1)S(1)} %slice.75), channel_id=1, source_target_pairs={{0,24},{8,0},{16,8},{24,16},{32,56},{40,32},{48,40},{56,48},{64,88... | collective-permute-start | bytes 3145736 | tf_op jit(solution)/shard_map/ppermute | solution.py:51
  204.7 16.8 %collective-permute-start.27 = (bf16[128,4096]{1,0:T(8,128)(2,1)S(1)}, bf16[128,4096]{1,0:T(8,128)(2,1)S(1)}, u32[]{:S(2)}, u32[]{:S(2)}) collective-permute-start(bf16[128,4096]{1,0:T(8,128)(2,1)S(1)} %get-tuple-element.72), channel_id=1, source_target_pairs={{0,24},{8,0},{16,8},{24,16},{32,56},{40,32},{48,40},{56,48},{64,88... | collective-permute-start | bytes 3145736 | tf_op jit(solution)/shard_map/ppermute | solution.py:51
  221.5 14.8 %collective-permute-start.28 = (bf16[128,4096]{1,0:T(8,128)(2,1)S(1)}, bf16[128,4096]{1,0:T(8,128)(2,1)S(1)}, u32[]{:S(2)}, u32[]{:S(2)}) collective-permute-start(bf16[128,4096]{1,0:T(8,128)(2,1)S(1)} %get-tuple-element.74), channel_id=1, source_target_pairs={{0,8},{8,16},{16,24},{24,0},{32,40},{40,48},{48,56},{56,32},{64,72... | collective-permute-start | bytes 3145736 | tf_op jit(solution)/shard_map/ppermute | solution.py:51
  221.5 16.0 %collective-permute-start.29 = (bf16[128,4096]{1,0:T(8,128)(2,1)S(1)}, bf16[128,4096]{1,0:T(8,128)(2,1)S(1)}, u32[]{:S(2)}, u32[]{:S(2)}) collective-permute-start(bf16[128,4096]{1,0:T(8,128)(2,1)S(1)} %get-tuple-element.75), channel_id=1, source_target_pairs={{0,24},{8,0},{16,8},{24,16},{32,56},{40,32},{48,40},{56,48},{64,88... | collective-permute-start | bytes 3145736 | tf_op jit(solution)/shard_map/ppermute | solution.py:51
  237.8 14.9 %collective-permute-start.30 = (bf16[128,4096]{1,0:T(8,128)(2,1)S(1)}, bf16[128,4096]{1,0:T(8,128)(2,1)S(1)}, u32[]{:S(2)}, u32[]{:S(2)}) collective-permute-start(bf16[128,4096]{1,0:T(8,128)(2,1)S(1)} %add_convert_fusion.3), channel_id=1, source_target_pairs={{0,8},{8,16},{16,24},{24,0},{32,40},{40,48},{48,56},{56,32},{64,72... | collective-permute-start | bytes 3145736 | tf_op jit(solution)/shard_map/ppermute | solution.py:51
  238.1 27.5 %collective-permute-start.32 = (bf16[128,4096]{1,0:T(8,128)(2,1)S(1)}, bf16[128,4096]{1,0:T(8,128)(2,1)S(1)}, u32[]{:S(2)}, u32[]{:S(2)}) collective-permute-start(bf16[128,4096]{1,0:T(8,128)(2,1)S(1)} %get-tuple-element.80), channel_id=1, source_target_pairs={{0,8},{8,16},{16,24},{24,0},{32,40},{40,48},{48,56},{56,32},{64,72... | collective-permute-start | bytes 3145736 | tf_op jit(solution)/shard_map/ppermute | solution.py:51
  240.3 25.2 %collective-permute-start.33 = (bf16[128,4096]{1,0:T(8,128)(2,1)S(1)}, bf16[128,4096]{1,0:T(8,128)(2,1)S(1)}, u32[]{:S(2)}, u32[]{:S(2)}) collective-permute-start(bf16[128,4096]{1,0:T(8,128)(2,1)S(1)} %add_convert_fusion.1), channel_id=1, source_target_pairs={{0,24},{8,0},{16,8},{24,16},{32,56},{40,32},{48,40},{56,48},{64,88... | collective-permute-start | bytes 3145736 | tf_op jit(solution)/shard_map/ppermute | solution.py:51
  253.2 17.0 %collective-permute-start.31 = (bf16[64,4096]{1,0:T(8,128)(2,1)S(1)}, bf16[64,4096]{1,0:T(8,128)(2,1)S(1)}, u32[]{:S(2)}, u32[]{:S(2)}) collective-permute-start(bf16[64,4096]{1,0:T(8,128)(2,1)S(1)} %slice.91), channel_id=1, source_target_pairs={{0,96},{32,0},{64,32},{96,64},{8,104},{40,8},{72,40},{104,72},{16,... | collective-permute-start | bytes 1572872 | tf_op jit(solution)/shard_map/ppermute | solution.py:51
  266.1 10.5 %collective-permute-start.34 = (bf16[64,4096]{1,0:T(8,128)(2,1)S(1)}, bf16[64,4096]{1,0:T(8,128)(2,1)S(1)}, u32[]{:S(2)}, u32[]{:S(2)}) collective-permute-start(bf16[64,4096]{1,0:T(8,128)(2,1)S(1)} %get-tuple-element.93), channel_id=1, source_target_pairs={{0,32},{32,64},{64,96},{96,0},{8,40},{40,72},{72,104},{104,8},{16,... | collective-permute-start | bytes 1572872 | tf_op jit(solution)/shard_map/ppermute | solution.py:51
  268.9 14.1 %collective-permute-start.35 = (bf16[64,4096]{1,0:T(8,128)(2,1)S(1)}, bf16[64,4096]{1,0:T(8,128)(2,1)S(1)}, u32[]{:S(2)}, u32[]{:S(2)}) collective-permute-start(bf16[64,4096]{1,0:T(8,128)(2,1)S(1)} %get-tuple-element.94), channel_id=1, source_target_pairs={{0,64},{32,96},{64,0},{96,32},{8,72},{40,104},{72,8},{104,40},{16,... | collective-permute-start | bytes 1572872 | tf_op jit(solution)/shard_map/ppermute | solution.py:51
Sparse Core Ops, SparseCore 0:
  26.5 51.3 all-gather.1

commit v4 on v3

--- a/solution.py
+++ b/solution.py
@@ -135,15 +135,17 @@
     proj_hbm,
     bias_hbm,
     packed_ref,
-    y_ref,
-    delta_ref,
     msg_ref,
+    y_hbm,
+    delta_hbm,
     before_hbm,
     enter_hbm,
     b_wide,
     c_wide,
     proj_ref,
     bias_ref,
+    y_ref,
+    delta_ref,
     before_ref,
     enter_ref,
     in_sems,
@@ -220,6 +222,10 @@
             pltpu.make_async_copy(
                 enter_ref.at[:, :, lanes], enter_hbm.at[:, :, lanes], out_sems.at[1, block]
             ),
+            pltpu.make_async_copy(y_ref.at[:, lanes], y_hbm.at[:, lanes], out_sems.at[2, block]),
+            pltpu.make_async_copy(
+                delta_ref.at[:, lanes], delta_hbm.at[:, lanes], out_sems.at[3, block]
+            ),
         ]
         for copy in fresh:
             copy.start()
@@ -277,23 +283,26 @@
     order_ref,
     entering_ref,
     rates_ref,
-    delta_ref,
     packed_ref,
-    y_ref,
     mixed_ref,
     before_hbm,
     enter_hbm,
     skip_hbm,
     z_hbm,
+    y_hbm,
+    delta_hbm,
     gated_ref,
     before_ref,
     enter_ref,
     skip_ref,
     z_ref,
+    y_ref,
+    delta_ref,
     c_wide,
     z_wide,
     gated,
     sems,
+    block_sems,
 ):
     length, channels = mixed_ref.shape
     steps = length // SEG
@@ -302,6 +311,17 @@
     copies = [pltpu.make_async_copy(*pair, sems.at[k]) for k, pair in enumerate(zip(sources, targets))]
     for copy in copies:
         copy.start()
+    blocks = []
+    for lane in range(0, channels, LANES):
+        lanes = pl.ds(lane, LANES)
+        y_sem, delta_sem = block_sems.at[0, lane // LANES], block_sems.at[1, lane // LANES]
+        pair = (
+            pltpu.make_async_copy(y_hbm.at[:, lanes], y_ref.at[:, lanes], y_sem),
+            pltpu.make_async_copy(delta_hbm.at[:, lanes], delta_ref.at[:, lanes], delta_sem),
+        )
+        for copy in pair:
+            copy.start()
+        blocks.append(pair)
     spread(c_wide, packed_ref, STATE)
     for copy in copies:
         copy.wait()
@@ -313,6 +333,8 @@
         rates = [
             jnp.broadcast_to(rates_ref[n : n + 1, lanes], (SEG, LANES)) for n in range(STATE)
         ]
+        for copy in blocks[lane // LANES]:
+            copy.wait()
         before = before_ref[:, lanes]
         held = [
             jnp.exp2(before * rates[n]) * entering_ref[n : n + 1, lanes] + enter_ref[n, :, lanes]
@@ -343,7 +365,7 @@
             ].astype(BF16)
 
 
-def outward_kernel(order_ref, gated_ref, proj_hbm, send_ref, keep_ref, proj, arrived):
+def outward_kernel(gated_ref, proj_hbm, send_ref, keep_ref, proj, arrived):
     parts, _, width = proj_hbm.shape
     middle = send_ref.shape[0]
     for part in range(parts):
@@ -351,7 +373,7 @@
 
     def product(part, carry):
         pltpu.make_async_copy(proj_hbm.at[part], proj.at[part], arrived.at[part]).wait()
-        columns = pl.ds(pl.multiple_of(order_ref[part] * width, width), width)
+        columns = pl.ds(pl.multiple_of(part * width, width), width)
         terms = jnp.dot(gated_ref[...], proj[part], preferred_element_type=F32)
         send_ref[:, columns] = terms[:middle].astype(BF16)
         keep_ref[:, columns] = terms[middle:]
@@ -394,9 +416,7 @@
         scratch_shapes=[pltpu.VMEM((count, hidden), BF16)],
         compiler_params=params(12),
         cost_estimate=pl.CostEstimate(
-            flops=6 * count * features * hidden,
-            bytes_accessed=4 * count * features,
-            transcendentals=count * hidden,
+            flops=count * features, bytes_accessed=count * features, transcendentals=count
         ),
         name="expert",
     )(rows, gate, up, down)
@@ -420,30 +440,33 @@
     ahead = along(rows, 0, -1)
     across = along(rows, 0, 2)
     own = jnp.concatenate([rows, behind, ahead, across], axis=0)
-    behind = along(own, 1, 1)
-    ahead = along(own, 1, -1)
+    own_first, own_second = halves(own)
+    behind_first = along(own_first, 1, 1)
+    ahead_second = along(own_second, 1, -1)
+    behind_second = along(own_second, 1, 1)
+    ahead_first = along(own_first, 1, -1)
     own_out = run(own)
-    behind, ahead, own_out = lax.optimization_barrier((behind, ahead, own_out))
-    far_first = along(halves(behind)[0], 1, 1)
-    far_second = along(halves(ahead)[1], 1, -1)
-    behind_first, behind_second = run(behind)
-    early_first = along(behind_first, 1, -1)
-    far_first, far_second, behind_second = lax.optimization_barrier(
-        (far_first, far_second, behind_second)
+    behind_first, ahead_second, own_out = lax.optimization_barrier(
+        (behind_first, ahead_second, own_out)
+    )
+    far_first = along(behind_first, 1, 1)
+    far_second = along(ahead_second, 1, -1)
+    behind_out, ahead_out = run(jnp.concatenate([behind_first, ahead_second], axis=0))
+    early_first = along(behind_out, 1, -1)
+    early_second = along(ahead_out, 1, 1)
+    behind_second, ahead_first, behind_out = lax.optimization_barrier(
+        (behind_second, ahead_first, behind_out)
+    )
+    behind_rest, ahead_rest = run(jnp.concatenate([behind_second, ahead_first], axis=0))
+    far_first, far_second, behind_rest = lax.optimization_barrier(
+        (far_first, far_second, behind_rest)
     )
     across_first, across_second = run(jnp.concatenate([far_first, far_second], axis=0))
-    across_first, across_second, early_first = lax.optimization_barrier(
-        (across_first, across_second, early_first)
-    )
-    from_behind = along(across_first, 1, 1)
-    from_ahead = along(across_second, 1, -1)
-    ahead_first, ahead_second = run(ahead)
-    early_second = along(ahead_second, 1, 1)
-    from_behind, from_ahead, ahead_first = lax.optimization_barrier(
-        (from_behind, from_ahead, ahead_first)
-    )
-    late_first = along(added(ahead_first, from_behind), 1, 1)
-    late_second = along(added(behind_second, from_ahead), 1, -1)
+    across_first, across_second, early_first, early_second = lax.optimization_barrier(
+        (across_first, across_second, early_first, early_second)
+    )
+    late_first = along(added(ahead_rest, along(across_first, 1, 1)), 1, 1)
+    late_second = along(added(behind_rest, along(across_second, 1, -1)), 1, -1)
     first = added(own_out[0], early_first, late_first)
     second = added(own_out[1], early_second, late_second)
     (kept, behind), (ahead, across) = halves(first), halves(second)
@@ -457,13 +480,13 @@
     seqs = lax.axis_size("seq")
     side = owners // 2
     owner = lax.axis_index("exp").astype(jnp.int32)
-    place = lax.axis_index("seq").astype(jnp.int32)
     chip, core = owner // 2, owner % 2
     swap = [(e, e + 1 - 2 * (e % 2)) for e in range(owners)]
 
     def along_z(block, hop):
         return lax.ppermute(block, "exp", [(e, (e + 2 * hop) % owners) for e in range(owners)])
 
+    columns = lax.all_gather(out_proj, "seq", axis=0)
     hops = jnp.arange(side, dtype=jnp.int32)
     onward, back = (chip + hops) % side, (chip - hops) % side
     order = jnp.concatenate([onward * 2 + 1 - core, onward * 2 + core])
@@ -471,18 +494,6 @@
 
     rates = (-jnp.exp(a_log) * LOG2E).T
     rim = passed_along(x_in[length - (CONV - 1) :], "seq", 1)
-    block = out_proj[None]
-    own_line = jnp.concatenate([block] + [along(block, 0, d) for d in (1, -1, 2)], axis=0)
-    columns = lax.all_gather(
-        own_line, ("seq", "exp"), axis_index_groups=lines(1), axis=0, tiled=True
-    )
-    grid_x, grid_y = place // side, place % side
-    shift = jnp.array([0, -1, 1, 2], dtype=jnp.int32)
-    fixed = jnp.arange(side, dtype=jnp.int32)[:, None]
-    by_x = ((grid_x + shift) % side)[None, :] * side + fixed
-    by_y = fixed * side + ((grid_y + shift) % side)[None, :]
-    column_order = jnp.where(core == 0, by_x, by_y).reshape(-1)
-
     mixed, send, keep = pl.pallas_call(
         conv_kernel,
         out_shape=(
@@ -514,61 +525,66 @@
     near = jnp.concatenate([summed[:, :RANK].astype(BF16), coef_high, coef_low], axis=1)
     near = jnp.concatenate([near] + [along_z(near, hop) for hop in range(1, side)], axis=0)
     other = lax.ppermute(near, "exp", swap)
-    packed, y_local, delta, message, before, enter = pl.pallas_call(
+    packed, message, y_local, delta, before, enter = pl.pallas_call(
         scan_kernel,
         out_shape=(
             jax.ShapeDtypeStruct((length, RANK + 4 * STATE), BF16),
+            jax.ShapeDtypeStruct((STATE + 1, channels), F32),
             jax.ShapeDtypeStruct((length, channels), F32),
             jax.ShapeDtypeStruct((length, channels), F32),
-            jax.ShapeDtypeStruct((STATE + 1, channels), F32),
             jax.ShapeDtypeStruct((SEG, channels), F32),
             jax.ShapeDtypeStruct((STATE, SEG, channels), F32),
         ),
         in_specs=[pl.BlockSpec(memory_space=pltpu.SMEM)] + [whole()] * 4 + [far()] * 2,
-        out_specs=[whole()] * 4 + [far()] * 2,
+        out_specs=[whole()] * 2 + [far()] * 4,
         scratch_shapes=[
             pltpu.VMEM((STATE, length, LANES), F32),
             pltpu.VMEM((STATE, length, LANES), F32),
             pltpu.VMEM(dt_proj.shape, BF16),
             pltpu.VMEM((1, channels), F32),
+            pltpu.VMEM((length, channels), F32),
+            pltpu.VMEM((length, channels), F32),
             pltpu.VMEM((SEG, channels), F32),
             pltpu.VMEM((STATE, SEG, channels), F32),
             pltpu.SemaphoreType.DMA((2,)),
-            pltpu.SemaphoreType.DMA((2, channels // LANES)),
+            pltpu.SemaphoreType.DMA((4, channels // LANES)),
         ],
-        compiler_params=params(14),
+        compiler_params=params(16),
         name="scan",
     )(arrival, near, other, mixed, rates, dt_proj, dt_bias[None, :])
     entering = entering_state(message, rates)
     gated = pl.pallas_call(
         finish_kernel,
         out_shape=jax.ShapeDtypeStruct((length, channels), BF16),
-        in_specs=[pl.BlockSpec(memory_space=pltpu.SMEM)] + [whole()] * 6 + [far()] * 4,
+        in_specs=[pl.BlockSpec(memory_space=pltpu.SMEM)] + [whole()] * 4 + [far()] * 6,
         out_specs=whole(),
         scratch_shapes=[
             pltpu.VMEM((SEG, channels), F32),
             pltpu.VMEM((STATE, SEG, channels), F32),
             pltpu.VMEM((1, channels), F32),
             pltpu.VMEM((length, channels), BF16),
+            pltpu.VMEM((length, channels), F32),
+            pltpu.VMEM((length, channels), F32),
             pltpu.VMEM((STATE, length, LANES), F32),
             pltpu.VMEM((channels // LANES, length, LANES), F32),
             pltpu.VMEM((channels // LANES, length, LANES), F32),
             pltpu.SemaphoreType.DMA((4,)),
+            pltpu.SemaphoreType.DMA((2, channels // LANES)),
         ],
-        compiler_params=params(14),
+        compiler_params=params(18),
         name="finish",
     )(
         order,
         entering,
         rates,
-        delta,
         packed,
-        y_local,
         mixed,
         before,
         enter,
         d_skip[None, :],
         z_in,
+        y_local,
+        delta,
     )
     width = out_proj.shape[1]
     features = seqs * width
@@ -578,7 +594,7 @@
             jax.ShapeDtypeStruct((length // 2, features), BF16),
             jax.ShapeDtypeStruct((length // 2, features), F32),
         ),
-        in_specs=[pl.BlockSpec(memory_space=pltpu.SMEM), whole(), far()],
+        in_specs=[whole(), far()],
         out_specs=[whole()] * 2,
         scratch_shapes=[
             pltpu.VMEM((seqs, channels, width), BF16),
@@ -586,7 +602,7 @@
         ],
         compiler_params=params(50),
         name="outward",
-    )(column_order, gated, columns)
+    )(gated, columns)
     sums = keep + lax.ppermute(send, "exp", swap).astype(F32)
     sums = sums.reshape(side, length // owners, features)
     total = sums[0]

time: 307 us -> 289 us (0.941)
  waiting for transfers between devices: 133 us -> 110 us
  starting transfers between devices: 47 us -> 56.3 us
    ppermute x19 -> x18, waiting for transfers between devices: 89.9 us -> 59.4 us  [along(): return lax.ppermute(block, ('seq', 'exp'), route)]
    ppermute x19 -> x18, starting transfers between devices: 24.1 us -> 32.7 us  [along(): return lax.ppermute(block, ('seq', 'exp'), route)]
    ppermute x4, waiting for transfers between devices: 17.9 us -> 25.5 us  [entering_state(): got = lax.ppermute(message, 'seq', route)]
    unnamed x47 -> x48, local copies, waits for them, and re-layouts: 10.8 us -> 9.42 us
  transfers between devices with their start and end apart: 37 -> 36, of which waited for: 32 -> 26; matrix products, arithmetic and copies ran while one was open for 1% -> 2% of each run, Pallas kernels for 18% -> 19%
where the time goes in v4:
time: 289 us; the launch traced here: 288 us
  waiting for transfers between devices  110 us (38%)
  Pallas kernels  62.5 us (22%)
  starting transfers between devices  56.3 us (19%)
  blocking collectives  27.2 us (9%)
  between operations  14 us (5%)
  local copies, waits for them, and re-layouts  10.9 us (4%)
  other arithmetic  5.83 us (2%)
    ppermute x18, waiting for transfers between devices, along(): return lax.ppermute(block, ('seq', 'exp'), route)  59.4 us
    pallas_call x4, Pallas kernels, expert(): pl.pallas_call(expert_kernel, out_shape=(jax.ShapeDtypeStruct((count // 2...  33.5 us
    ppermute x18, starting transfers between devices, along(): return lax.ppermute(block, ('seq', 'exp'), route)  32.7 us
    ppermute x4, waiting for transfers between devices, entering_state(): got = lax.ppermute(message, 'seq', route)  25.5 us
    ppermute x9, waiting for transfers between devices, along_z(): lax.ppermute(block, 'exp', [(e, (e + 2 * hop) % owners) for e in range(ow...  17.7 us
    ppermute x9, starting transfers between devices, along_z(): lax.ppermute(block, 'exp', [(e, (e + 2 * hop) % owners) for e in range(ow...  15.2 us
    all_to_all x1, blocking collectives, shards(): lax.all_to_all(outgoing, 'exp', split_axis=0, concat_axis=0, tiled=True)  14.4 us
    all_to_all x1, blocking collectives, shards(): lax.all_to_all(expert_out, 'exp', split_axis=0, concat_axis=0, tiled=True)  12.8 us
  transfers between devices with their start and end apart: 36, of which 26 were waited for; matrix products, arithmetic and copies ran while one was open for 2% of the time, Pallas kernels for 19%

profile of v4, /device:TPU:24, one launch (start us, length us, event | category | flops | bytes accessed | tf_op | source)
XLA Modules:
  0.0 288.4 jit_solution(3928863296462238641)
XLA Ops:
  7.3 0.7 slice.61
  8.0 3.0 %collective-permute-start = (bf16[3,1024]{1,0:T(4,128)(2,1)S(1)}, bf16[3,1024]{1,0:T(4,128)(2,1)S(1)}, u32[]{:S(2)}, u32[]{:S(2)}) collective-permute-start(bf16[3,1024]{1,0:T(4,128)(2,1)S(1)} %slice.61), channel_id=1, source_target_pairs={{0,8},{8,16},{16,24},{24,32},{32,40},{40,48},{48,56},{56,64},{64,7... | collective-permute-start | bytes 18440 | tf_op jit(solution)/shard_map/ppermute | solution.py:57
  11.2 2.4 collective-permute-done.rim_ref
  13.5 1.1 copy-done.5
  14.6 1.0 copy-done.6
  17.0 4.4 %conv.1 = (f32[256,1024]{1,0:T(8,128)S(1)}, f32[128,288]{1,0:T(8,128)S(1)}, f32[128,288]{1,0:T(8,128)S(1)}) custom-call(s32[8]{0:T(128)S(1)} %pad_add_fusion.order_ref, bf16[256,1024]{1,0:T(8,128)(2,1)S(1)} %copy-done.6, f32[4,1024]{1,0:T(4,128)S(1)} %copy-done.9, f32[1,1024]{1,0:T(1,128)S(1)} %bitcast.43, bf16[288,1024]{1,0:T(8,128)(2,1)S(1)} %bitcast.42, ...), custom_call_target="tpu_custom_call" | custom-call | tf_op jit(solution)/shard_map/conv/pallas_call | solution.py:497
  21.5 1.4 collective-permute-done.1
  23.0 2.0 collective-permute-start.2
  25.0 3.6 %collective-permute-start.3 = (f32[32,288]{1,0:T(8,128)S(1)}, f32[32,288]{1,0:T(8,128)S(1)}, u32[]{:S(2)}, u32[]{:S(2)}) collective-permute-start(f32[32,288]{1,0:T(8,128)S(1)} %get-tuple-element.100), channel_id=1, source_target_pairs={{0,4},{1,5},{2,6},{3,7},{4,0},{5,1},{6,2},{7,3},{8,12},{9,13},{10,... | collective-permute-start | bytes 110600 | tf_op jit(solution)/shard_map/ppermute | solution.py:487
  28.6 1.0 collective-permute-start.4
  29.6 1.7 collective-permute-done.3
  31.4 1.3 collective-permute-done.4
  32.8 3.7 %collective-permute-start.6 = (bf16[32,320]{1,0:T(8,128)(2,1)S(1)}, bf16[32,320]{1,0:T(8,128)(2,1)S(1)}, u32[]{:S(2)}, u32[]{:S(2)}) collective-permute-start(bf16[32,320]{1,0:T(8,128)(2,1)S(1)} %pad_maximum_fusion.6), channel_id=1, source_target_pairs={{0,4},{1,5},{2,6},{3,7},{4,0},{5,1},{6,2},{7,3},{8,12},{9,13},{10,... | collective-permute-start | bytes 61448 | tf_op jit(solution)/shard_map/ppermute | solution.py:487
  36.9 0.9 collective-permute-done.5
  38.5 1.8 collective-permute-done.7
  40.5 1.2 collective-permute-done.8.other_ref
  41.7 9.2 %scan.1 = (bf16[256,320]{1,0:T(8,128)(2,1)S(1)}, f32[17,1024]{1,0:T(8,128)S(1)}, f32[256,1024]{1,0:T(8,128)S(1)}, f32[256,1024]{1,0:T(8,128)S(1)}, f32[8,1024]{1,0:T(8,128)S(1)}, /*index=5*/f32[16,8,1024]{2,1,0:T(8,128)S(1)}) custom-call(s32[8]{0:T(128)S(1)} %pad_add_fusion.1.order_ref, bf16[128,320]{1,0:T(8,128)(2,1)S(1)} %pad_maximum_fusion.5.near_ref, ...), custom_call_target="tpu_custom_call" | custom-call | tf_op jit(solution)/shard_map/scan/pallas_call | solution.py:528
  50.9 1.0 copy-done.1
  51.9 1.0 copy-done.3
  52.9 0.7 collective-permute-start.9
  53.6 6.7 %collective-permute-done.9.got_ref = f32[17,1024]{1,0:T(8,128)S(1)} collective-permute-done((f32[17,1024]{1,0:T(8,128)S(1)}, f32[17,1024]{1,0:T(8,128)S(1)}, u32[]{:S(2)}, u32[]{:S(2)}) %collective-permute-start.9) | collective-permute-done | bytes 69664 | tf_op jit(solution)/shard_map/ppermute | solution.py:269
  60.5 8.4 %collective-permute-done.10.got_ref = f32[17,1024]{1,0:T(8,128)S(1)} collective-permute-done((f32[17,1024]{1,0:T(8,128)S(1)}, f32[17,1024]{1,0:T(8,128)S(1)}, u32[]{:S(2)}, u32[]{:S(2)}) %collective-permute-start.10) | collective-permute-done | bytes 69664 | tf_op jit(solution)/shard_map/ppermute | solution.py:269
  68.9 1.6 collective-permute-start.11
  70.5 5.5 %collective-permute-done.11.got_ref = f32[17,1024]{1,0:T(8,128)S(1)} collective-permute-done((f32[17,1024]{1,0:T(8,128)S(1)}, f32[17,1024]{1,0:T(8,128)S(1)}, u32[]{:S(2)}, u32[]{:S(2)}) %collective-permute-start.11) | collective-permute-done | bytes 69664 | tf_op jit(solution)/shard_map/ppermute | solution.py:269
  76.0 2.8 collective-permute-start.12
  78.9 4.9 %collective-permute-done.12.got_ref = f32[17,1024]{1,0:T(8,128)S(1)} collective-permute-done((f32[17,1024]{1,0:T(8,128)S(1)}, f32[17,1024]{1,0:T(8,128)S(1)}, u32[]{:S(2)}, u32[]{:S(2)}) %collective-permute-start.12) | collective-permute-done | bytes 69664 | tf_op jit(solution)/shard_map/ppermute | solution.py:269
  84.5 1.2 copy-done.2
  85.7 1.2 copy-done.4
  86.9 7.5 %finish.1.gated_ref = bf16[256,1024]{1,0:T(8,128)(2,1)S(1)} custom-call(s32[8]{0:T(128)S(1)} %pad_add_fusion.order_ref, f32[17,1024]{1,0:T(8,128)S(1)} %get-tuple-element.54.entering_ref, f32[16,1024]{1,0:T(8,128)S(1)} %multiply_bitcast_fusion.rates_ref, bf16[256,320]{1,0:T(8,128)(2,1)S(1)} %get-tuple-element.55.packed_ref, ...), custom_call_target="tpu_custom_call" | custom-call | tf_op jit(solution)/shard_map/finish/pallas_call | solution.py:556
  94.5 7.1 %outward.1 = (bf16[128,4096]{1,0:T(8,128)(2,1)}, f32[128,4096]{1,0:T(8,128)S(1)}) custom-call(bf16[256,1024]{1,0:T(8,128)(2,1)S(1)} %finish.1.gated_ref, bf16[16,1024,256]{2,1,0:T(8,128)(2,1)} %bitcast.46), custom_call_target="tpu_custom_call" | custom-call | tf_op jit(solution)/shard_map/outward/pallas_call | solution.py:591
  101.7 1.3 copy-done
  104.0 1.9 collective-permute-done.13
  105.9 2.1 fusion.18
  108.7 2.7 collective-permute-start.15
  111.5 1.0 collective-permute-start.16
  112.6 5.8 %collective-permute-done.14 = bf16[32,4096]{1,0:T(8,128)(2,1)S(1)} collective-permute-done((bf16[32,4096]{1,0:T(8,128)(2,1)S(1)}, bf16[32,4096]{1,0:T(8,128)(2,1)S(1)}, u32[]{:S(2)}, u32[]{:S(2)}) %collective-permute-start.14) | collective-permute-done | bytes 262176 | tf_op jit(solution)/shard_map/ppermute | solution.py:487
  118.3 5.1 %collective-permute-done.15 = bf16[32,4096]{1,0:T(8,128)(2,1)S(1)} collective-permute-done((bf16[32,4096]{1,0:T(8,128)(2,1)S(1)}, bf16[32,4096]{1,0:T(8,128)(2,1)S(1)}, u32[]{:S(2)}, u32[]{:S(2)}) %collective-permute-start.15) | collective-permute-done | bytes 262176 | tf_op jit(solution)/shard_map/ppermute | solution.py:487
  124.6 14.4 %all_to_all.10 = bf16[8,8,4096]{2,1,0:T(8,128)(2,1)S(1)} all-to-all(bf16[8,8,4096]{2,1,0:T(8,128)(2,1)S(1)} %fusion), channel_id=1, replica_groups=mesh['seq'=16,'exp'=8] {'exp'}, dimensions={0} | all-to-all | bytes 1048576 | tf_op jit(solution)/shard_map/all_to_all | solution.py:661
  138.9 1.1 collective-permute-start.19
  140.0 1.2 collective-permute-start.20
  141.3 6.8 %collective-permute-done.19 = bf16[64,4096]{1,0:T(8,128)(2,1)S(1)} collective-permute-done((bf16[64,4096]{1,0:T(8,128)(2,1)S(1)}, bf16[64,4096]{1,0:T(8,128)(2,1)S(1)}, u32[]{:S(2)}, u32[]{:S(2)}) %collective-permute-start.19) | collective-permute-done | bytes 524320 | tf_op jit(solution)/shard_map/ppermute | solution.py:51
  148.1 2.6 collective-permute-done.20
  151.2 5.1 %collective-permute-done.17 = bf16[64,4096]{1,0:T(8,128)(2,1)S(1)} collective-permute-done((bf16[64,4096]{1,0:T(8,128)(2,1)S(1)}, bf16[64,4096]{1,0:T(8,128)(2,1)S(1)}, u32[]{:S(2)}, u32[]{:S(2)}) %collective-permute-start.17) | collective-permute-done | bytes 524320 | tf_op jit(solution)/shard_map/ppermute | solution.py:51
  156.4 2.0 collective-permute-start.18
  158.5 1.9 collective-permute-start.25
  160.8 8.4 %expert.4 = (bf16[128,4096]{1,0:T(8,128)(2,1)S(1)}, bf16[128,4096]{1,0:T(8,128)(2,1)S(1)}) custom-call(bf16[256,4096]{1,0:T(8,128)(2,1)S(1)} %pad_maximum_fusion.rows_ref, bf16[4096,768]{1,0:T(8,128)(2,1)S(1)} %bitcast.26, bf16[4096,768]{1,0:T(8,128)(2,1)S(1)} %bitcast.32, bf16[768,4096]{1,0:T(8,128)(2,1)S(1)} %bitcast.38), custom_call_target="tpu_custom_call" | custom-call | flops 1048576 | bytes 1048576 | tf_op jit(solution)/shard_map/expert/pallas_call | solution.py:411
  169.2 2.1 collective-permute-done.18
  171.3 3.2 %collective-permute-start.22 = (bf16[128,4096]{1,0:T(8,128)(2,1)S(1)}, bf16[128,4096]{1,0:T(8,128)(2,1)S(1)}, u32[]{:S(2)}, u32[]{:S(2)}) collective-permute-start(bf16[128,4096]{1,0:T(8,128)(2,1)S(1)} %collective-permute-done.18), channel_id=1, source_target_pairs={{0,8},{8,16},{16,24},{24,0},{32,40},{40,48},{48,56},{56,32},{64,72... | collective-permute-start | bytes 3145736 | tf_op jit(solution)/shard_map/ppermute | solution.py:51
  174.7 8.4 %expert.5 = (bf16[128,4096]{1,0:T(8,128)(2,1)S(1)}, bf16[128,4096]{1,0:T(8,128)(2,1)S(1)}) custom-call(bf16[256,4096]{1,0:T(8,128)(2,1)S(1)} %pad_maximum_fusion.1.rows_ref, bf16[4096,768]{1,0:T(8,128)(2,1)S(1)} %bitcast.27, bf16[4096,768]{1,0:T(8,128)(2,1)S(1)} %bitcast.33, bf16[768,4096]{1,0:T(8,128)(2,1)S(1)} %bitcast.39), custom_call_target="tpu_custom_call" | custom-call | flops 1048576 | bytes 1048576 | tf_op jit(solution)/shard_map/expert/pallas_call | solution.py:411
  183.1 3.3 %collective-permute-start.27 = (bf16[128,4096]{1,0:T(8,128)(2,1)S(1)}, bf16[128,4096]{1,0:T(8,128)(2,1)S(1)}, u32[]{:S(2)}, u32[]{:S(2)}) collective-permute-start(bf16[128,4096]{1,0:T(8,128)(2,1)S(1)} %get-tuple-element.75), channel_id=1, source_target_pairs={{0,8},{8,16},{16,24},{24,0},{32,40},{40,48},{48,56},{56,32},{64,72... | collective-permute-start | bytes 3145736 | tf_op jit(solution)/shard_map/ppermute | solution.py:51
  186.7 8.4 %expert.6 = (bf16[128,4096]{1,0:T(8,128)(2,1)S(1)}, bf16[128,4096]{1,0:T(8,128)(2,1)S(1)}) custom-call(bf16[256,4096]{1,0:T(8,128)(2,1)S(1)} %pad_maximum_fusion.2.rows_ref, bf16[4096,768]{1,0:T(8,128)(2,1)S(1)} %bitcast.28, bf16[4096,768]{1,0:T(8,128)(2,1)S(1)} %bitcast.34, bf16[768,4096]{1,0:T(8,128)(2,1)S(1)} %bitcast.40), custom_call_target="tpu_custom_call" | custom-call | flops 1048576 | bytes 1048576 | tf_op jit(solution)/shard_map/expert/pallas_call | solution.py:411
  195.3 8.4 %expert.7 = (bf16[128,4096]{1,0:T(8,128)(2,1)S(1)}, bf16[128,4096]{1,0:T(8,128)(2,1)S(1)}) custom-call(bf16[256,4096]{1,0:T(8,128)(2,1)S(1)} %pad_maximum_fusion.3.rows_ref, bf16[4096,768]{1,0:T(8,128)(2,1)S(1)} %bitcast.29, bf16[4096,768]{1,0:T(8,128)(2,1)S(1)} %bitcast.35, bf16[768,4096]{1,0:T(8,128)(2,1)S(1)} %bitcast.41), custom_call_target="tpu_custom_call" | custom-call | flops 1048576 | bytes 1048576 | tf_op jit(solution)/shard_map/expert/pallas_call | solution.py:411
  203.7 1.3 collective-permute-done.27
  205.0 3.2 %collective-permute-start.28 = (bf16[128,4096]{1,0:T(8,128)(2,1)S(1)}, bf16[128,4096]{1,0:T(8,128)(2,1)S(1)}, u32[]{:S(2)}, u32[]{:S(2)}) collective-permute-start(bf16[128,4096]{1,0:T(8,128)(2,1)S(1)} %get-tuple-element.78), channel_id=1, source_target_pairs={{0,8},{8,16},{16,24},{24,0},{32,40},{40,48},{48,56},{56,32},{64,72... | collective-permute-start | bytes 3145736 | tf_op jit(solution)/shard_map/ppermute | solution.py:51
  208.2 12.3 %collective-permute-done.28 = bf16[128,4096]{1,0:T(8,128)(2,1)S(1)} collective-permute-done((bf16[128,4096]{1,0:T(8,128)(2,1)S(1)}, bf16[128,4096]{1,0:T(8,128)(2,1)S(1)}, u32[]{:S(2)}, u32[]{:S(2)}) %collective-permute-start.28) | collective-permute-done | bytes 1048608 | tf_op jit(solution)/shard_map/ppermute | solution.py:51
  220.7 3.8 %collective-permute-start.29 = (bf16[128,4096]{1,0:T(8,128)(2,1)S(1)}, bf16[128,4096]{1,0:T(8,128)(2,1)S(1)}, u32[]{:S(2)}, u32[]{:S(2)}) collective-permute-start(bf16[128,4096]{1,0:T(8,128)(2,1)S(1)} %add_convert_fusion.3), channel_id=1, source_target_pairs={{0,8},{8,16},{16,24},{24,0},{32,40},{40,48},{48,56},{56,32},{64,72... | collective-permute-start | bytes 3145736 | tf_op jit(solution)/shard_map/ppermute | solution.py:51
  225.0 11.8 %collective-permute-done.29 = bf16[128,4096]{1,0:T(8,128)(2,1)S(1)} collective-permute-done((bf16[128,4096]{1,0:T(8,128)(2,1)S(1)}, bf16[128,4096]{1,0:T(8,128)(2,1)S(1)}, u32[]{:S(2)}, u32[]{:S(2)}) %collective-permute-start.29) | collective-permute-done | bytes 1048608 | tf_op jit(solution)/shard_map/ppermute | solution.py:51
  237.3 1.5 collective-permute-start.30
  238.9 4.6 %collective-permute-done.32 = bf16[128,4096]{1,0:T(8,128)(2,1)S(1)} collective-permute-done((bf16[128,4096]{1,0:T(8,128)(2,1)S(1)}, bf16[128,4096]{1,0:T(8,128)(2,1)S(1)}, u32[]{:S(2)}, u32[]{:S(2)}) %collective-permute-start.32) | collective-permute-done | bytes 1048608 | tf_op jit(solution)/shard_map/ppermute | solution.py:51
  244.1 10.5 %collective-permute-start.34 = (bf16[64,4096]{1,0:T(8,128)(2,1)S(1)}, bf16[64,4096]{1,0:T(8,128)(2,1)S(1)}, u32[]{:S(2)}, u32[]{:S(2)}) collective-permute-start(bf16[64,4096]{1,0:T(8,128)(2,1)S(1)} %get-tuple-element.94), channel_id=1, source_target_pairs={{0,64},{32,96},{64,0},{96,32},{8,72},{40,104},{72,8},{104,40},{16,... | collective-permute-start | bytes 1572872 | tf_op jit(solution)/shard_map/ppermute | solution.py:51
  254.5 5.7 %collective-permute-done.33 = bf16[64,4096]{1,0:T(8,128)(2,1)S(1)} collective-permute-done((bf16[64,4096]{1,0:T(8,128)(2,1)S(1)}, bf16[64,4096]{1,0:T(8,128)(2,1)S(1)}, u32[]{:S(2)}, u32[]{:S(2)}) %collective-permute-start.33) | collective-permute-done | bytes 524320 | tf_op jit(solution)/shard_map/ppermute | solution.py:51
  260.2 7.1 %collective-permute-done.34 = bf16[64,4096]{1,0:T(8,128)(2,1)S(1)} collective-permute-done((bf16[64,4096]{1,0:T(8,128)(2,1)S(1)}, bf16[64,4096]{1,0:T(8,128)(2,1)S(1)}, u32[]{:S(2)}, u32[]{:S(2)}) %collective-permute-start.34) | collective-permute-done | bytes 524320 | tf_op jit(solution)/shard_map/ppermute | solution.py:51
  267.6 12.8 %all_to_all.11 = bf16[8,8,4096]{2,1,0:T(8,128)(2,1)S(1)} all-to-all(bf16[8,8,4096]{2,1,0:T(8,128)(2,1)S(1)} %fusion.1), channel_id=1, replica_groups=mesh['seq'=16,'exp'=8] {'exp'}, dimensions={0} | all-to-all | bytes 1048576 | tf_op jit(solution)/shard_map/all_to_all | solution.py:664
  280.4 1.2 convolution_add_fusion
  (118 shorter events, 11.5 us)
Async XLA Ops:
  6.5 23.0 %copy-start.14 = (f32[1024,16]{0,1:T(8,128)S(1)}, f32[1024,16]{0,1:T(8,128)}, u32[]{:S(2)}) copy-start(f32[1024,16]{0,1:T(8,128)} %param.23) | copy-start | bytes 196612
  6.5 35.1 %copy-start.11 = (f32[1024]{0:T(1024)S(1)}, f32[1024]{0:T(1024)}, u32[]{:S(2)}) copy-start(f32[1024]{0:T(1024)} %param.22) | copy-start | bytes 12292
  6.5 35.1 %copy-start.8 = (bf16[256,1024]{1,0:T(8,128)(2,1)S(1)}, bf16[256,1024]{1,0:T(8,128)(2,1)}, u32[]{:S(2)}) copy-start(bf16[256,1024]{1,0:T(8,128)(2,1)} %proj_hbm.1) | copy-start | bytes 1572868
  6.5 87.9 %all-gather.3.cloned.1.call-start = ((), (), s32[]{:S(2)}) async-start(), calls=%async_computation.2 | async-start | bytes 8912896 | tf_op jit(solution)/shard_map/all_gather | solution.py:489
  8.0 5.5 %collective-permute-start = (bf16[3,1024]{1,0:T(4,128)(2,1)S(1)}, bf16[3,1024]{1,0:T(4,128)(2,1)S(1)}, u32[]{:S(2)}, u32[]{:S(2)}) collective-permute-start(bf16[3,1024]{1,0:T(4,128)(2,1)S(1)} %slice.61), channel_id=1, source_target_pairs={{0,8},{8,16},{16,24},{24,32},{32,40},{40,48},{48,56},{56,64},{64,7... | collective-permute-start | bytes 18440 | tf_op jit(solution)/shard_map/ppermute | solution.py:57
  13.5 1.1 copy-start.5
  14.6 1.0 copy-start.6
  15.6 0.7 copy-start.9
  16.3 0.7 copy-start.10
  21.4 1.5 collective-permute-start.1
  23.0 6.6 %collective-permute-start.2 = (f32[32,288]{1,0:T(8,128)S(1)}, f32[32,288]{1,0:T(8,128)S(1)}, u32[]{:S(2)}, u32[]{:S(2)}) collective-permute-start(f32[32,288]{1,0:T(8,128)S(1)} %get-tuple-element.98), channel_id=1, source_target_pairs={{0,2},{1,3},{2,4},{3,5},{4,6},{5,7},{6,0},{7,1},{8,10},{9,11},{10,... | collective-permute-start | bytes 110600 | tf_op jit(solution)/shard_map/ppermute | solution.py:487
  25.0 6.4 %collective-permute-start.3 = (f32[32,288]{1,0:T(8,128)S(1)}, f32[32,288]{1,0:T(8,128)S(1)}, u32[]{:S(2)}, u32[]{:S(2)}) collective-permute-start(f32[32,288]{1,0:T(8,128)S(1)} %get-tuple-element.100), channel_id=1, source_target_pairs={{0,4},{1,5},{2,6},{3,7},{4,0},{5,1},{6,2},{7,3},{8,12},{9,13},{10,... | collective-permute-start | bytes 110600 | tf_op jit(solution)/shard_map/ppermute | solution.py:487
  28.6 4.1 %collective-permute-start.4 = (f32[32,288]{1,0:T(8,128)S(1)}, f32[32,288]{1,0:T(8,128)S(1)}, u32[]{:S(2)}, u32[]{:S(2)}) collective-permute-start(f32[32,288]{1,0:T(8,128)S(1)} %get-tuple-element.99), channel_id=1, source_target_pairs={{0,6},{1,7},{2,0},{3,1},{4,2},{5,3},{6,4},{7,5},{8,14},{9,15},{10,... | collective-permute-start | bytes 110600 | tf_op jit(solution)/shard_map/ppermute | solution.py:487
  29.6 54.9 %copy-start.7 = (bf16[256,1024]{1,0:T(8,128)(2,1)S(1)}, bf16[256,1024]{1,0:T(8,128)(2,1)}, u32[]{:S(2)}) copy-start(bf16[256,1024]{1,0:T(8,128)(2,1)} %z_hbm.1) | copy-start | bytes 1572868
  29.6 54.9 %copy-start.12 = (f32[1024]{0:T(1024)S(1)}, f32[1024]{0:T(1024)}, u32[]{:S(2)}) copy-start(f32[1024]{0:T(1024)} %param.24) | copy-start | bytes 12292
  32.8 5.0 %collective-permute-start.5 = (bf16[32,320]{1,0:T(8,128)(2,1)S(1)}, bf16[32,320]{1,0:T(8,128)(2,1)S(1)}, u32[]{:S(2)}, u32[]{:S(2)}) collective-permute-start(bf16[32,320]{1,0:T(8,128)(2,1)S(1)} %pad_maximum_fusion.6), channel_id=1, source_target_pairs={{0,2},{1,3},{2,4},{3,5},{4,6},{5,7},{6,0},{7,1},{8,10},{9,11},{10,... | collective-permute-start | bytes 61448 | tf_op jit(solution)/shard_map/ppermute | solution.py:487
  32.8 5.7 %collective-permute-start.6 = (bf16[32,320]{1,0:T(8,128)(2,1)S(1)}, bf16[32,320]{1,0:T(8,128)(2,1)S(1)}, u32[]{:S(2)}, u32[]{:S(2)}) collective-permute-start(bf16[32,320]{1,0:T(8,128)(2,1)S(1)} %pad_maximum_fusion.6), channel_id=1, source_target_pairs={{0,4},{1,5},{2,6},{3,7},{4,0},{5,1},{6,2},{7,3},{8,12},{9,13},{10,... | collective-permute-start | bytes 61448 | tf_op jit(solution)/shard_map/ppermute | solution.py:487
  36.5 3.8 %collective-permute-start.7 = (bf16[32,320]{1,0:T(8,128)(2,1)S(1)}, bf16[32,320]{1,0:T(8,128)(2,1)S(1)}, u32[]{:S(2)}, u32[]{:S(2)}) collective-permute-start(bf16[32,320]{1,0:T(8,128)(2,1)S(1)} %pad_maximum_fusion.6), channel_id=1, source_target_pairs={{0,6},{1,7},{2,0},{3,1},{4,2},{5,3},{6,4},{7,5},{8,14},{9,15},{10,... | collective-permute-start | bytes 61448 | tf_op jit(solution)/shard_map/ppermute | solution.py:487
  40.4 1.3 collective-permute-start.8
  50.9 1.0 copy-start.1
  51.9 1.0 copy-start.3
  52.9 7.5 %collective-permute-start.9 = (f32[17,1024]{1,0:T(8,128)S(1)}, f32[17,1024]{1,0:T(8,128)S(1)}, u32[]{:S(2)}, u32[]{:S(2)}) collective-permute-start(f32[17,1024]{1,0:T(8,128)S(1)} %get-tuple-element.47.own_ref), channel_id=1, source_target_pairs={{0,8},{8,0},{16,24},{24,16},{32,40},{40,32},{48,56},{56,48},{64,72... | collective-permute-start | bytes 208904 | tf_op jit(solution)/shard_map/ppermute | solution.py:269
  60.4 8.5 %collective-permute-start.10 = (f32[17,1024]{1,0:T(8,128)S(1)}, f32[17,1024]{1,0:T(8,128)S(1)}, u32[]{:S(2)}, u32[]{:S(2)}) collective-permute-start(f32[17,1024]{1,0:T(8,128)S(1)} %get-tuple-element.48.own_ref), channel_id=1, source_target_pairs={{0,24},{8,16},{16,8},{24,0},{32,56},{40,48},{48,40},{56,32},{64,88... | collective-permute-start | bytes 208904 | tf_op jit(solution)/shard_map/ppermute | solution.py:269
  68.9 7.0 %collective-permute-start.11 = (f32[17,1024]{1,0:T(8,128)S(1)}, f32[17,1024]{1,0:T(8,128)S(1)}, u32[]{:S(2)}, u32[]{:S(2)}) collective-permute-start(f32[17,1024]{1,0:T(8,128)S(1)} %get-tuple-element.50.own_ref), channel_id=1, source_target_pairs={{0,32},{8,40},{16,48},{24,56},{32,0},{40,8},{48,16},{56,24},{64,96... | collective-permute-start | bytes 208904 | tf_op jit(solution)/shard_map/ppermute | solution.py:269
  76.0 7.8 %collective-permute-start.12 = (f32[17,1024]{1,0:T(8,128)S(1)}, f32[17,1024]{1,0:T(8,128)S(1)}, u32[]{:S(2)}, u32[]{:S(2)}) collective-permute-start(f32[17,1024]{1,0:T(8,128)S(1)} %get-tuple-element.52.own_ref), channel_id=1, source_target_pairs={{0,96},{8,104},{16,112},{24,120},{32,64},{40,72},{48,80},{56,88},{... | collective-permute-start | bytes 208904 | tf_op jit(solution)/shard_map/ppermute | solution.py:269
  84.5 1.2 copy-start.2
  85.7 1.2 copy-start.4
  94.5 8.6 %copy-start.15 = (s32[32,2]{0,1:T(2,128)S(1)}, s32[32,2]{0,1:T(2,128)}, u32[]{:S(2)}) copy-start(s32[32,2]{0,1:T(2,128)} %param.27) | copy-start | bytes 772
  94.5 18.0 %copy-start.16 = (f32[32,2]{0,1:T(2,128)S(1)}, f32[32,2]{0,1:T(2,128)}, u32[]{:S(2)}) copy-start(f32[32,2]{0,1:T(2,128)} %param.28) | copy-start | bytes 772
  94.5 29.4 %copy-start.13 = (bf16[32,4096]{1,0:T(8,128)(2,1)S(1)}, bf16[32,4096]{1,0:T(8,128)(2,1)}, u32[]{:S(2)}) copy-start(bf16[32,4096]{1,0:T(8,128)(2,1)} %param.26) | copy-start | bytes 786436
  94.5 66.2 %slice-start.4 = ((s8[6291456]{0:T(1024)(128)(4,1)}), s8[2097152]{0:T(1024)(128)(4,1)S(1)}, s32[]{:S(2)}) async-start(s8[6291456]{0:T(1024)(128)(4,1)} %bitcast.36), calls=%async_computation.7 | async-start | bytes 4194304
  101.7 1.3 copy-start
  103.0 2.9 collective-permute-start.13
  105.9 54.8 %slice-start = ((s8[6291456]{0:T(1024)(128)(4,1)}), s8[4194304]{0:T(1024)(128)(4,1)S(1)}, s32[]{:S(2)}) async-start(s8[6291456]{0:T(1024)(128)(4,1)} %bitcast.24), calls=%async_computation.3 | async-start | bytes 8388608
  105.9 54.8 %slice-start.2 = ((s8[6291456]{0:T(1024)(128)(4,1)}), s8[4194304]{0:T(1024)(128)(4,1)S(1)}, s32[]{:S(2)}) async-start(s8[6291456]{0:T(1024)(128)(4,1)} %bitcast.30), calls=%async_computation.5 | async-start | bytes 8388608
  105.9 54.8 %slice-start.5 = ((s8[6291456]{0:T(1024)(128)(4,1)}), s8[4194304]{0:T(1024)(128)(4,1)S(1)}, s32[]{:S(2)}) async-start(s8[6291456]{0:T(1024)(128)(4,1)} %bitcast.36), calls=%async_computation.8 | async-start | bytes 8388608
  108.0 10.3 %collective-permute-start.14 = (bf16[32,4096]{1,0:T(8,128)(2,1)S(1)}, bf16[32,4096]{1,0:T(8,128)(2,1)S(1)}, u32[]{:S(2)}, u32[]{:S(2)}) collective-permute-start(bf16[32,4096]{1,0:T(8,128)(2,1)S(1)} %get-tuple-element.95), channel_id=1, source_target_pairs={{0,2},{1,3},{2,4},{3,5},{4,6},{5,7},{6,0},{7,1},{8,10},{9,11},{10,... | collective-permute-start | bytes 786440 | tf_op jit(solution)/shard_map/ppermute | solution.py:487
  108.7 14.7 %collective-permute-start.15 = (bf16[32,4096]{1,0:T(8,128)(2,1)S(1)}, bf16[32,4096]{1,0:T(8,128)(2,1)S(1)}, u32[]{:S(2)}, u32[]{:S(2)}) collective-permute-start(bf16[32,4096]{1,0:T(8,128)(2,1)S(1)} %get-tuple-element.97), channel_id=1, source_target_pairs={{0,4},{1,5},{2,6},{3,7},{4,0},{5,1},{6,2},{7,3},{8,12},{9,13},{10,... | collective-permute-start | bytes 786440 | tf_op jit(solution)/shard_map/ppermute | solution.py:487
  111.5 12.4 %collective-permute-start.16 = (bf16[32,4096]{1,0:T(8,128)(2,1)S(1)}, bf16[32,4096]{1,0:T(8,128)(2,1)S(1)}, u32[]{:S(2)}, u32[]{:S(2)}) collective-permute-start(bf16[32,4096]{1,0:T(8,128)(2,1)S(1)} %get-tuple-element.96), channel_id=1, source_target_pairs={{0,6},{1,7},{2,0},{3,1},{4,2},{5,3},{6,4},{7,5},{8,14},{9,15},{10,... | collective-permute-start | bytes 786440 | tf_op jit(solution)/shard_map/ppermute | solution.py:487
  124.2 36.5 %slice-start.1 = ((s8[6291456]{0:T(1024)(128)(4,1)}), s8[2097152]{0:T(1024)(128)(4,1)S(1)}, s32[]{:S(2)}) async-start(s8[6291456]{0:T(1024)(128)(4,1)} %bitcast.24), calls=%async_computation.4 | async-start | bytes 4194304
  124.2 36.5 %slice-start.3 = ((s8[6291456]{0:T(1024)(128)(4,1)}), s8[2097152]{0:T(1024)(128)(4,1)S(1)}, s32[]{:S(2)}) async-start(s8[6291456]{0:T(1024)(128)(4,1)} %bitcast.30), calls=%async_computation.6 | async-start | bytes 4194304
  138.9 9.2 %collective-permute-start.19 = (bf16[64,4096]{1,0:T(8,128)(2,1)S(1)}, bf16[64,4096]{1,0:T(8,128)(2,1)S(1)}, u32[]{:S(2)}, u32[]{:S(2)}) collective-permute-start(bf16[64,4096]{1,0:T(8,128)(2,1)S(1)} %bitcast.47), channel_id=1, source_target_pairs={{0,96},{32,0},{64,32},{96,64},{8,104},{40,8},{72,40},{104,72},{16,... | collective-permute-start | bytes 1572872 | tf_op jit(solution)/shard_map/ppermute | solution.py:51
  140.0 10.8 %collective-permute-start.20 = (bf16[64,4096]{1,0:T(8,128)(2,1)S(1)}, bf16[64,4096]{1,0:T(8,128)(2,1)S(1)}, u32[]{:S(2)}, u32[]{:S(2)}) collective-permute-start(bf16[64,4096]{1,0:T(8,128)(2,1)S(1)} %bitcast.48), channel_id=1, source_target_pairs={{0,64},{32,96},{64,0},{96,32},{8,72},{40,104},{72,8},{104,40},{16,... | collective-permute-start | bytes 1572872 | tf_op jit(solution)/shard_map/ppermute | solution.py:51
  141.2 15.1 %collective-permute-start.17 = (bf16[64,4096]{1,0:T(8,128)(2,1)S(1)}, bf16[64,4096]{1,0:T(8,128)(2,1)S(1)}, u32[]{:S(2)}, u32[]{:S(2)}) collective-permute-start(bf16[64,4096]{1,0:T(8,128)(2,1)S(1)} %bitcast.49), channel_id=1, source_target_pairs={{0,32},{32,64},{64,96},{96,0},{8,40},{40,72},{72,104},{104,8},{16,... | collective-permute-start | bytes 1572872 | tf_op jit(solution)/shard_map/ppermute | solution.py:51
  150.8 18.3 %collective-permute-start.21 = (bf16[128,4096]{1,0:T(8,128)(2,1)S(1)}, bf16[128,4096]{1,0:T(8,128)(2,1)S(1)}, u32[]{:S(2)}, u32[]{:S(2)}) collective-permute-start(bf16[128,4096]{1,0:T(8,128)(2,1)S(1)} %constant_dynamic-update-slice_fusion), channel_id=1, source_target_pairs={{0,24},{8,0},{16,8},{24,16},{32,56},{40,32},{48,40},{56,48},{64,88... | collective-permute-start | bytes 3145736 | tf_op jit(solution)/shard_map/ppermute | solution.py:51
  156.4 14.9 %collective-permute-start.18 = (bf16[128,4096]{1,0:T(8,128)(2,1)S(1)}, bf16[128,4096]{1,0:T(8,128)(2,1)S(1)}, u32[]{:S(2)}, u32[]{:S(2)}) collective-permute-start(bf16[128,4096]{1,0:T(8,128)(2,1)S(1)} %pad_maximum_fusion.4), channel_id=1, source_target_pairs={{0,8},{8,16},{16,24},{24,0},{32,40},{40,48},{48,56},{56,32},{64,72... | collective-permute-start | bytes 3145736 | tf_op jit(solution)/shard_map/ppermute | solution.py:51
  158.4 24.7 %collective-permute-start.24 = (bf16[128,4096]{1,0:T(8,128)(2,1)S(1)}, bf16[128,4096]{1,0:T(8,128)(2,1)S(1)}, u32[]{:S(2)}, u32[]{:S(2)}) collective-permute-start(bf16[128,4096]{1,0:T(8,128)(2,1)S(1)} %constant_dynamic-update-slice_fusion), channel_id=1, source_target_pairs={{0,8},{8,16},{16,24},{24,0},{32,40},{40,48},{48,56},{56,32},{64,72... | collective-permute-start | bytes 3145736 | tf_op jit(solution)/shard_map/ppermute | solution.py:51
  158.5 27.9 %collective-permute-start.25 = (bf16[128,4096]{1,0:T(8,128)(2,1)S(1)}, bf16[128,4096]{1,0:T(8,128)(2,1)S(1)}, u32[]{:S(2)}, u32[]{:S(2)}) collective-permute-start(bf16[128,4096]{1,0:T(8,128)(2,1)S(1)} %pad_maximum_fusion.4), channel_id=1, source_target_pairs={{0,24},{8,0},{16,8},{24,16},{32,56},{40,32},{48,40},{56,48},{64,88... | collective-permute-start | bytes 3145736 | tf_op jit(solution)/shard_map/ppermute | solution.py:51
  171.3 23.8 %collective-permute-start.22 = (bf16[128,4096]{1,0:T(8,128)(2,1)S(1)}, bf16[128,4096]{1,0:T(8,128)(2,1)S(1)}, u32[]{:S(2)}, u32[]{:S(2)}) collective-permute-start(bf16[128,4096]{1,0:T(8,128)(2,1)S(1)} %collective-permute-done.18), channel_id=1, source_target_pairs={{0,8},{8,16},{16,24},{24,0},{32,40},{40,48},{48,56},{56,32},{64,72... | collective-permute-start | bytes 3145736 | tf_op jit(solution)/shard_map/ppermute | solution.py:51
  174.4 20.6 %collective-permute-start.23 = (bf16[128,4096]{1,0:T(8,128)(2,1)S(1)}, bf16[128,4096]{1,0:T(8,128)(2,1)S(1)}, u32[]{:S(2)}, u32[]{:S(2)}) collective-permute-start(bf16[128,4096]{1,0:T(8,128)(2,1)S(1)} %collective-permute-done.21), channel_id=1, source_target_pairs={{0,24},{8,0},{16,8},{24,16},{32,56},{40,32},{48,40},{56,48},{64,88... | collective-permute-start | bytes 3145736 | tf_op jit(solution)/shard_map/ppermute | solution.py:51
  183.0 20.6 %collective-permute-start.26 = (bf16[128,4096]{1,0:T(8,128)(2,1)S(1)}, bf16[128,4096]{1,0:T(8,128)(2,1)S(1)}, u32[]{:S(2)}, u32[]{:S(2)}) collective-permute-start(bf16[128,4096]{1,0:T(8,128)(2,1)S(1)} %get-tuple-element.67), channel_id=1, source_target_pairs={{0,24},{8,0},{16,8},{24,16},{32,56},{40,32},{48,40},{56,48},{64,88... | collective-permute-start | bytes 3145736 | tf_op jit(solution)/shard_map/ppermute | solution.py:51
  183.1 21.8 %collective-permute-start.27 = (bf16[128,4096]{1,0:T(8,128)(2,1)S(1)}, bf16[128,4096]{1,0:T(8,128)(2,1)S(1)}, u32[]{:S(2)}, u32[]{:S(2)}) collective-permute-start(bf16[128,4096]{1,0:T(8,128)(2,1)S(1)} %get-tuple-element.75), channel_id=1, source_target_pairs={{0,8},{8,16},{16,24},{24,0},{32,40},{40,48},{48,56},{56,32},{64,72... | collective-permute-start | bytes 3145736 | tf_op jit(solution)/shard_map/ppermute | solution.py:51
  205.0 15.5 %collective-permute-start.28 = (bf16[128,4096]{1,0:T(8,128)(2,1)S(1)}, bf16[128,4096]{1,0:T(8,128)(2,1)S(1)}, u32[]{:S(2)}, u32[]{:S(2)}) collective-permute-start(bf16[128,4096]{1,0:T(8,128)(2,1)S(1)} %get-tuple-element.78), channel_id=1, source_target_pairs={{0,8},{8,16},{16,24},{24,0},{32,40},{40,48},{48,56},{56,32},{64,72... | collective-permute-start | bytes 3145736 | tf_op jit(solution)/shard_map/ppermute | solution.py:51
  208.2 16.3 %collective-permute-start.31 = (bf16[128,4096]{1,0:T(8,128)(2,1)S(1)}, bf16[128,4096]{1,0:T(8,128)(2,1)S(1)}, u32[]{:S(2)}, u32[]{:S(2)}) collective-permute-start(bf16[128,4096]{1,0:T(8,128)(2,1)S(1)} %get-tuple-element.82), channel_id=1, source_target_pairs={{0,24},{8,0},{16,8},{24,16},{32,56},{40,32},{48,40},{56,48},{64,88... | collective-permute-start | bytes 3145736 | tf_op jit(solution)/shard_map/ppermute | solution.py:51
  220.7 16.1 %collective-permute-start.29 = (bf16[128,4096]{1,0:T(8,128)(2,1)S(1)}, bf16[128,4096]{1,0:T(8,128)(2,1)S(1)}, u32[]{:S(2)}, u32[]{:S(2)}) collective-permute-start(bf16[128,4096]{1,0:T(8,128)(2,1)S(1)} %add_convert_fusion.3), channel_id=1, source_target_pairs={{0,8},{8,16},{16,24},{24,0},{32,40},{40,48},{48,56},{56,32},{64,72... | collective-permute-start | bytes 3145736 | tf_op jit(solution)/shard_map/ppermute | solution.py:51
  224.7 18.7 %collective-permute-start.32 = (bf16[128,4096]{1,0:T(8,128)(2,1)S(1)}, bf16[128,4096]{1,0:T(8,128)(2,1)S(1)}, u32[]{:S(2)}, u32[]{:S(2)}) collective-permute-start(bf16[128,4096]{1,0:T(8,128)(2,1)S(1)} %add_convert_fusion.1), channel_id=1, source_target_pairs={{0,24},{8,0},{16,8},{24,16},{32,56},{40,32},{48,40},{56,48},{64,88... | collective-permute-start | bytes 3145736 | tf_op jit(solution)/shard_map/ppermute | solution.py:51
  237.3 17.2 %collective-permute-start.30 = (bf16[64,4096]{1,0:T(8,128)(2,1)S(1)}, bf16[64,4096]{1,0:T(8,128)(2,1)S(1)}, u32[]{:S(2)}, u32[]{:S(2)}) collective-permute-start(bf16[64,4096]{1,0:T(8,128)(2,1)S(1)} %slice.87), channel_id=1, source_target_pairs={{0,96},{32,0},{64,32},{96,64},{8,104},{40,8},{72,40},{104,72},{16,... | collective-permute-start | bytes 1572872 | tf_op jit(solution)/shard_map/ppermute | solution.py:51
  244.0 16.2 %collective-permute-start.33 = (bf16[64,4096]{1,0:T(8,128)(2,1)S(1)}, bf16[64,4096]{1,0:T(8,128)(2,1)S(1)}, u32[]{:S(2)}, u32[]{:S(2)}) collective-permute-start(bf16[64,4096]{1,0:T(8,128)(2,1)S(1)} %get-tuple-element.93), channel_id=1, source_target_pairs={{0,32},{32,64},{64,96},{96,0},{8,40},{40,72},{72,104},{104,8},{16,... | collective-permute-start | bytes 1572872 | tf_op jit(solution)/shard_map/ppermute | solution.py:51
  244.1 23.2 %collective-permute-start.34 = (bf16[64,4096]{1,0:T(8,128)(2,1)S(1)}, bf16[64,4096]{1,0:T(8,128)(2,1)S(1)}, u32[]{:S(2)}, u32[]{:S(2)}) collective-permute-start(bf16[64,4096]{1,0:T(8,128)(2,1)S(1)} %get-tuple-element.94), channel_id=1, source_target_pairs={{0,64},{32,96},{64,0},{96,32},{8,72},{40,104},{72,8},{104,40},{16,... | collective-permute-start | bytes 1572872 | tf_op jit(solution)/shard_map/ppermute | solution.py:51
Sparse Core Ops, SparseCore 0:
  9.5 74.7 all-gather.2

commit v5 on v4

--- a/solution.py
+++ b/solution.py
@@ -60,31 +60,27 @@
 def conv_kernel(
     order_ref,
     x_hbm,
-    weight_hbm,
-    bias_hbm,
     proj_hbm,
+    weight_ref,
     rim_ref,
     mixed_ref,
     send_ref,
     keep_ref,
     x_ref,
-    weight_ref,
-    bias_ref,
     proj_ref,
     padded,
     part_ref,
     sems,
 ):
-    sources = (x_hbm, weight_hbm, bias_hbm, proj_hbm)
-    targets = (x_ref, weight_ref, bias_ref, proj_ref)
+    sources = (x_hbm, proj_hbm)
+    targets = (x_ref, proj_ref)
     copies = [pltpu.make_async_copy(*pair, sems.at[k]) for k, pair in enumerate(zip(sources, targets))]
     for copy in copies:
         copy.start()
     length, channels = x_ref.shape
     steps = length // SEG
     head = 8
-    for copy in copies[:3]:
-        copy.wait()
+    copies[0].wait()
     for lane in range(0, channels, LANES):
         block = padded.at[lane // LANES]
         block[head - (CONV - 1) : head, :] = rim_ref[:, lane : lane + LANES].astype(F32)
@@ -94,7 +90,7 @@
         rows = pl.ds(pl.multiple_of(i * SEG, SEG), SEG)
         for lane in range(0, channels, LANES):
             lanes = pl.ds(lane, LANES)
-            acc = jnp.broadcast_to(bias_ref[:, lanes], (SEG, LANES))
+            acc = jnp.broadcast_to(weight_ref[CONV : CONV + 1, lanes], (SEG, LANES))
             for tap in range(CONV):
                 taken = padded[
                     lane // LANES, pl.ds(i + head - (CONV - 1) + tap, SEG, stride=steps), :
@@ -104,7 +100,7 @@
         return carry
 
     lax.fori_loop(0, steps, step, 0)
-    copies[3].wait()
+    copies[1].wait()
     part_ref[...] = lax.dot_general(
         mixed_ref[...].astype(BF16),
         proj_ref[...],
@@ -438,14 +434,17 @@
     run = functools.partial(expert, gate=gate, up=up, down=down)
     behind = along(rows, 0, 1)
     ahead = along(rows, 0, -1)
-    across = along(rows, 0, 2)
-    own = jnp.concatenate([rows, behind, ahead, across], axis=0)
-    own_first, own_second = halves(own)
+    across = jnp.concatenate(
+        [along(halves(behind)[0], 0, 1), along(halves(ahead)[1], 0, -1)], axis=0
+    )
+    own_first = jnp.concatenate([rows, behind], axis=0)
     behind_first = along(own_first, 1, 1)
-    ahead_second = along(own_second, 1, -1)
+    across, own_first_later = lax.optimization_barrier((across, own_first))
+    own_second = jnp.concatenate([ahead, across], axis=0)
+    ahead_second = jnp.concatenate([along(ahead, 1, -1), along(across, 1, -1)], axis=0)
     behind_second = along(own_second, 1, 1)
-    ahead_first = along(own_first, 1, -1)
-    own_out = run(own)
+    ahead_first = along(own_first_later, 1, -1)
+    own_out = run(jnp.concatenate([own_first, own_second], axis=0))
     behind_first, ahead_second, own_out = lax.optimization_barrier(
         (behind_first, ahead_second, own_out)
     )
@@ -467,10 +466,16 @@
     )
     late_first = along(added(ahead_rest, along(across_first, 1, 1)), 1, 1)
     late_second = along(added(behind_rest, along(across_second, 1, -1)), 1, -1)
-    first = added(own_out[0], early_first, late_first)
-    second = added(own_out[1], early_second, late_second)
-    (kept, behind), (ahead, across) = halves(first), halves(second)
-    return added(kept, along(behind, 0, -1), along(ahead, 0, 1), along(across, 0, 2))
+    kept, behind = halves(added(own_out[0], early_first, late_first))
+    ahead, across = halves(added(own_out[1], early_second, late_second))
+    across_first, across_second = halves(across)
+    ahead_first, ahead_second = halves(ahead)
+    behind_first, behind_second = halves(behind)
+    ahead_first = added(ahead_first, along(across_first, 0, 1))
+    behind_second = added(behind_second, along(across_second, 0, -1))
+    from_behind = along(jnp.concatenate([ahead_first, ahead_second], axis=0), 0, 1)
+    from_ahead = along(jnp.concatenate([behind_first, behind_second], axis=0), 0, -1)
+    return added(kept, from_behind, from_ahead)
 
 
 def mixer(x_in, z_in, conv_weight, conv_bias, x_proj, dt_proj, dt_bias, a_log, d_skip, out_proj):
@@ -501,20 +506,18 @@
             jax.ShapeDtypeStruct((length // 2, RANK + 2 * STATE), F32),
             jax.ShapeDtypeStruct((length // 2, RANK + 2 * STATE), F32),
         ),
-        in_specs=[pl.BlockSpec(memory_space=pltpu.SMEM)] + [far()] * 4 + [whole()],
+        in_specs=[pl.BlockSpec(memory_space=pltpu.SMEM)] + [far()] * 2 + [whole()] * 2,
         out_specs=[whole()] * 3,
         scratch_shapes=[
             pltpu.VMEM(x_in.shape, BF16),
-            pltpu.VMEM(conv_weight.shape, F32),
-            pltpu.VMEM((1, channels), F32),
             pltpu.VMEM(x_proj.shape[::-1], BF16),
             pltpu.VMEM((channels // LANES, length + 8, LANES), F32),
             pltpu.VMEM((length, RANK + 2 * STATE), F32),
-            pltpu.SemaphoreType.DMA((4,)),
+            pltpu.SemaphoreType.DMA((2,)),
         ],
-        compiler_params=params(12),
+        compiler_params=params(59),
         name="conv",
-    )(order, x_in, conv_weight, conv_bias[None, :], x_proj.T, rim)
+    )(order, x_in, x_proj.T, jnp.concatenate([conv_weight, conv_bias[None, :]], axis=0), rim)
     sums = (keep + lax.ppermute(send, "exp", swap)).reshape(side, length // owners, -1)
     summed = sums[0]
     for hop in range(1, side):
@@ -549,7 +552,7 @@
             pltpu.SemaphoreType.DMA((2,)),
             pltpu.SemaphoreType.DMA((4, channels // LANES)),
         ],
-        compiler_params=params(16),
+        compiler_params=params(58),
         name="scan",
     )(arrival, near, other, mixed, rates, dt_proj, dt_bias[None, :])
     entering = entering_state(message, rates)
@@ -571,7 +574,7 @@
             pltpu.SemaphoreType.DMA((4,)),
             pltpu.SemaphoreType.DMA((2, channels // LANES)),
         ],
-        compiler_params=params(18),
+        compiler_params=params(58),
         name="finish",
     )(
         order,

time: 289 us -> 280 us (0.969)
  waiting for transfers between devices: 110 us -> 93.3 us
  Pallas kernels: 62.5 us -> 67.7 us
  other arithmetic: 5.83 us -> 10.4 us
  local copies, waits for them, and re-layouts: 10.9 us -> 6.67 us
    ppermute x18 -> x21, waiting for transfers between devices: 59.4 us -> 47.7 us  [along(): return lax.ppermute(block, ('seq', 'exp'), route)]
    unnamed x48 -> x37, local copies, waits for them, and re-layouts: 9.42 us -> 5.27 us
    ppermute x18 -> x21, starting transfers between devices: 32.7 us -> 32.5 us  [along(): return lax.ppermute(block, ('seq', 'exp'), route)]
  transfers between devices with their start and end apart: 36 -> 39, of which waited for: 26 -> 21; matrix products, arithmetic and copies ran while one was open for 2% -> 3% of each run, Pallas kernels for 19% -> 22%
where the time goes in v5:
time: 280 us; the launch traced here: 279 us
  waiting for transfers between devices  93.3 us (33%)
  Pallas kernels  67.7 us (24%)
  starting transfers between devices  57.8 us (21%)
  blocking collectives  27.1 us (10%)
  between operations  14.1 us (5%)
  other arithmetic  10.4 us (4%)
  local copies, waits for them, and re-layouts  6.67 us (2%)
    ppermute x21, waiting for transfers between devices, along(): return lax.ppermute(block, ('seq', 'exp'), route)  47.7 us
    pallas_call x4, Pallas kernels, expert(): pl.pallas_call(expert_kernel, out_shape=(jax.ShapeDtypeStruct((count // 2...  33.5 us
    ppermute x21, starting transfers between devices, along(): return lax.ppermute(block, ('seq', 'exp'), route)  32.5 us
    ppermute x4, waiting for transfers between devices, entering_state(): got = lax.ppermute(message, 'seq', route)  23.9 us
    ppermute x9, starting transfers between devices, along_z(): lax.ppermute(block, 'exp', [(e, (e + 2 * hop) % owners) for e in range(ow...  16.6 us
    ppermute x9, waiting for transfers between devices, along_z(): lax.ppermute(block, 'exp', [(e, (e + 2 * hop) % owners) for e in range(ow...  16.2 us
    all_to_all x1, blocking collectives, shards(): lax.all_to_all(outgoing, 'exp', split_axis=0, concat_axis=0, tiled=True)  14.3 us
    all_to_all x1, blocking collectives, shards(): lax.all_to_all(expert_out, 'exp', split_axis=0, concat_axis=0, tiled=True)  12.8 us
  transfers between devices with their start and end apart: 39, of which 21 were waited for; matrix products, arithmetic and copies ran while one was open for 3% of the time, Pallas kernels for 22%

profile of v5, /device:TPU:24, one launch (start us, length us, event | category | flops | bytes accessed | tf_op | source)
XLA Modules:
  0.0 278.5 jit_solution(17168876678908044132)
XLA Ops:
  6.5 0.7 all-gather.3.cloned.1.call-update
  7.3 0.7 slice.81
  8.0 3.0 %collective-permute-start = (bf16[3,1024]{1,0:T(4,128)(2,1)S(1)}, bf16[3,1024]{1,0:T(4,128)(2,1)S(1)}, u32[]{:S(2)}, u32[]{:S(2)}) collective-permute-start(bf16[3,1024]{1,0:T(4,128)(2,1)S(1)} %slice.81), channel_id=1, source_target_pairs={{0,8},{8,16},{16,24},{24,32},{32,40},{40,48},{48,56},{56,64},{64,7... | collective-permute-start | bytes 18440 | tf_op jit(solution)/shard_map/ppermute | solution.py:57
  11.1 1.4 pad_maximum_fusion.11.weight_ref
  14.1 6.2 %conv.1 = (f32[256,1024]{1,0:T(8,128)}, f32[128,288]{1,0:T(8,128)}, f32[128,288]{1,0:T(8,128)}) custom-call(s32[8]{0:T(128)} %pad_add_fusion.order_ref, bf16[256,1024]{1,0:T(8,128)(2,1)} %x_hbm.1, bf16[288,1024]{1,0:T(8,128)(2,1)} %bitcast.47, f32[5,1024]{1,0:T(8,128)} %pad_maximum_fusion.11.weight_ref, bf16[3,1024]{1,0:T(4,128)(2,1)} %copy-done.9), custom_call_target="tpu_custom_call" | custom-call | tf_op jit(solution)/shard_map/conv/pallas_call | solution.py:502
  20.4 1.6 collective-permute-done.1
  22.0 1.0 add.162
  23.0 2.0 collective-permute-start.2
  25.0 3.5 %collective-permute-start.3 = (f32[32,288]{1,0:T(8,128)S(1)}, f32[32,288]{1,0:T(8,128)S(1)}, u32[]{:S(2)}, u32[]{:S(2)}) collective-permute-start(f32[32,288]{1,0:T(8,128)S(1)} %get-tuple-element.105), channel_id=1, source_target_pairs={{0,4},{1,5},{2,6},{3,7},{4,0},{5,1},{6,2},{7,3},{8,12},{9,13},{10,... | collective-permute-start | bytes 110600 | tf_op jit(solution)/shard_map/ppermute | solution.py:492
  28.6 1.0 collective-permute-start.4
  29.6 0.6 multiply_bitcast_fusion.rates_ref
  30.2 1.1 collective-permute-done.3
  31.4 1.3 collective-permute-done.4
  32.8 3.7 %collective-permute-start.6 = (bf16[32,320]{1,0:T(8,128)(2,1)S(1)}, bf16[32,320]{1,0:T(8,128)(2,1)S(1)}, u32[]{:S(2)}, u32[]{:S(2)}) collective-permute-start(bf16[32,320]{1,0:T(8,128)(2,1)S(1)} %pad_maximum_fusion.12), channel_id=1, source_target_pairs={{0,4},{1,5},{2,6},{3,7},{4,0},{5,1},{6,2},{7,3},{8,12},{9,13},{10,... | collective-permute-start | bytes 61448 | tf_op jit(solution)/shard_map/ppermute | solution.py:492
  36.9 0.9 collective-permute-done.5
  37.8 0.7 collective-permute-done.6
  38.5 1.8 collective-permute-done.7
  41.0 0.7 collective-permute-done.8.other_ref
  42.4 11.0 %scan.1 = (bf16[256,320]{1,0:T(8,128)(2,1)}, f32[17,1024]{1,0:T(8,128)}, f32[256,1024]{1,0:T(8,128)}, f32[256,1024]{1,0:T(8,128)}, f32[8,1024]{1,0:T(8,128)}, /*index=5*/f32[16,8,1024]{2,1,0:T(8,128)}) custom-call(s32[8]{0:T(128)} %pad_add_fusion.1.order_ref, bf16[128,320]{1,0:T(8,128)(2,1)} %copy-done.5, bf16[128,320]{1,0:T(8,128)(2,1)} %copy-done.7, ...), custom_call_target="tpu_custom_call" | custom-call | tf_op jit(solution)/shard_map/scan/pallas_call | solution.py:531
  53.4 0.8 collective-permute-start.9
  54.2 6.9 %collective-permute-done.9.got_ref = f32[17,1024]{1,0:T(8,128)S(1)} collective-permute-done((f32[17,1024]{1,0:T(8,128)}, f32[17,1024]{1,0:T(8,128)S(1)}, u32[]{:S(2)}, u32[]{:S(2)}) %collective-permute-start.9) | collective-permute-done | bytes 69664 | tf_op jit(solution)/shard_map/ppermute | solution.py:265
  61.2 0.9 copy-done.3
  62.4 8.2 %collective-permute-done.10.got_ref = f32[17,1024]{1,0:T(8,128)S(1)} collective-permute-done((f32[17,1024]{1,0:T(8,128)S(1)}, f32[17,1024]{1,0:T(8,128)S(1)}, u32[]{:S(2)}, u32[]{:S(2)}) %collective-permute-start.10) | collective-permute-done | bytes 69664 | tf_op jit(solution)/shard_map/ppermute | solution.py:265
  70.7 1.6 collective-permute-start.11
  72.2 5.5 %collective-permute-done.11.got_ref = f32[17,1024]{1,0:T(8,128)S(1)} collective-permute-done((f32[17,1024]{1,0:T(8,128)S(1)}, f32[17,1024]{1,0:T(8,128)S(1)}, u32[]{:S(2)}, u32[]{:S(2)}) %collective-permute-start.11) | collective-permute-done | bytes 69664 | tf_op jit(solution)/shard_map/ppermute | solution.py:265
  77.7 2.8 %collective-permute-start.12 = (f32[17,1024]{1,0:T(8,128)S(1)}, f32[17,1024]{1,0:T(8,128)S(1)}, u32[]{:S(2)}, u32[]{:S(2)}) collective-permute-start(f32[17,1024]{1,0:T(8,128)S(1)} %get-tuple-element.54.own_ref), channel_id=1, source_target_pairs={{0,96},{8,104},{16,112},{24,120},{32,64},{40,72},{48,80},{56,88},{... | collective-permute-start | bytes 208904 | tf_op jit(solution)/shard_map/ppermute | solution.py:265
  80.6 3.3 %collective-permute-done.12.got_ref = f32[17,1024]{1,0:T(8,128)S(1)} collective-permute-done((f32[17,1024]{1,0:T(8,128)S(1)}, f32[17,1024]{1,0:T(8,128)S(1)}, u32[]{:S(2)}, u32[]{:S(2)}) %collective-permute-start.12) | collective-permute-done | bytes 69664 | tf_op jit(solution)/shard_map/ppermute | solution.py:265
  83.9 0.7 meet.7
  84.5 0.6 copy-done.4
  85.2 10.0 %finish.1.gated_ref = bf16[256,1024]{1,0:T(8,128)(2,1)} custom-call(s32[8]{0:T(128)} %pad_add_fusion.order_ref, f32[17,1024]{1,0:T(8,128)} %copy-done.4, f32[16,1024]{1,0:T(8,128)} %multiply_bitcast_fusion.rates_ref, bf16[256,320]{1,0:T(8,128)(2,1)} %get-tuple-element.57.packed_ref, f32[256,1024]{1,0:T(8,128)} %get-tuple-element.48.mixed_ref, ...), custom_call_target="tpu_custom_call" | custom-call | tf_op jit(solution)/shard_map/finish/pallas_call | solution.py:559
  95.3 1.0 copy-done.2
  96.3 6.2 %outward.1 = (bf16[128,4096]{1,0:T(8,128)(2,1)S(1)}, f32[128,4096]{1,0:T(8,128)S(1)}) custom-call(bf16[256,1024]{1,0:T(8,128)(2,1)S(1)} %copy-done.2, bf16[16,1024,256]{2,1,0:T(8,128)(2,1)} %bitcast.42), custom_call_target="tpu_custom_call" | custom-call | tf_op jit(solution)/shard_map/outward/pallas_call | solution.py:594
  102.5 1.3 copy-done.1
  104.8 1.8 collective-permute-done.13
  106.7 2.3 fusion.18
  109.1 1.6 collective-permute-start.14
  110.7 2.9 %collective-permute-start.15 = (bf16[32,4096]{1,0:T(8,128)(2,1)S(1)}, bf16[32,4096]{1,0:T(8,128)(2,1)S(1)}, u32[]{:S(2)}, u32[]{:S(2)}) collective-permute-start(bf16[32,4096]{1,0:T(8,128)(2,1)S(1)} %get-tuple-element.102), channel_id=1, source_target_pairs={{0,4},{1,5},{2,6},{3,7},{4,0},{5,1},{6,2},{7,3},{8,12},{9,13},{10,... | collective-permute-start | bytes 786440 | tf_op jit(solution)/shard_map/ppermute | solution.py:492
  113.5 1.4 collective-permute-start.16
  115.0 3.7 %collective-permute-done.14 = bf16[32,4096]{1,0:T(8,128)(2,1)S(1)} collective-permute-done((bf16[32,4096]{1,0:T(8,128)(2,1)S(1)}, bf16[32,4096]{1,0:T(8,128)(2,1)S(1)}, u32[]{:S(2)}, u32[]{:S(2)}) %collective-permute-start.14) | collective-permute-done | bytes 262176 | tf_op jit(solution)/shard_map/ppermute | solution.py:492
  118.7 6.8 %collective-permute-done.15 = bf16[32,4096]{1,0:T(8,128)(2,1)S(1)} collective-permute-done((bf16[32,4096]{1,0:T(8,128)(2,1)S(1)}, bf16[32,4096]{1,0:T(8,128)(2,1)S(1)}, u32[]{:S(2)}, u32[]{:S(2)}) %collective-permute-start.15) | collective-permute-done | bytes 262176 | tf_op jit(solution)/shard_map/ppermute | solution.py:492
  126.2 14.3 %all_to_all.10 = bf16[8,8,4096]{2,1,0:T(8,128)(2,1)S(1)} all-to-all(bf16[8,8,4096]{2,1,0:T(8,128)(2,1)S(1)} %fusion), channel_id=1, replica_groups=mesh['seq'=16,'exp'=8] {'exp'}, dimensions={0} | all-to-all | bytes 1048576 | tf_op jit(solution)/shard_map/all_to_all | solution.py:664
  140.7 3.0 %collective-permute-start.19 = (bf16[64,4096]{1,0:T(8,128)(2,1)S(1)}, bf16[64,4096]{1,0:T(8,128)(2,1)S(1)}, u32[]{:S(2)}, u32[]{:S(2)}) collective-permute-start(bf16[64,4096]{1,0:T(8,128)(2,1)S(1)} %bitcast.44), channel_id=1, source_target_pairs={{0,96},{32,0},{64,32},{96,64},{8,104},{40,8},{72,40},{104,72},{16,... | collective-permute-start | bytes 1572872 | tf_op jit(solution)/shard_map/ppermute | solution.py:51
  143.7 7.2 %collective-permute-done.17 = bf16[64,4096]{1,0:T(8,128)(2,1)S(1)} collective-permute-done((bf16[64,4096]{1,0:T(8,128)(2,1)S(1)}, bf16[64,4096]{1,0:T(8,128)(2,1)S(1)}, u32[]{:S(2)}, u32[]{:S(2)}) %collective-permute-start.17) | collective-permute-done | bytes 524320 | tf_op jit(solution)/shard_map/ppermute | solution.py:51
  151.0 3.3 %collective-permute-start.22 = (bf16[32,4096]{1,0:T(8,128)(2,1)S(1)}, bf16[32,4096]{1,0:T(8,128)(2,1)S(1)}, u32[]{:S(2)}, u32[]{:S(2)}) collective-permute-start(bf16[32,4096]{1,0:T(8,128)(2,1)S(1)} %slice.112), channel_id=1, source_target_pairs={{0,96},{32,0},{64,32},{96,64},{8,104},{40,8},{72,40},{104,72},{16,... | collective-permute-start | bytes 786440 | tf_op jit(solution)/shard_map/ppermute | solution.py:51
  154.4 1.4 collective-permute-start.18
  155.8 0.7 collective-permute-start.20
  156.5 4.8 %collective-permute-done.21 = bf16[32,4096]{1,0:T(8,128)(2,1)S(1)} collective-permute-done((bf16[32,4096]{1,0:T(8,128)(2,1)S(1)}, bf16[32,4096]{1,0:T(8,128)(2,1)S(1)}, u32[]{:S(2)}, u32[]{:S(2)}) %collective-permute-start.21) | collective-permute-done | bytes 262176 | tf_op jit(solution)/shard_map/ppermute | solution.py:51
  161.9 2.9 %collective-permute-start.26 = (bf16[128,4096]{1,0:T(8,128)(2,1)S(1)}, bf16[128,4096]{1,0:T(8,128)(2,1)S(1)}, u32[]{:S(2)}, u32[]{:S(2)}) collective-permute-start(bf16[128,4096]{1,0:T(8,128)(2,1)S(1)} %pad_maximum_fusion.6), channel_id=1, source_target_pairs={{0,8},{8,16},{16,24},{24,0},{32,40},{40,48},{48,56},{56,32},{64,72... | collective-permute-start | bytes 3145736 | tf_op jit(solution)/shard_map/ppermute | solution.py:51
  165.1 8.4 %expert.4 = (bf16[128,4096]{1,0:T(8,128)(2,1)S(1)}, bf16[128,4096]{1,0:T(8,128)(2,1)S(1)}) custom-call(bf16[256,4096]{1,0:T(8,128)(2,1)S(1)} %pad_maximum_fusion.rows_ref, bf16[4096,768]{1,0:T(8,128)(2,1)S(1)} %bitcast.26, bf16[4096,768]{1,0:T(8,128)(2,1)S(1)} %bitcast.32, bf16[768,4096]{1,0:T(8,128)(2,1)S(1)} %bitcast.38), custom_call_target="tpu_custom_call" | custom-call | flops 1048576 | bytes 1048576 | tf_op jit(solution)/shard_map/expert/pallas_call | solution.py:407
  173.7 3.3 %collective-permute-start.24 = (bf16[128,4096]{1,0:T(8,128)(2,1)S(1)}, bf16[128,4096]{1,0:T(8,128)(2,1)S(1)}, u32[]{:S(2)}, u32[]{:S(2)}) collective-permute-start(bf16[128,4096]{1,0:T(8,128)(2,1)S(1)} %collective-permute-done.18), channel_id=1, source_target_pairs={{0,8},{8,16},{16,24},{24,0},{32,40},{40,48},{48,56},{56,32},{64,72... | collective-permute-start | bytes 3145736 | tf_op jit(solution)/shard_map/ppermute | solution.py:51
  177.2 8.4 %expert.5 = (bf16[128,4096]{1,0:T(8,128)(2,1)S(1)}, bf16[128,4096]{1,0:T(8,128)(2,1)S(1)}) custom-call(bf16[256,4096]{1,0:T(8,128)(2,1)S(1)} %pad_maximum_fusion.1.rows_ref, bf16[4096,768]{1,0:T(8,128)(2,1)S(1)} %bitcast.27, bf16[4096,768]{1,0:T(8,128)(2,1)S(1)} %bitcast.33, bf16[768,4096]{1,0:T(8,128)(2,1)S(1)} %bitcast.39), custom_call_target="tpu_custom_call" | custom-call | flops 1048576 | bytes 1048576 | tf_op jit(solution)/shard_map/expert/pallas_call | solution.py:407
  185.7 3.3 %collective-permute-start.29 = (bf16[128,4096]{1,0:T(8,128)(2,1)S(1)}, bf16[128,4096]{1,0:T(8,128)(2,1)S(1)}, u32[]{:S(2)}, u32[]{:S(2)}) collective-permute-start(bf16[128,4096]{1,0:T(8,128)(2,1)S(1)} %get-tuple-element.79), channel_id=1, source_target_pairs={{0,8},{8,16},{16,24},{24,0},{32,40},{40,48},{48,56},{56,32},{64,72... | collective-permute-start | bytes 3145736 | tf_op jit(solution)/shard_map/ppermute | solution.py:51
  189.2 8.4 %expert.6 = (bf16[128,4096]{1,0:T(8,128)(2,1)S(1)}, bf16[128,4096]{1,0:T(8,128)(2,1)S(1)}) custom-call(bf16[256,4096]{1,0:T(8,128)(2,1)S(1)} %pad_maximum_fusion.2.rows_ref, bf16[4096,768]{1,0:T(8,128)(2,1)S(1)} %bitcast.28, bf16[4096,768]{1,0:T(8,128)(2,1)S(1)} %bitcast.34, bf16[768,4096]{1,0:T(8,128)(2,1)S(1)} %bitcast.40), custom_call_target="tpu_custom_call" | custom-call | flops 1048576 | bytes 1048576 | tf_op jit(solution)/shard_map/expert/pallas_call | solution.py:407
  197.8 8.4 %expert.7 = (bf16[128,4096]{1,0:T(8,128)(2,1)S(1)}, bf16[128,4096]{1,0:T(8,128)(2,1)S(1)}) custom-call(bf16[256,4096]{1,0:T(8,128)(2,1)S(1)} %pad_maximum_fusion.3.rows_ref, bf16[4096,768]{1,0:T(8,128)(2,1)S(1)} %bitcast.29, bf16[4096,768]{1,0:T(8,128)(2,1)S(1)} %bitcast.35, bf16[768,4096]{1,0:T(8,128)(2,1)S(1)} %bitcast.41), custom_call_target="tpu_custom_call" | custom-call | flops 1048576 | bytes 1048576 | tf_op jit(solution)/shard_map/expert/pallas_call | solution.py:407
  206.3 3.2 %collective-permute-start.30 = (bf16[128,4096]{1,0:T(8,128)(2,1)S(1)}, bf16[128,4096]{1,0:T(8,128)(2,1)S(1)}, u32[]{:S(2)}, u32[]{:S(2)}) collective-permute-start(bf16[128,4096]{1,0:T(8,128)(2,1)S(1)} %get-tuple-element.82), channel_id=1, source_target_pairs={{0,8},{8,16},{16,24},{24,0},{32,40},{40,48},{48,56},{56,32},{64,72... | collective-permute-start | bytes 3145736 | tf_op jit(solution)/shard_map/ppermute | solution.py:51
  209.5 12.8 %collective-permute-done.32 = bf16[128,4096]{1,0:T(8,128)(2,1)S(1)} collective-permute-done((bf16[128,4096]{1,0:T(8,128)(2,1)S(1)}, bf16[128,4096]{1,0:T(8,128)(2,1)S(1)}, u32[]{:S(2)}, u32[]{:S(2)}) %collective-permute-start.32) | collective-permute-done | bytes 1048608 | tf_op jit(solution)/shard_map/ppermute | solution.py:51
  222.9 3.5 %collective-permute-start.31 = (bf16[128,4096]{1,0:T(8,128)(2,1)S(1)}, bf16[128,4096]{1,0:T(8,128)(2,1)S(1)}, u32[]{:S(2)}, u32[]{:S(2)}) collective-permute-start(bf16[128,4096]{1,0:T(8,128)(2,1)S(1)} %add_convert_fusion.3), channel_id=1, source_target_pairs={{0,8},{8,16},{16,24},{24,0},{32,40},{40,48},{48,56},{56,32},{64,72... | collective-permute-start | bytes 3145736 | tf_op jit(solution)/shard_map/ppermute | solution.py:51
  226.4 12.2 %collective-permute-done.33 = bf16[128,4096]{1,0:T(8,128)(2,1)S(1)} collective-permute-done((bf16[128,4096]{1,0:T(8,128)(2,1)S(1)}, bf16[128,4096]{1,0:T(8,128)(2,1)S(1)}, u32[]{:S(2)}, u32[]{:S(2)}) %collective-permute-start.33) | collective-permute-done | bytes 1048608 | tf_op jit(solution)/shard_map/ppermute | solution.py:51
  239.2 3.5 %collective-permute-start.36 = (bf16[32,4096]{1,0:T(8,128)(2,1)S(1)}, bf16[32,4096]{1,0:T(8,128)(2,1)S(1)}, u32[]{:S(2)}, u32[]{:S(2)}) collective-permute-start(bf16[32,4096]{1,0:T(8,128)(2,1)S(1)} %get-tuple-element.98), channel_id=1, source_target_pairs={{0,96},{32,0},{64,32},{96,64},{8,104},{40,8},{72,40},{104,72},{16,... | collective-permute-start | bytes 786440 | tf_op jit(solution)/shard_map/ppermute | solution.py:51
  243.2 3.8 %collective-permute-done.34 = bf16[32,4096]{1,0:T(8,128)(2,1)S(1)} collective-permute-done((bf16[32,4096]{1,0:T(8,128)(2,1)S(1)}, bf16[32,4096]{1,0:T(8,128)(2,1)S(1)}, u32[]{:S(2)}, u32[]{:S(2)}) %collective-permute-start.34) | collective-permute-done | bytes 262176 | tf_op jit(solution)/shard_map/ppermute | solution.py:51
  247.3 3.3 %collective-permute-start.37 = (bf16[64,4096]{1,0:T(8,128)(2,1)S(1)}, bf16[64,4096]{1,0:T(8,128)(2,1)S(1)}, u32[]{:S(2)}, u32[]{:S(2)}) collective-permute-start(bf16[64,4096]{1,0:T(8,128)(2,1)S(1)} %pad_maximum_fusion.9), channel_id=1, source_target_pairs={{0,96},{32,0},{64,32},{96,64},{8,104},{40,8},{72,40},{104,72},{16,... | collective-permute-start | bytes 1572872 | tf_op jit(solution)/shard_map/ppermute | solution.py:51
  250.5 7.0 %collective-permute-done.35 = bf16[64,4096]{1,0:T(8,128)(2,1)S(1)} collective-permute-done((bf16[64,4096]{1,0:T(8,128)(2,1)S(1)}, bf16[64,4096]{1,0:T(8,128)(2,1)S(1)}, u32[]{:S(2)}, u32[]{:S(2)}) %collective-permute-start.35) | collective-permute-done | bytes 524320 | tf_op jit(solution)/shard_map/ppermute | solution.py:51
  257.7 12.8 %all_to_all.11 = bf16[8,8,4096]{2,1,0:T(8,128)(2,1)S(1)} all-to-all(bf16[8,8,4096]{2,1,0:T(8,128)(2,1)S(1)} %fusion.1), channel_id=1, replica_groups=mesh['seq'=16,'exp'=8] {'exp'}, dimensions={0} | all-to-all | bytes 1048576 | tf_op jit(solution)/shard_map/all_to_all | solution.py:667
  270.5 1.1 convolution_add_fusion
  (122 shorter events, 10.3 us)
Async XLA Ops:
  6.5 23.1 %copy-start.8 = (f32[1024,16]{0,1:T(8,128)S(1)}, f32[1024,16]{0,1:T(8,128)}, u32[]{:S(2)}) copy-start(f32[1024,16]{0,1:T(8,128)} %param.23) | copy-start | bytes 196612
  6.5 88.7 %all-gather.3.cloned.1.call-start = ((), (), s32[]{:S(2)}) async-start(), calls=%async_computation.2 | async-start | bytes 8912896 | tf_op jit(solution)/shard_map/all_gather | solution.py:494
  8.0 5.5 %collective-permute-start = (bf16[3,1024]{1,0:T(4,128)(2,1)S(1)}, bf16[3,1024]{1,0:T(4,128)(2,1)S(1)}, u32[]{:S(2)}, u32[]{:S(2)}) collective-permute-start(bf16[3,1024]{1,0:T(4,128)(2,1)S(1)} %slice.81), channel_id=1, source_target_pairs={{0,8},{8,16},{16,24},{24,32},{32,40},{40,48},{48,56},{56,64},{64,7... | collective-permute-start | bytes 18440 | tf_op jit(solution)/shard_map/ppermute | solution.py:57
  13.5 0.6 copy-start.9
  20.3 1.7 collective-permute-start.1
  23.0 7.2 %collective-permute-start.2 = (f32[32,288]{1,0:T(8,128)S(1)}, f32[32,288]{1,0:T(8,128)S(1)}, u32[]{:S(2)}, u32[]{:S(2)}) collective-permute-start(f32[32,288]{1,0:T(8,128)S(1)} %get-tuple-element.103), channel_id=1, source_target_pairs={{0,2},{1,3},{2,4},{3,5},{4,6},{5,7},{6,0},{7,1},{8,10},{9,11},{10,... | collective-permute-start | bytes 110600 | tf_op jit(solution)/shard_map/ppermute | solution.py:492
  25.0 6.4 %collective-permute-start.3 = (f32[32,288]{1,0:T(8,128)S(1)}, f32[32,288]{1,0:T(8,128)S(1)}, u32[]{:S(2)}, u32[]{:S(2)}) collective-permute-start(f32[32,288]{1,0:T(8,128)S(1)} %get-tuple-element.105), channel_id=1, source_target_pairs={{0,4},{1,5},{2,6},{3,7},{4,0},{5,1},{6,2},{7,3},{8,12},{9,13},{10,... | collective-permute-start | bytes 110600 | tf_op jit(solution)/shard_map/ppermute | solution.py:492
  28.6 4.1 %collective-permute-start.4 = (f32[32,288]{1,0:T(8,128)S(1)}, f32[32,288]{1,0:T(8,128)S(1)}, u32[]{:S(2)}, u32[]{:S(2)}) collective-permute-start(f32[32,288]{1,0:T(8,128)S(1)} %get-tuple-element.104), channel_id=1, source_target_pairs={{0,6},{1,7},{2,0},{3,1},{4,2},{5,3},{6,4},{7,5},{8,14},{9,15},{10,... | collective-permute-start | bytes 110600 | tf_op jit(solution)/shard_map/ppermute | solution.py:492
  30.2 30.9 %copy-start = (f32[16,1024]{1,0:T(8,128)S(1)}, f32[16,1024]{1,0:T(8,128)}, u32[]{:S(2)}) copy-start(f32[16,1024]{1,0:T(8,128)} %multiply_bitcast_fusion.rates_ref) | copy-start | bytes 196612
  32.8 5.0 %collective-permute-start.5 = (bf16[32,320]{1,0:T(8,128)(2,1)S(1)}, bf16[32,320]{1,0:T(8,128)(2,1)S(1)}, u32[]{:S(2)}, u32[]{:S(2)}) collective-permute-start(bf16[32,320]{1,0:T(8,128)(2,1)S(1)} %pad_maximum_fusion.12), channel_id=1, source_target_pairs={{0,2},{1,3},{2,4},{3,5},{4,6},{5,7},{6,0},{7,1},{8,10},{9,11},{10,... | collective-permute-start | bytes 61448 | tf_op jit(solution)/shard_map/ppermute | solution.py:492
  32.8 5.7 %collective-permute-start.6 = (bf16[32,320]{1,0:T(8,128)(2,1)S(1)}, bf16[32,320]{1,0:T(8,128)(2,1)S(1)}, u32[]{:S(2)}, u32[]{:S(2)}) collective-permute-start(bf16[32,320]{1,0:T(8,128)(2,1)S(1)} %pad_maximum_fusion.12), channel_id=1, source_target_pairs={{0,4},{1,5},{2,6},{3,7},{4,0},{5,1},{6,2},{7,3},{8,12},{9,13},{10,... | collective-permute-start | bytes 61448 | tf_op jit(solution)/shard_map/ppermute | solution.py:492
  36.5 3.8 %collective-permute-start.7 = (bf16[32,320]{1,0:T(8,128)(2,1)S(1)}, bf16[32,320]{1,0:T(8,128)(2,1)S(1)}, u32[]{:S(2)}, u32[]{:S(2)}) collective-permute-start(bf16[32,320]{1,0:T(8,128)(2,1)S(1)} %pad_maximum_fusion.12), channel_id=1, source_target_pairs={{0,6},{1,7},{2,0},{3,1},{4,2},{5,3},{6,4},{7,5},{8,14},{9,15},{10,... | collective-permute-start | bytes 61448 | tf_op jit(solution)/shard_map/ppermute | solution.py:492
  40.4 1.3 copy-start.5
  40.4 1.3 collective-permute-start.8
  41.7 0.6 copy-start.7
  53.4 7.8 %collective-permute-start.9 = (f32[17,1024]{1,0:T(8,128)}, f32[17,1024]{1,0:T(8,128)S(1)}, u32[]{:S(2)}, u32[]{:S(2)}) collective-permute-start(f32[17,1024]{1,0:T(8,128)} %get-tuple-element.49.own_ref), channel_id=1, source_target_pairs={{0,8},{8,0},{16,24},{24,16},{32,40},{40,32},{48,56},{56,48},{64,72... | collective-permute-start | bytes 208904 | tf_op jit(solution)/shard_map/ppermute | solution.py:265
  61.2 0.9 copy-start.3
  62.1 8.5 %collective-permute-start.10 = (f32[17,1024]{1,0:T(8,128)S(1)}, f32[17,1024]{1,0:T(8,128)S(1)}, u32[]{:S(2)}, u32[]{:S(2)}) collective-permute-start(f32[17,1024]{1,0:T(8,128)S(1)} %get-tuple-element.50.own_ref), channel_id=1, source_target_pairs={{0,24},{8,16},{16,8},{24,0},{32,56},{40,48},{48,40},{56,32},{64,88... | collective-permute-start | bytes 208904 | tf_op jit(solution)/shard_map/ppermute | solution.py:265
  70.7 7.0 %collective-permute-start.11 = (f32[17,1024]{1,0:T(8,128)S(1)}, f32[17,1024]{1,0:T(8,128)S(1)}, u32[]{:S(2)}, u32[]{:S(2)}) collective-permute-start(f32[17,1024]{1,0:T(8,128)S(1)} %get-tuple-element.52.own_ref), channel_id=1, source_target_pairs={{0,32},{8,40},{16,48},{24,56},{32,0},{40,8},{48,16},{56,24},{64,96... | collective-permute-start | bytes 208904 | tf_op jit(solution)/shard_map/ppermute | solution.py:265
  77.7 6.1 %collective-permute-start.12 = (f32[17,1024]{1,0:T(8,128)S(1)}, f32[17,1024]{1,0:T(8,128)S(1)}, u32[]{:S(2)}, u32[]{:S(2)}) collective-permute-start(f32[17,1024]{1,0:T(8,128)S(1)} %get-tuple-element.54.own_ref), channel_id=1, source_target_pairs={{0,96},{8,104},{16,112},{24,120},{32,64},{40,72},{48,80},{56,88},{... | collective-permute-start | bytes 208904 | tf_op jit(solution)/shard_map/ppermute | solution.py:265
  84.5 0.7 copy-start.4
  95.3 1.0 copy-start.2
  96.3 7.6 %copy-start.10 = (s32[32,2]{0,1:T(2,128)S(1)}, s32[32,2]{0,1:T(2,128)}, u32[]{:S(2)}) copy-start(s32[32,2]{0,1:T(2,128)} %param.27) | copy-start | bytes 772
  96.3 68.8 %slice-start.4 = ((s8[6291456]{0:T(1024)(128)(4,1)}), s8[2097152]{0:T(1024)(128)(4,1)S(1)}, s32[]{:S(2)}) async-start(s8[6291456]{0:T(1024)(128)(4,1)} %bitcast.36), calls=%async_computation.7 | async-start | bytes 4194304
  102.5 1.3 copy-start.1
  103.9 2.8 %collective-permute-start.13 = (bf16[128,4096]{1,0:T(8,128)(2,1)S(1)}, bf16[128,4096]{1,0:T(8,128)(2,1)}, u32[]{:S(2)}, u32[]{:S(2)}) collective-permute-start(bf16[128,4096]{1,0:T(8,128)(2,1)S(1)} %get-tuple-element.63), channel_id=1, source_target_pairs={{0,1},{1,0},{2,3},{3,2},{4,5},{5,4},{6,7},{7,6},{8,9},{9,8},{10,11... | collective-permute-start | bytes 3145736 | tf_op jit(solution)/shard_map/ppermute | solution.py:609
  106.6 8.3 %copy-start.11 = (f32[32,2]{0,1:T(2,128)S(1)}, f32[32,2]{0,1:T(2,128)}, u32[]{:S(2)}) copy-start(f32[32,2]{0,1:T(2,128)} %param.28) | copy-start | bytes 772
  106.6 18.8 %copy-start.6 = (bf16[32,4096]{1,0:T(8,128)(2,1)S(1)}, bf16[32,4096]{1,0:T(8,128)(2,1)}, u32[]{:S(2)}) copy-start(bf16[32,4096]{1,0:T(8,128)(2,1)} %param.26) | copy-start | bytes 786436
  106.7 58.4 %slice-start.2 = ((s8[6291456]{0:T(1024)(128)(4,1)}), s8[4194304]{0:T(1024)(128)(4,1)S(1)}, s32[]{:S(2)}) async-start(s8[6291456]{0:T(1024)(128)(4,1)} %bitcast.30), calls=%async_computation.5 | async-start | bytes 8388608
  109.0 56.1 %slice-start.5 = ((s8[6291456]{0:T(1024)(128)(4,1)}), s8[4194304]{0:T(1024)(128)(4,1)S(1)}, s32[]{:S(2)}) async-start(s8[6291456]{0:T(1024)(128)(4,1)} %bitcast.36), calls=%async_computation.8 | async-start | bytes 8388608
  109.1 9.6 %collective-permute-start.14 = (bf16[32,4096]{1,0:T(8,128)(2,1)S(1)}, bf16[32,4096]{1,0:T(8,128)(2,1)S(1)}, u32[]{:S(2)}, u32[]{:S(2)}) collective-permute-start(bf16[32,4096]{1,0:T(8,128)(2,1)S(1)} %get-tuple-element.100), channel_id=1, source_target_pairs={{0,2},{1,3},{2,4},{3,5},{4,6},{5,7},{6,0},{7,1},{8,10},{9,11},{10,... | collective-permute-start | bytes 786440 | tf_op jit(solution)/shard_map/ppermute | solution.py:492
  110.7 14.8 %collective-permute-start.15 = (bf16[32,4096]{1,0:T(8,128)(2,1)S(1)}, bf16[32,4096]{1,0:T(8,128)(2,1)S(1)}, u32[]{:S(2)}, u32[]{:S(2)}) collective-permute-start(bf16[32,4096]{1,0:T(8,128)(2,1)S(1)} %get-tuple-element.102), channel_id=1, source_target_pairs={{0,4},{1,5},{2,6},{3,7},{4,0},{5,1},{6,2},{7,3},{8,12},{9,13},{10,... | collective-permute-start | bytes 786440 | tf_op jit(solution)/shard_map/ppermute | solution.py:492
  113.5 11.9 %collective-permute-start.16 = (bf16[32,4096]{1,0:T(8,128)(2,1)S(1)}, bf16[32,4096]{1,0:T(8,128)(2,1)S(1)}, u32[]{:S(2)}, u32[]{:S(2)}) collective-permute-start(bf16[32,4096]{1,0:T(8,128)(2,1)S(1)} %get-tuple-element.101), channel_id=1, source_target_pairs={{0,6},{1,7},{2,0},{3,1},{4,2},{5,3},{6,4},{7,5},{8,14},{9,15},{10,... | collective-permute-start | bytes 786440 | tf_op jit(solution)/shard_map/ppermute | solution.py:492
  125.5 39.6 %slice-start = ((s8[6291456]{0:T(1024)(128)(4,1)}), s8[4194304]{0:T(1024)(128)(4,1)S(1)}, s32[]{:S(2)}) async-start(s8[6291456]{0:T(1024)(128)(4,1)} %bitcast.24), calls=%async_computation.3 | async-start | bytes 8388608
  126.1 38.9 %slice-start.3 = ((s8[6291456]{0:T(1024)(128)(4,1)}), s8[2097152]{0:T(1024)(128)(4,1)S(1)}, s32[]{:S(2)}) async-start(s8[6291456]{0:T(1024)(128)(4,1)} %bitcast.30), calls=%async_computation.6 | async-start | bytes 4194304
  140.5 10.4 %collective-permute-start.17 = (bf16[64,4096]{1,0:T(8,128)(2,1)S(1)}, bf16[64,4096]{1,0:T(8,128)(2,1)S(1)}, u32[]{:S(2)}, u32[]{:S(2)}) collective-permute-start(bf16[64,4096]{1,0:T(8,128)(2,1)S(1)} %bitcast.43), channel_id=1, source_target_pairs={{0,32},{32,64},{64,96},{96,0},{8,40},{40,72},{72,104},{104,8},{16,... | collective-permute-start | bytes 1572872 | tf_op jit(solution)/shard_map/ppermute | solution.py:51
  140.7 10.2 %collective-permute-start.19 = (bf16[64,4096]{1,0:T(8,128)(2,1)S(1)}, bf16[64,4096]{1,0:T(8,128)(2,1)S(1)}, u32[]{:S(2)}, u32[]{:S(2)}) collective-permute-start(bf16[64,4096]{1,0:T(8,128)(2,1)S(1)} %bitcast.44), channel_id=1, source_target_pairs={{0,96},{32,0},{64,32},{96,64},{8,104},{40,8},{72,40},{104,72},{16,... | collective-permute-start | bytes 1572872 | tf_op jit(solution)/shard_map/ppermute | solution.py:51
  150.9 10.4 %collective-permute-start.21 = (bf16[32,4096]{1,0:T(8,128)(2,1)S(1)}, bf16[32,4096]{1,0:T(8,128)(2,1)S(1)}, u32[]{:S(2)}, u32[]{:S(2)}) collective-permute-start(bf16[32,4096]{1,0:T(8,128)(2,1)S(1)} %slice.111), channel_id=1, source_target_pairs={{0,32},{32,64},{64,96},{96,0},{8,40},{40,72},{72,104},{104,8},{16,... | collective-permute-start | bytes 786440 | tf_op jit(solution)/shard_map/ppermute | solution.py:51
  151.0 14.1 %slice-start.1 = ((s8[6291456]{0:T(1024)(128)(4,1)}), s8[2097152]{0:T(1024)(128)(4,1)S(1)}, s32[]{:S(2)}) async-start(s8[6291456]{0:T(1024)(128)(4,1)} %bitcast.24), calls=%async_computation.4 | async-start | bytes 4194304
  151.0 10.3 %collective-permute-start.22 = (bf16[32,4096]{1,0:T(8,128)(2,1)S(1)}, bf16[32,4096]{1,0:T(8,128)(2,1)S(1)}, u32[]{:S(2)}, u32[]{:S(2)}) collective-permute-start(bf16[32,4096]{1,0:T(8,128)(2,1)S(1)} %slice.112), channel_id=1, source_target_pairs={{0,96},{32,0},{64,32},{96,64},{8,104},{40,8},{72,40},{104,72},{16,... | collective-permute-start | bytes 786440 | tf_op jit(solution)/shard_map/ppermute | solution.py:51
  154.4 19.2 %collective-permute-start.18 = (bf16[128,4096]{1,0:T(8,128)(2,1)S(1)}, bf16[128,4096]{1,0:T(8,128)(2,1)S(1)}, u32[]{:S(2)}, u32[]{:S(2)}) collective-permute-start(bf16[128,4096]{1,0:T(8,128)(2,1)S(1)} %pad_maximum_fusion.4), channel_id=1, source_target_pairs={{0,8},{8,16},{16,24},{24,0},{32,40},{40,48},{48,56},{56,32},{64,72... | collective-permute-start | bytes 3145736 | tf_op jit(solution)/shard_map/ppermute | solution.py:51
  155.8 17.7 %collective-permute-start.20 = (bf16[64,4096]{1,0:T(8,128)(2,1)S(1)}, bf16[64,4096]{1,0:T(8,128)(2,1)S(1)}, u32[]{:S(2)}, u32[]{:S(2)}) collective-permute-start(bf16[64,4096]{1,0:T(8,128)(2,1)S(1)} %collective-permute-done.19), channel_id=1, source_target_pairs={{0,24},{8,0},{16,8},{24,16},{32,56},{40,32},{48,40},{56,48},{64,88... | collective-permute-start | bytes 1572872 | tf_op jit(solution)/shard_map/ppermute | solution.py:51
  161.4 12.2 %collective-permute-start.23 = (bf16[64,4096]{1,0:T(8,128)(2,1)S(1)}, bf16[64,4096]{1,0:T(8,128)(2,1)S(1)}, u32[]{:S(2)}, u32[]{:S(2)}) collective-permute-start(bf16[64,4096]{1,0:T(8,128)(2,1)S(1)} %pad_maximum_fusion.7), channel_id=1, source_target_pairs={{0,24},{8,0},{16,8},{24,16},{32,56},{40,32},{48,40},{56,48},{64,88... | collective-permute-start | bytes 1572872 | tf_op jit(solution)/shard_map/ppermute | solution.py:51
  161.9 23.7 %collective-permute-start.26 = (bf16[128,4096]{1,0:T(8,128)(2,1)S(1)}, bf16[128,4096]{1,0:T(8,128)(2,1)S(1)}, u32[]{:S(2)}, u32[]{:S(2)}) collective-permute-start(bf16[128,4096]{1,0:T(8,128)(2,1)S(1)} %pad_maximum_fusion.6), channel_id=1, source_target_pairs={{0,8},{8,16},{16,24},{24,0},{32,40},{40,48},{48,56},{56,32},{64,72... | collective-permute-start | bytes 3145736 | tf_op jit(solution)/shard_map/ppermute | solution.py:51
  164.8 24.1 %collective-permute-start.27 = (bf16[128,4096]{1,0:T(8,128)(2,1)S(1)}, bf16[128,4096]{1,0:T(8,128)(2,1)S(1)}, u32[]{:S(2)}, u32[]{:S(2)}) collective-permute-start(bf16[128,4096]{1,0:T(8,128)(2,1)S(1)} %pad_maximum_fusion.4), channel_id=1, source_target_pairs={{0,24},{8,0},{16,8},{24,16},{32,56},{40,32},{48,40},{56,48},{64,88... | collective-permute-start | bytes 3145736 | tf_op jit(solution)/shard_map/ppermute | solution.py:51
  173.7 23.9 %collective-permute-start.24 = (bf16[128,4096]{1,0:T(8,128)(2,1)S(1)}, bf16[128,4096]{1,0:T(8,128)(2,1)S(1)}, u32[]{:S(2)}, u32[]{:S(2)}) collective-permute-start(bf16[128,4096]{1,0:T(8,128)(2,1)S(1)} %collective-permute-done.18), channel_id=1, source_target_pairs={{0,8},{8,16},{16,24},{24,0},{32,40},{40,48},{48,56},{56,32},{64,72... | collective-permute-start | bytes 3145736 | tf_op jit(solution)/shard_map/ppermute | solution.py:51
  177.0 20.6 %collective-permute-start.25 = (bf16[128,4096]{1,0:T(8,128)(2,1)S(1)}, bf16[128,4096]{1,0:T(8,128)(2,1)S(1)}, u32[]{:S(2)}, u32[]{:S(2)}) collective-permute-start(bf16[128,4096]{1,0:T(8,128)(2,1)S(1)} %pad_maximum_fusion.5), channel_id=1, source_target_pairs={{0,24},{8,0},{16,8},{24,16},{32,56},{40,32},{48,40},{56,48},{64,88... | collective-permute-start | bytes 3145736 | tf_op jit(solution)/shard_map/ppermute | solution.py:51
  185.6 20.6 %collective-permute-start.28 = (bf16[128,4096]{1,0:T(8,128)(2,1)S(1)}, bf16[128,4096]{1,0:T(8,128)(2,1)S(1)}, u32[]{:S(2)}, u32[]{:S(2)}) collective-permute-start(bf16[128,4096]{1,0:T(8,128)(2,1)S(1)} %get-tuple-element.71), channel_id=1, source_target_pairs={{0,24},{8,0},{16,8},{24,16},{32,56},{40,32},{48,40},{56,48},{64,88... | collective-permute-start | bytes 3145736 | tf_op jit(solution)/shard_map/ppermute | solution.py:51
  185.7 20.5 %collective-permute-start.29 = (bf16[128,4096]{1,0:T(8,128)(2,1)S(1)}, bf16[128,4096]{1,0:T(8,128)(2,1)S(1)}, u32[]{:S(2)}, u32[]{:S(2)}) collective-permute-start(bf16[128,4096]{1,0:T(8,128)(2,1)S(1)} %get-tuple-element.79), channel_id=1, source_target_pairs={{0,8},{8,16},{16,24},{24,0},{32,40},{40,48},{48,56},{56,32},{64,72... | collective-permute-start | bytes 3145736 | tf_op jit(solution)/shard_map/ppermute | solution.py:51
  206.2 16.1 %collective-permute-start.32 = (bf16[128,4096]{1,0:T(8,128)(2,1)S(1)}, bf16[128,4096]{1,0:T(8,128)(2,1)S(1)}, u32[]{:S(2)}, u32[]{:S(2)}) collective-permute-start(bf16[128,4096]{1,0:T(8,128)(2,1)S(1)} %get-tuple-element.86), channel_id=1, source_target_pairs={{0,24},{8,0},{16,8},{24,16},{32,56},{40,32},{48,40},{56,48},{64,88... | collective-permute-start | bytes 3145736 | tf_op jit(solution)/shard_map/ppermute | solution.py:51
  206.3 16.3 %collective-permute-start.30 = (bf16[128,4096]{1,0:T(8,128)(2,1)S(1)}, bf16[128,4096]{1,0:T(8,128)(2,1)S(1)}, u32[]{:S(2)}, u32[]{:S(2)}) collective-permute-start(bf16[128,4096]{1,0:T(8,128)(2,1)S(1)} %get-tuple-element.82), channel_id=1, source_target_pairs={{0,8},{8,16},{16,24},{24,0},{32,40},{40,48},{48,56},{56,32},{64,72... | collective-permute-start | bytes 3145736 | tf_op jit(solution)/shard_map/ppermute | solution.py:51
  222.5 16.1 %collective-permute-start.33 = (bf16[128,4096]{1,0:T(8,128)(2,1)S(1)}, bf16[128,4096]{1,0:T(8,128)(2,1)S(1)}, u32[]{:S(2)}, u32[]{:S(2)}) collective-permute-start(bf16[128,4096]{1,0:T(8,128)(2,1)S(1)} %add_convert_fusion.1), channel_id=1, source_target_pairs={{0,24},{8,0},{16,8},{24,16},{32,56},{40,32},{48,40},{56,48},{64,88... | collective-permute-start | bytes 3145736 | tf_op jit(solution)/shard_map/ppermute | solution.py:51
  222.9 19.8 %collective-permute-start.31 = (bf16[128,4096]{1,0:T(8,128)(2,1)S(1)}, bf16[128,4096]{1,0:T(8,128)(2,1)S(1)}, u32[]{:S(2)}, u32[]{:S(2)}) collective-permute-start(bf16[128,4096]{1,0:T(8,128)(2,1)S(1)} %add_convert_fusion.3), channel_id=1, source_target_pairs={{0,8},{8,16},{16,24},{24,0},{32,40},{40,48},{48,56},{56,32},{64,72... | collective-permute-start | bytes 3145736 | tf_op jit(solution)/shard_map/ppermute | solution.py:51
  239.1 7.8 %collective-permute-start.34 = (bf16[32,4096]{1,0:T(8,128)(2,1)S(1)}, bf16[32,4096]{1,0:T(8,128)(2,1)S(1)}, u32[]{:S(2)}, u32[]{:S(2)}) collective-permute-start(bf16[32,4096]{1,0:T(8,128)(2,1)S(1)} %get-tuple-element.97), channel_id=1, source_target_pairs={{0,32},{32,64},{64,96},{96,0},{8,40},{40,72},{72,104},{104,8},{16,... | collective-permute-start | bytes 786440 | tf_op jit(solution)/shard_map/ppermute | solution.py:51
  239.2 7.9 %collective-permute-start.36 = (bf16[32,4096]{1,0:T(8,128)(2,1)S(1)}, bf16[32,4096]{1,0:T(8,128)(2,1)S(1)}, u32[]{:S(2)}, u32[]{:S(2)}) collective-permute-start(bf16[32,4096]{1,0:T(8,128)(2,1)S(1)} %get-tuple-element.98), channel_id=1, source_target_pairs={{0,96},{32,0},{64,32},{96,64},{8,104},{40,8},{72,40},{104,72},{16,... | collective-permute-start | bytes 786440 | tf_op jit(solution)/shard_map/ppermute | solution.py:51
  247.0 10.5 %collective-permute-start.35 = (bf16[64,4096]{1,0:T(8,128)(2,1)S(1)}, bf16[64,4096]{1,0:T(8,128)(2,1)S(1)}, u32[]{:S(2)}, u32[]{:S(2)}) collective-permute-start(bf16[64,4096]{1,0:T(8,128)(2,1)S(1)} %pad_maximum_fusion.8), channel_id=1, source_target_pairs={{0,32},{32,64},{64,96},{96,0},{8,40},{40,72},{72,104},{104,8},{16,... | collective-permute-start | bytes 1572872 | tf_op jit(solution)/shard_map/ppermute | solution.py:51
  247.3 10.3 %collective-permute-start.37 = (bf16[64,4096]{1,0:T(8,128)(2,1)S(1)}, bf16[64,4096]{1,0:T(8,128)(2,1)S(1)}, u32[]{:S(2)}, u32[]{:S(2)}) collective-permute-start(bf16[64,4096]{1,0:T(8,128)(2,1)S(1)} %pad_maximum_fusion.9), channel_id=1, source_target_pairs={{0,96},{32,0},{64,32},{96,64},{8,104},{40,8},{72,40},{104,72},{16,... | collective-permute-start | bytes 1572872 | tf_op jit(solution)/shard_map/ppermute | solution.py:51
Sparse Core Ops, SparseCore 0:
  9.5 73.9 all-gather.2

commit v6 on v5

--- a/solution.py
+++ b/solution.py
@@ -132,16 +132,16 @@
     bias_hbm,
     packed_ref,
     msg_ref,
-    y_hbm,
-    delta_hbm,
+    y_ref,
+    delta_ref,
     before_hbm,
     enter_hbm,
     b_wide,
     c_wide,
     proj_ref,
     bias_ref,
-    y_ref,
-    delta_ref,
+    ends_ref,
+    deltas_ref,
     before_ref,
     enter_ref,
     in_sems,
@@ -208,9 +208,11 @@
                 state = decay * shifted(state, by, 0.0) + state
                 decay = decay * shifted(decay, by, 1.0)
             enter_ref[n, :, lanes] = shifted(state, 1, 0.0)
-            msg_ref[n : n + 1, lanes] = state[SEG - 1 : SEG, :]
-        msg_ref[STATE : STATE + 1, lanes] = last
+            ends_ref[n : n + 1, lanes] = state[SEG - 1 : SEG, :]
         block = lane // LANES
+        high = last.astype(BF16).astype(F32)
+        deltas_ref[block : block + 1, :] = high
+        deltas_ref[SEG + block : SEG + block + 1, :] = last - high
         fresh = [
             pltpu.make_async_copy(
                 before_ref.at[:, lanes], before_hbm.at[:, lanes], out_sems.at[0, block]
@@ -218,87 +220,95 @@
             pltpu.make_async_copy(
                 enter_ref.at[:, :, lanes], enter_hbm.at[:, :, lanes], out_sems.at[1, block]
             ),
-            pltpu.make_async_copy(y_ref.at[:, lanes], y_hbm.at[:, lanes], out_sems.at[2, block]),
-            pltpu.make_async_copy(
-                delta_ref.at[:, lanes], delta_hbm.at[:, lanes], out_sems.at[3, block]
-            ),
         ]
         for copy in fresh:
             copy.start()
         copies += fresh
+    msg_ref[:, :channels] = ends_ref[...].astype(BF16)
+    msg_ref[:, channels:] = deltas_ref[...].astype(BF16)
     for copy in copies:
         copy.wait()
 
 
-def meet_kernel(before_ref, own_ref, got_ref, prefix_ref, rates_ref, total_ref, next_ref):
-    partner_first = before_ref[0] > 0
-    rates = rates_ref[...]
-    own, got = own_ref[:STATE, :], got_ref[:STATE, :]
-    own_delta, got_delta = own_ref[STATE : STATE + 1, :], got_ref[STATE : STATE + 1, :]
-    prefix, prefix_delta = prefix_ref[:STATE, :], prefix_ref[STATE : STATE + 1, :]
-    late_delta = jnp.where(partner_first, own_delta, got_delta)
-    early = jnp.where(partner_first, got, own)
-    late = jnp.where(partner_first, own, got)
-    total_ref[:STATE, :] = jnp.exp2(late_delta * rates) * early + late
-    total_ref[STATE : STATE + 1, :] = own_delta + got_delta
-    joined = jnp.exp2(prefix_delta * rates) * got + prefix
-    next_ref[:STATE, :] = jnp.where(partner_first, joined, prefix)
-    next_ref[STATE : STATE + 1, :] = jnp.where(partner_first, prefix_delta + got_delta, prefix_delta)
-
-
-def entering_state(message, rates):
+def unpacked(message, block):
+    lanes = slice(block * LANES, (block + 1) * LANES)
+    tail = message[:, message.shape[1] - LANES :].astype(F32)
+    delta = tail[block : block + 1] + tail[SEG + block : SEG + block + 1]
+    return message[:, lanes].astype(F32), delta
+
+
+def joined(run, later, rates, chosen):
+    state, delta = run
+    more, more_delta = later
+    state = jnp.where(chosen, jnp.exp2(more_delta * rates) * state + more, state)
+    return state, jnp.where(chosen, delta + more_delta, delta)
+
+
+def meet_kernel(place_ref, own_ref, third_ref, second_ref, first_ref, rates_ref, msg_ref, prefix_ref):
+    place = place_ref[0]
+    channels = rates_ref.shape[1]
+    for block in range(channels // LANES):
+        lanes = slice(block * LANES, (block + 1) * LANES)
+        rates = rates_ref[:, lanes]
+        others = [
+            (hops, unpacked(ref[...], block))
+            for hops, ref in ((3, third_ref), (2, second_ref), (1, first_ref))
+        ]
+        run = (jnp.zeros((STATE, LANES), F32), jnp.zeros((1, LANES), F32))
+        for hops, message in others:
+            run = joined(run, message, rates, hops <= place)
+        prefix_ref[:STATE, lanes] = run[0]
+        prefix_ref[STATE : STATE + 1, lanes] = run[1]
+        run = joined(run, unpacked(own_ref[...], block), rates, place >= 0)
+        for hops, message in others:
+            run = joined(run, message, rates, hops > place)
+        state, delta = run
+        high = delta.astype(BF16).astype(F32)
+        msg_ref[:STATE, lanes] = state
+        msg_ref[block : block + 1, channels:] = high
+        msg_ref[SEG + block : SEG + block + 1, channels:] = delta - high
+
+
+def ringed(message, axis):
     seqs = lax.axis_size("seq")
     side = math.isqrt(seqs)
-    place = lax.axis_index("seq").astype(jnp.int32)
-    shape = jax.ShapeDtypeStruct(message.shape, F32)
-    prefix = jnp.zeros(message.shape, F32)
-
-    def flipped(index, axis, far_step):
-        x, y = index // side, index % side
-        value = x if axis == "x" else y
-        value = side - 1 - value if far_step else value + 1 - 2 * (value % 2)
-        return value * side + y if axis == "x" else x * side + value
-
-    for axis in ("y", "x"):
-        for far_step in (False, True):
-            route = [(i, flipped(i, axis, far_step)) for i in range(seqs)]
-            got = lax.ppermute(message, "seq", route)
-            before = (flipped(place, axis, far_step) < place).astype(jnp.int32).reshape(1)
-            message, prefix = pl.pallas_call(
-                meet_kernel,
-                out_shape=(shape, shape),
-                in_specs=[pl.BlockSpec(memory_space=pltpu.SMEM)] + [whole()] * 4,
-                out_specs=[whole()] * 2,
-                compiler_params=params(4),
-                name="meet",
-            )(before, message, got, prefix, rates)
-    return prefix
+    got = []
+    for hops in range(1, side):
+        route = []
+        for i in range(seqs):
+            x, y = i // side, i % side
+            target = ((x + hops) % side, y) if axis == "x" else (x, (y + hops) % side)
+            route.append((i, target[0] * side + target[1]))
+        got.append(lax.ppermute(message, "seq", route))
+    return got[::-1]
 
 
 def finish_kernel(
     order_ref,
-    entering_ref,
+    place_ref,
+    prefix_ref,
+    third_ref,
+    second_ref,
+    first_ref,
     rates_ref,
+    delta_ref,
     packed_ref,
+    y_ref,
     mixed_ref,
     before_hbm,
     enter_hbm,
     skip_hbm,
     z_hbm,
-    y_hbm,
-    delta_hbm,
     gated_ref,
     before_ref,
     enter_ref,
     skip_ref,
     z_ref,
-    y_ref,
-    delta_ref,
     c_wide,
     z_wide,
     gated,
+    entering_ref,
     sems,
-    block_sems,
 ):
     length, channels = mixed_ref.shape
     steps = length // SEG
@@ -307,17 +317,14 @@
     copies = [pltpu.make_async_copy(*pair, sems.at[k]) for k, pair in enumerate(zip(sources, targets))]
     for copy in copies:
         copy.start()
-    blocks = []
-    for lane in range(0, channels, LANES):
-        lanes = pl.ds(lane, LANES)
-        y_sem, delta_sem = block_sems.at[0, lane // LANES], block_sems.at[1, lane // LANES]
-        pair = (
-            pltpu.make_async_copy(y_hbm.at[:, lanes], y_ref.at[:, lanes], y_sem),
-            pltpu.make_async_copy(delta_hbm.at[:, lanes], delta_ref.at[:, lanes], delta_sem),
-        )
-        for copy in pair:
-            copy.start()
-        blocks.append(pair)
+    for block in range(channels // LANES):
+        lanes = slice(block * LANES, (block + 1) * LANES)
+        rates = rates_ref[:, lanes]
+        run = (jnp.zeros((STATE, LANES), F32), jnp.zeros((1, LANES), F32))
+        for hops, ref in ((3, third_ref), (2, second_ref), (1, first_ref)):
+            run = joined(run, unpacked(ref[...], block), rates, hops <= place_ref[0])
+        near = (prefix_ref[:STATE, lanes], prefix_ref[STATE : STATE + 1, lanes])
+        entering_ref[:, lanes] = joined(run, near, rates, place_ref[0] >= 0)[0]
     spread(c_wide, packed_ref, STATE)
     for copy in copies:
         copy.wait()
@@ -329,8 +336,6 @@
         rates = [
             jnp.broadcast_to(rates_ref[n : n + 1, lanes], (SEG, LANES)) for n in range(STATE)
         ]
-        for copy in blocks[lane // LANES]:
-            copy.wait()
         before = before_ref[:, lanes]
         held = [
             jnp.exp2(before * rates[n]) * entering_ref[n : n + 1, lanes] + enter_ref[n, :, lanes]
@@ -515,7 +520,7 @@
             pltpu.VMEM((length, RANK + 2 * STATE), F32),
             pltpu.SemaphoreType.DMA((2,)),
         ],
-        compiler_params=params(59),
+        compiler_params=params(12),
         name="conv",
     )(order, x_in, x_proj.T, jnp.concatenate([conv_weight, conv_bias[None, :]], axis=0), rim)
     sums = (keep + lax.ppermute(send, "exp", swap)).reshape(side, length // owners, -1)
@@ -532,62 +537,75 @@
         scan_kernel,
         out_shape=(
             jax.ShapeDtypeStruct((length, RANK + 4 * STATE), BF16),
-            jax.ShapeDtypeStruct((STATE + 1, channels), F32),
+            jax.ShapeDtypeStruct((STATE, channels + LANES), BF16),
             jax.ShapeDtypeStruct((length, channels), F32),
             jax.ShapeDtypeStruct((length, channels), F32),
             jax.ShapeDtypeStruct((SEG, channels), F32),
             jax.ShapeDtypeStruct((STATE, SEG, channels), F32),
         ),
         in_specs=[pl.BlockSpec(memory_space=pltpu.SMEM)] + [whole()] * 4 + [far()] * 2,
-        out_specs=[whole()] * 2 + [far()] * 4,
+        out_specs=[whole()] * 4 + [far()] * 2,
         scratch_shapes=[
             pltpu.VMEM((STATE, length, LANES), F32),
             pltpu.VMEM((STATE, length, LANES), F32),
             pltpu.VMEM(dt_proj.shape, BF16),
             pltpu.VMEM((1, channels), F32),
-            pltpu.VMEM((length, channels), F32),
-            pltpu.VMEM((length, channels), F32),
+            pltpu.VMEM((STATE, channels), F32),
+            pltpu.VMEM((STATE, LANES), F32),
             pltpu.VMEM((SEG, channels), F32),
             pltpu.VMEM((STATE, SEG, channels), F32),
             pltpu.SemaphoreType.DMA((2,)),
-            pltpu.SemaphoreType.DMA((4, channels // LANES)),
+            pltpu.SemaphoreType.DMA((2, channels // LANES)),
         ],
-        compiler_params=params(58),
+        compiler_params=params(14),
         name="scan",
     )(arrival, near, other, mixed, rates, dt_proj, dt_bias[None, :])
-    entering = entering_state(message, rates)
+    place = lax.axis_index("seq").astype(jnp.int32).reshape(1)
+    grid_side = math.isqrt(seqs)
+    totals, prefix = pl.pallas_call(
+        meet_kernel,
+        out_shape=(
+            jax.ShapeDtypeStruct((STATE, channels + LANES), F32),
+            jax.ShapeDtypeStruct((STATE + 1, channels), F32),
+        ),
+        in_specs=[pl.BlockSpec(memory_space=pltpu.SMEM)] + [whole()] * 5,
+        out_specs=[whole()] * 2,
+        compiler_params=params(4),
+        name="meet",
+    )(place % grid_side, message, *ringed(message, "y"), rates)
+    lines_before = ringed(totals.astype(BF16), "x")
     gated = pl.pallas_call(
         finish_kernel,
         out_shape=jax.ShapeDtypeStruct((length, channels), BF16),
-        in_specs=[pl.BlockSpec(memory_space=pltpu.SMEM)] + [whole()] * 4 + [far()] * 6,
+        in_specs=[pl.BlockSpec(memory_space=pltpu.SMEM)] * 2 + [whole()] * 9 + [far()] * 4,
         out_specs=whole(),
         scratch_shapes=[
             pltpu.VMEM((SEG, channels), F32),
             pltpu.VMEM((STATE, SEG, channels), F32),
             pltpu.VMEM((1, channels), F32),
             pltpu.VMEM((length, channels), BF16),
-            pltpu.VMEM((length, channels), F32),
-            pltpu.VMEM((length, channels), F32),
             pltpu.VMEM((STATE, length, LANES), F32),
             pltpu.VMEM((channels // LANES, length, LANES), F32),
             pltpu.VMEM((channels // LANES, length, LANES), F32),
+            pltpu.VMEM((STATE, channels), F32),
             pltpu.SemaphoreType.DMA((4,)),
-            pltpu.SemaphoreType.DMA((2, channels // LANES)),
         ],
-        compiler_params=params(58),
+        compiler_params=params(16),
         name="finish",
     )(
         order,
-        entering,
+        place // grid_side,
+        prefix,
+        *lines_before,
         rates,
+        delta,
         packed,
+        y_local,
         mixed,
         before,
         enter,
         d_skip[None, :],
         z_in,
-        y_local,
-        delta,
     )
     width = out_proj.shape[1]
     features = seqs * width

time: 280 us -> 268 us (0.957)
  waiting for transfers between devices: 93.3 us -> 85.3 us
  Pallas kernels: 67.7 us -> 60.8 us
  local copies, waits for them, and re-layouts: 6.67 us -> 11.2 us
  other arithmetic: 10.4 us -> 6.95 us
    ppermute x4 -> x6, waiting for transfers between devices: 23.9 us -> 11.2 us  [ringed(): got.append(lax.ppermute(message, 'seq', route))]
    unnamed x37 -> x47, local copies, waits for them, and re-layouts: 5.27 us -> 9.83 us
    pallas_call x1, Pallas kernels: 10 us -> 7.01 us  [mixer(): pl.pallas_call(finish_kernel, out_shape=jax.ShapeDtypeStruct((length, cha...]
    ppermute x4 -> x6, starting transfers between devices: 5.54 us -> 7.93 us  [ringed(): got.append(lax.ppermute(message, 'seq', route))]
  transfers between devices with their start and end apart: 39 -> 41, of which waited for: 21 -> 23; matrix products, arithmetic and copies ran while one was open for 3% -> 2% of each run, Pallas kernels for 22% -> 20%
where the time goes in v6:
time: 268 us; the launch traced here: 267 us
  waiting for transfers between devices  85.3 us (32%)
  Pallas kernels  60.8 us (23%)
  starting transfers between devices  60.1 us (22%)
  blocking collectives  27.1 us (10%)
  between operations  14.1 us (5%)
  local copies, waits for them, and re-layouts  11.2 us (4%)
  other arithmetic  6.95 us (3%)
    ppermute x21, waiting for transfers between devices, along(): return lax.ppermute(block, ('seq', 'exp'), route)  48.1 us
    pallas_call x4, Pallas kernels, expert(): pl.pallas_call(expert_kernel, out_shape=(jax.ShapeDtypeStruct((count // 2...  33.5 us
    ppermute x21, starting transfers between devices, along(): return lax.ppermute(block, ('seq', 'exp'), route)  32.4 us
    ppermute x9, waiting for transfers between devices, along_z(): lax.ppermute(block, 'exp', [(e, (e + 2 * hop) % owners) for e in range(ow...  16.9 us
    ppermute x9, starting transfers between devices, along_z(): lax.ppermute(block, 'exp', [(e, (e + 2 * hop) % owners) for e in range(ow...  16.6 us
    all_to_all x1, blocking collectives, shards(): lax.all_to_all(outgoing, 'exp', split_axis=0, concat_axis=0, tiled=True)  14.3 us
    all_to_all x1, blocking collectives, shards(): lax.all_to_all(expert_out, 'exp', split_axis=0, concat_axis=0, tiled=True)  12.8 us
    ppermute x6, waiting for transfers between devices, ringed(): got.append(lax.ppermute(message, 'seq', route))  11.2 us
  transfers between devices with their start and end apart: 41, of which 23 were waited for; matrix products, arithmetic and copies ran while one was open for 2% of the time, Pallas kernels for 20%

profile of v6, /device:TPU:24, one launch (start us, length us, event | category | flops | bytes accessed | tf_op | source)
XLA Modules:
  0.0 267.0 jit_solution(18222530071434283940)
XLA Ops:
  8.0 3.0 %collective-permute-start = (bf16[3,1024]{1,0:T(4,128)(2,1)S(1)}, bf16[3,1024]{1,0:T(4,128)(2,1)S(1)}, u32[]{:S(2)}, u32[]{:S(2)}) collective-permute-start(bf16[3,1024]{1,0:T(4,128)(2,1)S(1)} %slice.81), channel_id=1, source_target_pairs={{0,8},{8,16},{16,24},{24,32},{32,40},{40,48},{48,56},{56,64},{64,7... | collective-permute-start | bytes 18440 | tf_op jit(solution)/shard_map/ppermute | solution.py:57
  11.9 1.6 collective-permute-done.rim_ref
  13.5 1.1 copy-done.5
  14.6 1.0 copy-done.6
  15.6 4.3 %conv.1 = (f32[256,1024]{1,0:T(8,128)S(1)}, f32[128,288]{1,0:T(8,128)S(1)}, f32[128,288]{1,0:T(8,128)S(1)}) custom-call(s32[8]{0:T(128)S(1)} %pad_add_fusion.order_ref, bf16[256,1024]{1,0:T(8,128)(2,1)S(1)} %copy-done.6, bf16[288,1024]{1,0:T(8,128)(2,1)S(1)} %bitcast.39, f32[5,1024]{1,0:T(8,128)S(1)} %pad_maximum_fusion.11.weight_ref, ...), custom_call_target="tpu_custom_call" | custom-call | tf_op jit(solution)/shard_map/conv/pallas_call | solution.py:507
  20.1 1.4 collective-permute-done.1
  21.6 2.0 collective-permute-start.2
  23.5 3.6 %collective-permute-start.3 = (f32[32,288]{1,0:T(8,128)S(1)}, f32[32,288]{1,0:T(8,128)S(1)}, u32[]{:S(2)}, u32[]{:S(2)}) collective-permute-start(f32[32,288]{1,0:T(8,128)S(1)} %get-tuple-element.95), channel_id=1, source_target_pairs={{0,4},{1,5},{2,6},{3,7},{4,0},{5,1},{6,2},{7,3},{8,12},{9,13},{10,... | collective-permute-start | bytes 110600 | tf_op jit(solution)/shard_map/ppermute | solution.py:497
  27.1 1.0 collective-permute-start.4
  28.2 1.8 collective-permute-done.3
  29.9 1.3 collective-permute-done.4
  31.4 3.7 %collective-permute-start.6 = (bf16[32,320]{1,0:T(8,128)(2,1)S(1)}, bf16[32,320]{1,0:T(8,128)(2,1)S(1)}, u32[]{:S(2)}, u32[]{:S(2)}) collective-permute-start(bf16[32,320]{1,0:T(8,128)(2,1)S(1)} %pad_maximum_fusion.12), channel_id=1, source_target_pairs={{0,4},{1,5},{2,6},{3,7},{4,0},{5,1},{6,2},{7,3},{8,12},{9,13},{10,... | collective-permute-start | bytes 61448 | tf_op jit(solution)/shard_map/ppermute | solution.py:497
  35.5 0.9 collective-permute-done.5
  37.1 1.8 collective-permute-done.7
  39.0 1.2 collective-permute-done.8.other_ref
  40.3 8.7 %scan.1 = (bf16[256,320]{1,0:T(8,128)(2,1)S(1)}, bf16[16,1152]{1,0:T(8,128)(2,1)S(1)}, f32[256,1024]{1,0:T(8,128)S(1)}, f32[256,1024]{1,0:T(8,128)S(1)}, f32[8,1...) custom-call(s32[8]{0:T(128)S(1)} %pad_add_fusion.1.order_ref, bf16[128,320]{1,0:T(8,128)(2,1)S(1)} %pad_maximum_fusion.10.near_ref, ...), custom_call_target="tpu_custom_call" | custom-call | tf_op jit(solution)/shard_map/scan/pallas_call | solution.py:536
  49.0 1.0 copy-done.1
  50.0 1.0 copy-done.3
  51.7 1.2 collective-permute-start.10
  53.0 2.2 collective-permute-start.11
  55.2 3.1 %collective-permute-done.10.second_ref = bf16[16,1152]{1,0:T(8,128)(2,1)S(1)} collective-permute-done((bf16[16,1152]{1,0:T(8,128)(2,1)S(1)}, bf16[16,1152]{1,0:T(8,128)(2,1)S(1)}, u32[]{:S(2)}, u32[]{:S(2)}) %collective-permute-start.10) | collective-permute-done | bytes 36896 | tf_op jit(solution)/shard_map/ppermute | solution.py:282
  58.3 2.8 %collective-permute-done.9.third_ref = bf16[16,1152]{1,0:T(8,128)(2,1)S(1)} collective-permute-done((bf16[16,1152]{1,0:T(8,128)(2,1)S(1)}, bf16[16,1152]{1,0:T(8,128)(2,1)S(1)}, u32[]{:S(2)}, u32[]{:S(2)}) %collective-permute-start.9) | collective-permute-done | bytes 36896 | tf_op jit(solution)/shard_map/ppermute | solution.py:282
  61.2 2.8 %collective-permute-start.12 = (bf16[16,1152]{1,0:T(8,128)(2,1)S(1)}, bf16[16,1152]{1,0:T(8,128)(2,1)S(1)}, u32[]{:S(2)}, u32[]{:S(2)}) collective-permute-start(bf16[16,1152]{1,0:T(8,128)(2,1)S(1)} %convert_element_type.124), channel_id=1, source_target_pairs={{0,96},{8,104},{16,112},{24,120},{32,0},{40,8},{48,16},{56,24},{64... | collective-permute-start | bytes 110600 | tf_op jit(solution)/shard_map/ppermute | solution.py:282
  64.0 0.8 collective-permute-start.13
  64.8 0.9 collective-permute-start.14
  66.4 3.9 %collective-permute-done.13.second_ref = bf16[16,1152]{1,0:T(8,128)(2,1)S(1)} collective-permute-done((bf16[16,1152]{1,0:T(8,128)(2,1)S(1)}, bf16[16,1152]{1,0:T(8,128)(2,1)S(1)}, u32[]{:S(2)}, u32[]{:S(2)}) %collective-permute-start.13) | collective-permute-done | bytes 36896 | tf_op jit(solution)/shard_map/ppermute | solution.py:282
  71.0 1.2 copy-done.2
  72.2 1.2 copy-done.4
  73.5 1.1 copy-done.10
  74.5 7.0 %finish.1.gated_ref = bf16[256,1024]{1,0:T(8,128)(2,1)S(1)} custom-call(s32[8]{0:T(128)S(1)} %pad_add_fusion.order_ref, s32[1]{0:T(128)S(6)} %select_n.35.place_ref, f32[17,1024]{1,0:T(8,128)S(1)} %get-tuple-element.45.prefix_ref, bf16[16,1152]{1,0:T(8,128)(2,1)S(1)} %collective-permute-done.12.third_ref, ...), custom_call_target="tpu_custom_call" | custom-call | tf_op jit(solution)/shard_map/finish/pallas_call | solution.py:577
  81.5 2.2 all-gather.3.cloned.1.call-done
  83.8 7.1 %outward.1 = (bf16[128,4096]{1,0:T(8,128)(2,1)}, f32[128,4096]{1,0:T(8,128)S(1)}) custom-call(bf16[256,1024]{1,0:T(8,128)(2,1)S(1)} %finish.1.gated_ref, bf16[16,1024,256]{2,1,0:T(8,128)(2,1)} %bitcast.42), custom_call_target="tpu_custom_call" | custom-call | tf_op jit(solution)/shard_map/outward/pallas_call | solution.py:612
  90.9 1.3 copy-done
  93.2 1.9 collective-permute-done.15
  95.1 2.1 fusion.18
  97.3 1.6 collective-permute-start.16
  98.9 2.9 %collective-permute-start.17 = (bf16[32,4096]{1,0:T(8,128)(2,1)S(1)}, bf16[32,4096]{1,0:T(8,128)(2,1)S(1)}, u32[]{:S(2)}, u32[]{:S(2)}) collective-permute-start(bf16[32,4096]{1,0:T(8,128)(2,1)S(1)} %get-tuple-element.92), channel_id=1, source_target_pairs={{0,4},{1,5},{2,6},{3,7},{4,0},{5,1},{6,2},{7,3},{8,12},{9,13},{10,... | collective-permute-start | bytes 786440 | tf_op jit(solution)/shard_map/ppermute | solution.py:497
  101.8 1.4 collective-permute-start.18
  103.2 3.7 %collective-permute-done.16 = bf16[32,4096]{1,0:T(8,128)(2,1)S(1)} collective-permute-done((bf16[32,4096]{1,0:T(8,128)(2,1)S(1)}, bf16[32,4096]{1,0:T(8,128)(2,1)S(1)}, u32[]{:S(2)}, u32[]{:S(2)}) %collective-permute-start.16) | collective-permute-done | bytes 262176 | tf_op jit(solution)/shard_map/ppermute | solution.py:497
  106.9 6.8 %collective-permute-done.17 = bf16[32,4096]{1,0:T(8,128)(2,1)S(1)} collective-permute-done((bf16[32,4096]{1,0:T(8,128)(2,1)S(1)}, bf16[32,4096]{1,0:T(8,128)(2,1)S(1)}, u32[]{:S(2)}, u32[]{:S(2)}) %collective-permute-start.17) | collective-permute-done | bytes 262176 | tf_op jit(solution)/shard_map/ppermute | solution.py:497
  114.4 14.3 %all_to_all.10 = bf16[8,8,4096]{2,1,0:T(8,128)(2,1)S(1)} all-to-all(bf16[8,8,4096]{2,1,0:T(8,128)(2,1)S(1)} %fusion), channel_id=1, replica_groups=mesh['seq'=16,'exp'=8] {'exp'}, dimensions={0} | all-to-all | bytes 1048576 | tf_op jit(solution)/shard_map/all_to_all | solution.py:682
  129.0 3.0 %collective-permute-start.21 = (bf16[64,4096]{1,0:T(8,128)(2,1)S(1)}, bf16[64,4096]{1,0:T(8,128)(2,1)S(1)}, u32[]{:S(2)}, u32[]{:S(2)}) collective-permute-start(bf16[64,4096]{1,0:T(8,128)(2,1)S(1)} %bitcast.44), channel_id=1, source_target_pairs={{0,96},{32,0},{64,32},{96,64},{8,104},{40,8},{72,40},{104,72},{16,... | collective-permute-start | bytes 1572872 | tf_op jit(solution)/shard_map/ppermute | solution.py:51
  132.0 7.2 %collective-permute-done.19 = bf16[64,4096]{1,0:T(8,128)(2,1)S(1)} collective-permute-done((bf16[64,4096]{1,0:T(8,128)(2,1)S(1)}, bf16[64,4096]{1,0:T(8,128)(2,1)S(1)}, u32[]{:S(2)}, u32[]{:S(2)}) %collective-permute-start.19) | collective-permute-done | bytes 524320 | tf_op jit(solution)/shard_map/ppermute | solution.py:51
  139.3 3.3 %collective-permute-start.24 = (bf16[32,4096]{1,0:T(8,128)(2,1)S(1)}, bf16[32,4096]{1,0:T(8,128)(2,1)S(1)}, u32[]{:S(2)}, u32[]{:S(2)}) collective-permute-start(bf16[32,4096]{1,0:T(8,128)(2,1)S(1)} %slice.112), channel_id=1, source_target_pairs={{0,96},{32,0},{64,32},{96,64},{8,104},{40,8},{72,40},{104,72},{16,... | collective-permute-start | bytes 786440 | tf_op jit(solution)/shard_map/ppermute | solution.py:51
  143.3 1.5 collective-permute-start.22
  144.7 4.9 %collective-permute-done.23 = bf16[32,4096]{1,0:T(8,128)(2,1)S(1)} collective-permute-done((bf16[32,4096]{1,0:T(8,128)(2,1)S(1)}, bf16[32,4096]{1,0:T(8,128)(2,1)S(1)}, u32[]{:S(2)}, u32[]{:S(2)}) %collective-permute-start.23) | collective-permute-done | bytes 262176 | tf_op jit(solution)/shard_map/ppermute | solution.py:51
  149.7 0.9 collective-permute-start.25
  150.7 2.5 collective-permute-start.28
  153.5 8.4 %expert.4 = (bf16[128,4096]{1,0:T(8,128)(2,1)S(1)}, bf16[128,4096]{1,0:T(8,128)(2,1)S(1)}) custom-call(bf16[256,4096]{1,0:T(8,128)(2,1)S(1)} %pad_maximum_fusion.rows_ref, bf16[4096,768]{1,0:T(8,128)(2,1)S(1)} %bitcast.23, bf16[4096,768]{1,0:T(8,128)(2,1)S(1)} %bitcast.29, bf16[768,4096]{1,0:T(8,128)(2,1)S(1)} %bitcast.35), custom_call_target="tpu_custom_call" | custom-call | flops 1048576 | bytes 1048576 | tf_op jit(solution)/shard_map/expert/pallas_call | solution.py:412
  162.0 3.3 %collective-permute-start.26 = (bf16[128,4096]{1,0:T(8,128)(2,1)S(1)}, bf16[128,4096]{1,0:T(8,128)(2,1)S(1)}, u32[]{:S(2)}, u32[]{:S(2)}) collective-permute-start(bf16[128,4096]{1,0:T(8,128)(2,1)S(1)} %collective-permute-done.20), channel_id=1, source_target_pairs={{0,8},{8,16},{16,24},{24,0},{32,40},{40,48},{48,56},{56,32},{64,72... | collective-permute-start | bytes 3145736 | tf_op jit(solution)/shard_map/ppermute | solution.py:51
  165.5 8.4 %expert.5 = (bf16[128,4096]{1,0:T(8,128)(2,1)S(1)}, bf16[128,4096]{1,0:T(8,128)(2,1)S(1)}) custom-call(bf16[256,4096]{1,0:T(8,128)(2,1)S(1)} %pad_maximum_fusion.1.rows_ref, bf16[4096,768]{1,0:T(8,128)(2,1)S(1)} %bitcast.24, bf16[4096,768]{1,0:T(8,128)(2,1)S(1)} %bitcast.30, bf16[768,4096]{1,0:T(8,128)(2,1)S(1)} %bitcast.36), custom_call_target="tpu_custom_call" | custom-call | flops 1048576 | bytes 1048576 | tf_op jit(solution)/shard_map/expert/pallas_call | solution.py:412
  174.0 3.3 %collective-permute-start.31 = (bf16[128,4096]{1,0:T(8,128)(2,1)S(1)}, bf16[128,4096]{1,0:T(8,128)(2,1)S(1)}, u32[]{:S(2)}, u32[]{:S(2)}) collective-permute-start(bf16[128,4096]{1,0:T(8,128)(2,1)S(1)} %get-tuple-element.69), channel_id=1, source_target_pairs={{0,8},{8,16},{16,24},{24,0},{32,40},{40,48},{48,56},{56,32},{64,72... | collective-permute-start | bytes 3145736 | tf_op jit(solution)/shard_map/ppermute | solution.py:51
  177.5 8.4 %expert.6 = (bf16[128,4096]{1,0:T(8,128)(2,1)S(1)}, bf16[128,4096]{1,0:T(8,128)(2,1)S(1)}) custom-call(bf16[256,4096]{1,0:T(8,128)(2,1)S(1)} %pad_maximum_fusion.2.rows_ref, bf16[4096,768]{1,0:T(8,128)(2,1)S(1)} %bitcast.25, bf16[4096,768]{1,0:T(8,128)(2,1)S(1)} %bitcast.31, bf16[768,4096]{1,0:T(8,128)(2,1)S(1)} %bitcast.37), custom_call_target="tpu_custom_call" | custom-call | flops 1048576 | bytes 1048576 | tf_op jit(solution)/shard_map/expert/pallas_call | solution.py:412
  186.1 8.4 %expert.7 = (bf16[128,4096]{1,0:T(8,128)(2,1)S(1)}, bf16[128,4096]{1,0:T(8,128)(2,1)S(1)}) custom-call(bf16[256,4096]{1,0:T(8,128)(2,1)S(1)} %pad_maximum_fusion.3.rows_ref, bf16[4096,768]{1,0:T(8,128)(2,1)S(1)} %bitcast.26, bf16[4096,768]{1,0:T(8,128)(2,1)S(1)} %bitcast.32, bf16[768,4096]{1,0:T(8,128)(2,1)S(1)} %bitcast.38), custom_call_target="tpu_custom_call" | custom-call | flops 1048576 | bytes 1048576 | tf_op jit(solution)/shard_map/expert/pallas_call | solution.py:412
  194.6 3.2 %collective-permute-start.32 = (bf16[128,4096]{1,0:T(8,128)(2,1)S(1)}, bf16[128,4096]{1,0:T(8,128)(2,1)S(1)}, u32[]{:S(2)}, u32[]{:S(2)}) collective-permute-start(bf16[128,4096]{1,0:T(8,128)(2,1)S(1)} %get-tuple-element.72), channel_id=1, source_target_pairs={{0,8},{8,16},{16,24},{24,0},{32,40},{40,48},{48,56},{56,32},{64,72... | collective-permute-start | bytes 3145736 | tf_op jit(solution)/shard_map/ppermute | solution.py:51
  197.8 12.8 %collective-permute-done.34 = bf16[128,4096]{1,0:T(8,128)(2,1)S(1)} collective-permute-done((bf16[128,4096]{1,0:T(8,128)(2,1)S(1)}, bf16[128,4096]{1,0:T(8,128)(2,1)S(1)}, u32[]{:S(2)}, u32[]{:S(2)}) %collective-permute-start.34) | collective-permute-done | bytes 1048608 | tf_op jit(solution)/shard_map/ppermute | solution.py:51
  211.4 3.3 %collective-permute-start.33 = (bf16[128,4096]{1,0:T(8,128)(2,1)S(1)}, bf16[128,4096]{1,0:T(8,128)(2,1)S(1)}, u32[]{:S(2)}, u32[]{:S(2)}) collective-permute-start(bf16[128,4096]{1,0:T(8,128)(2,1)S(1)} %add_convert_fusion.3), channel_id=1, source_target_pairs={{0,8},{8,16},{16,24},{24,0},{32,40},{40,48},{48,56},{56,32},{64,72... | collective-permute-start | bytes 3145736 | tf_op jit(solution)/shard_map/ppermute | solution.py:51
  214.7 12.5 %collective-permute-done.35 = bf16[128,4096]{1,0:T(8,128)(2,1)S(1)} collective-permute-done((bf16[128,4096]{1,0:T(8,128)(2,1)S(1)}, bf16[128,4096]{1,0:T(8,128)(2,1)S(1)}, u32[]{:S(2)}, u32[]{:S(2)}) %collective-permute-start.35) | collective-permute-done | bytes 1048608 | tf_op jit(solution)/shard_map/ppermute | solution.py:51
  227.8 3.4 %collective-permute-start.38 = (bf16[32,4096]{1,0:T(8,128)(2,1)S(1)}, bf16[32,4096]{1,0:T(8,128)(2,1)S(1)}, u32[]{:S(2)}, u32[]{:S(2)}) collective-permute-start(bf16[32,4096]{1,0:T(8,128)(2,1)S(1)} %get-tuple-element.88), channel_id=1, source_target_pairs={{0,96},{32,0},{64,32},{96,64},{8,104},{40,8},{72,40},{104,72},{16,... | collective-permute-start | bytes 786440 | tf_op jit(solution)/shard_map/ppermute | solution.py:51
  231.7 3.8 %collective-permute-done.36 = bf16[32,4096]{1,0:T(8,128)(2,1)S(1)} collective-permute-done((bf16[32,4096]{1,0:T(8,128)(2,1)S(1)}, bf16[32,4096]{1,0:T(8,128)(2,1)S(1)}, u32[]{:S(2)}, u32[]{:S(2)}) %collective-permute-start.36) | collective-permute-done | bytes 262176 | tf_op jit(solution)/shard_map/ppermute | solution.py:51
  235.8 3.3 %collective-permute-start.39 = (bf16[64,4096]{1,0:T(8,128)(2,1)S(1)}, bf16[64,4096]{1,0:T(8,128)(2,1)S(1)}, u32[]{:S(2)}, u32[]{:S(2)}) collective-permute-start(bf16[64,4096]{1,0:T(8,128)(2,1)S(1)} %pad_maximum_fusion.9), channel_id=1, source_target_pairs={{0,96},{32,0},{64,32},{96,64},{8,104},{40,8},{72,40},{104,72},{16,... | collective-permute-start | bytes 1572872 | tf_op jit(solution)/shard_map/ppermute | solution.py:51
  239.1 7.0 %collective-permute-done.37 = bf16[64,4096]{1,0:T(8,128)(2,1)S(1)} collective-permute-done((bf16[64,4096]{1,0:T(8,128)(2,1)S(1)}, bf16[64,4096]{1,0:T(8,128)(2,1)S(1)}, u32[]{:S(2)}, u32[]{:S(2)}) %collective-permute-start.37) | collective-permute-done | bytes 524320 | tf_op jit(solution)/shard_map/ppermute | solution.py:51
  246.2 12.8 %all_to_all.11 = bf16[8,8,4096]{2,1,0:T(8,128)(2,1)S(1)} all-to-all(bf16[8,8,4096]{2,1,0:T(8,128)(2,1)S(1)} %fusion.1), channel_id=1, replica_groups=mesh['seq'=16,'exp'=8] {'exp'}, dimensions={0} | all-to-all | bytes 1048576 | tf_op jit(solution)/shard_map/all_to_all | solution.py:685
  259.0 1.2 convolution_add_fusion
  (133 shorter events, 12.7 us)
Async XLA Ops:
  6.5 21.6 %copy-start.14 = (f32[1024,16]{0,1:T(8,128)S(1)}, f32[1024,16]{0,1:T(8,128)}, u32[]{:S(2)}) copy-start(f32[1024,16]{0,1:T(8,128)} %param.23) | copy-start | bytes 196612
  6.5 33.7 %copy-start.11 = (f32[1024]{0:T(1024)S(1)}, f32[1024]{0:T(1024)}, u32[]{:S(2)}) copy-start(f32[1024]{0:T(1024)} %param.22) | copy-start | bytes 12292
  6.5 33.7 %copy-start.7 = (bf16[256,1024]{1,0:T(8,128)(2,1)S(1)}, bf16[256,1024]{1,0:T(8,128)(2,1)}, u32[]{:S(2)}) copy-start(bf16[256,1024]{1,0:T(8,128)(2,1)} %proj_hbm.1) | copy-start | bytes 1572868
  6.5 77.2 %all-gather.3.cloned.1.call-start = ((), (), s32[]{:S(2)}) async-start(), calls=%async_computation.2 | async-start | bytes 8912896 | tf_op jit(solution)/shard_map/all_gather | solution.py:499
  8.0 5.5 %collective-permute-start = (bf16[3,1024]{1,0:T(4,128)(2,1)S(1)}, bf16[3,1024]{1,0:T(4,128)(2,1)S(1)}, u32[]{:S(2)}, u32[]{:S(2)}) collective-permute-start(bf16[3,1024]{1,0:T(4,128)(2,1)S(1)} %slice.81), channel_id=1, source_target_pairs={{0,8},{8,16},{16,24},{24,32},{32,40},{40,48},{48,56},{56,64},{64,7... | collective-permute-start | bytes 18440 | tf_op jit(solution)/shard_map/ppermute | solution.py:57
  13.5 1.1 copy-start.5
  14.6 1.0 copy-start.6
  20.0 51.0 %copy-start.8 = (bf16[256,1024]{1,0:T(8,128)(2,1)S(1)}, bf16[256,1024]{1,0:T(8,128)(2,1)}, u32[]{:S(2)}) copy-start(bf16[256,1024]{1,0:T(8,128)(2,1)} %z_hbm.1) | copy-start | bytes 1572868
  20.0 51.0 %copy-start.12 = (f32[1024]{0:T(1024)S(1)}, f32[1024]{0:T(1024)}, u32[]{:S(2)}) copy-start(f32[1024]{0:T(1024)} %param.24) | copy-start | bytes 12292
  20.0 1.5 collective-permute-start.1
  21.6 6.6 %collective-permute-start.2 = (f32[32,288]{1,0:T(8,128)S(1)}, f32[32,288]{1,0:T(8,128)S(1)}, u32[]{:S(2)}, u32[]{:S(2)}) collective-permute-start(f32[32,288]{1,0:T(8,128)S(1)} %get-tuple-element.93), channel_id=1, source_target_pairs={{0,2},{1,3},{2,4},{3,5},{4,6},{5,7},{6,0},{7,1},{8,10},{9,11},{10,... | collective-permute-start | bytes 110600 | tf_op jit(solution)/shard_map/ppermute | solution.py:497
  23.5 6.4 %collective-permute-start.3 = (f32[32,288]{1,0:T(8,128)S(1)}, f32[32,288]{1,0:T(8,128)S(1)}, u32[]{:S(2)}, u32[]{:S(2)}) collective-permute-start(f32[32,288]{1,0:T(8,128)S(1)} %get-tuple-element.95), channel_id=1, source_target_pairs={{0,4},{1,5},{2,6},{3,7},{4,0},{5,1},{6,2},{7,3},{8,12},{9,13},{10,... | collective-permute-start | bytes 110600 | tf_op jit(solution)/shard_map/ppermute | solution.py:497
  27.1 4.1 %collective-permute-start.4 = (f32[32,288]{1,0:T(8,128)S(1)}, f32[32,288]{1,0:T(8,128)S(1)}, u32[]{:S(2)}, u32[]{:S(2)}) collective-permute-start(f32[32,288]{1,0:T(8,128)S(1)} %get-tuple-element.94), channel_id=1, source_target_pairs={{0,6},{1,7},{2,0},{3,1},{4,2},{5,3},{6,4},{7,5},{8,14},{9,15},{10,... | collective-permute-start | bytes 110600 | tf_op jit(solution)/shard_map/ppermute | solution.py:497
  31.3 5.0 %collective-permute-start.5 = (bf16[32,320]{1,0:T(8,128)(2,1)S(1)}, bf16[32,320]{1,0:T(8,128)(2,1)S(1)}, u32[]{:S(2)}, u32[]{:S(2)}) collective-permute-start(bf16[32,320]{1,0:T(8,128)(2,1)S(1)} %pad_maximum_fusion.12), channel_id=1, source_target_pairs={{0,2},{1,3},{2,4},{3,5},{4,6},{5,7},{6,0},{7,1},{8,10},{9,11},{10,... | collective-permute-start | bytes 61448 | tf_op jit(solution)/shard_map/ppermute | solution.py:497
  31.4 5.7 %collective-permute-start.6 = (bf16[32,320]{1,0:T(8,128)(2,1)S(1)}, bf16[32,320]{1,0:T(8,128)(2,1)S(1)}, u32[]{:S(2)}, u32[]{:S(2)}) collective-permute-start(bf16[32,320]{1,0:T(8,128)(2,1)S(1)} %pad_maximum_fusion.12), channel_id=1, source_target_pairs={{0,4},{1,5},{2,6},{3,7},{4,0},{5,1},{6,2},{7,3},{8,12},{9,13},{10,... | collective-permute-start | bytes 61448 | tf_op jit(solution)/shard_map/ppermute | solution.py:497
  35.0 3.8 %collective-permute-start.7 = (bf16[32,320]{1,0:T(8,128)(2,1)S(1)}, bf16[32,320]{1,0:T(8,128)(2,1)S(1)}, u32[]{:S(2)}, u32[]{:S(2)}) collective-permute-start(bf16[32,320]{1,0:T(8,128)(2,1)S(1)} %pad_maximum_fusion.12), channel_id=1, source_target_pairs={{0,6},{1,7},{2,0},{3,1},{4,2},{5,3},{6,4},{7,5},{8,14},{9,15},{10,... | collective-permute-start | bytes 61448 | tf_op jit(solution)/shard_map/ppermute | solution.py:497
  38.9 1.3 collective-permute-start.8
  49.0 1.0 copy-start.1
  50.0 1.0 copy-start.3
  51.0 0.8 copy-start.9
  51.7 6.6 %collective-permute-start.10 = (bf16[16,1152]{1,0:T(8,128)(2,1)S(1)}, bf16[16,1152]{1,0:T(8,128)(2,1)S(1)}, u32[]{:S(2)}, u32[]{:S(2)}) collective-permute-start(bf16[16,1152]{1,0:T(8,128)(2,1)S(1)} %get-tuple-element.44.own_ref), channel_id=1, source_target_pairs={{0,16},{8,24},{16,0},{24,8},{32,48},{40,56},{48,32},{56,40},{64,80... | collective-permute-start | bytes 110600 | tf_op jit(solution)/shard_map/ppermute | solution.py:282
  53.0 5.3 %collective-permute-start.11 = (bf16[16,1152]{1,0:T(8,128)(2,1)S(1)}, bf16[16,1152]{1,0:T(8,128)(2,1)S(1)}, u32[]{:S(2)}, u32[]{:S(2)}) collective-permute-start(bf16[16,1152]{1,0:T(8,128)(2,1)S(1)} %get-tuple-element.44.own_ref), channel_id=1, source_target_pairs={{0,8},{8,16},{16,24},{24,0},{32,40},{40,48},{48,56},{56,32},{64,72... | collective-permute-start | bytes 110600 | tf_op jit(solution)/shard_map/ppermute | solution.py:282
  55.2 5.9 %collective-permute-start.9 = (bf16[16,1152]{1,0:T(8,128)(2,1)S(1)}, bf16[16,1152]{1,0:T(8,128)(2,1)S(1)}, u32[]{:S(2)}, u32[]{:S(2)}) collective-permute-start(bf16[16,1152]{1,0:T(8,128)(2,1)S(1)} %get-tuple-element.44.own_ref), channel_id=1, source_target_pairs={{0,24},{8,0},{16,8},{24,16},{32,56},{40,32},{48,40},{56,48},{64,88... | collective-permute-start | bytes 110600 | tf_op jit(solution)/shard_map/ppermute | solution.py:282
  61.2 5.2 %collective-permute-start.12 = (bf16[16,1152]{1,0:T(8,128)(2,1)S(1)}, bf16[16,1152]{1,0:T(8,128)(2,1)S(1)}, u32[]{:S(2)}, u32[]{:S(2)}) collective-permute-start(bf16[16,1152]{1,0:T(8,128)(2,1)S(1)} %convert_element_type.124), channel_id=1, source_target_pairs={{0,96},{8,104},{16,112},{24,120},{32,0},{40,8},{48,16},{56,24},{64... | collective-permute-start | bytes 110600 | tf_op jit(solution)/shard_map/ppermute | solution.py:282
  64.0 6.2 %collective-permute-start.13 = (bf16[16,1152]{1,0:T(8,128)(2,1)S(1)}, bf16[16,1152]{1,0:T(8,128)(2,1)S(1)}, u32[]{:S(2)}, u32[]{:S(2)}) collective-permute-start(bf16[16,1152]{1,0:T(8,128)(2,1)S(1)} %convert_element_type.124), channel_id=1, source_target_pairs={{0,64},{8,72},{16,80},{24,88},{32,96},{40,104},{48,112},{56,120},{... | collective-permute-start | bytes 110600 | tf_op jit(solution)/shard_map/ppermute | solution.py:282
  64.8 6.1 %collective-permute-start.14 = (bf16[16,1152]{1,0:T(8,128)(2,1)S(1)}, bf16[16,1152]{1,0:T(8,128)(2,1)S(1)}, u32[]{:S(2)}, u32[]{:S(2)}) collective-permute-start(bf16[16,1152]{1,0:T(8,128)(2,1)S(1)} %convert_element_type.124), channel_id=1, source_target_pairs={{0,32},{8,40},{16,48},{24,56},{32,64},{40,72},{48,80},{56,88},{64,... | collective-permute-start | bytes 110600 | tf_op jit(solution)/shard_map/ppermute | solution.py:282
  71.0 1.2 copy-start.2
  72.2 1.2 copy-start.4
  73.5 1.1 copy-start.10
  83.8 8.5 %copy-start.15 = (s32[32,2]{0,1:T(2,128)S(1)}, s32[32,2]{0,1:T(2,128)}, u32[]{:S(2)}) copy-start(s32[32,2]{0,1:T(2,128)} %param.27) | copy-start | bytes 772
  83.8 69.6 %slice-start.4 = ((s8[6291456]{0:T(1024)(128)(4,1)}), s8[2097152]{0:T(1024)(128)(4,1)S(1)}, s32[]{:S(2)}) async-start(s8[6291456]{0:T(1024)(128)(4,1)} %bitcast.33), calls=%async_computation.7 | async-start | bytes 4194304
  90.9 1.3 copy-start
  92.3 2.9 %collective-permute-start.15 = (bf16[128,4096]{1,0:T(8,128)(2,1)}, bf16[128,4096]{1,0:T(8,128)(2,1)S(1)}, u32[]{:S(2)}, u32[]{:S(2)}) collective-permute-start(bf16[128,4096]{1,0:T(8,128)(2,1)} %get-tuple-element.53), channel_id=1, source_target_pairs={{0,1},{1,0},{2,3},{3,2},{4,5},{5,4},{6,7},{7,6},{8,9},{9,8},{10,11... | collective-permute-start | bytes 3145736 | tf_op jit(solution)/shard_map/ppermute | solution.py:627
  95.1 8.0 %copy-start.16 = (f32[32,2]{0,1:T(2,128)S(1)}, f32[32,2]{0,1:T(2,128)}, u32[]{:S(2)}) copy-start(f32[32,2]{0,1:T(2,128)} %param.28) | copy-start | bytes 772
  95.1 18.6 %copy-start.13 = (bf16[32,4096]{1,0:T(8,128)(2,1)S(1)}, bf16[32,4096]{1,0:T(8,128)(2,1)}, u32[]{:S(2)}) copy-start(bf16[32,4096]{1,0:T(8,128)(2,1)} %param.26) | copy-start | bytes 786436
  95.1 58.3 %slice-start.2 = ((s8[6291456]{0:T(1024)(128)(4,1)}), s8[4194304]{0:T(1024)(128)(4,1)S(1)}, s32[]{:S(2)}) async-start(s8[6291456]{0:T(1024)(128)(4,1)} %bitcast.27), calls=%async_computation.5 | async-start | bytes 8388608
  97.2 56.2 %slice-start.5 = ((s8[6291456]{0:T(1024)(128)(4,1)}), s8[4194304]{0:T(1024)(128)(4,1)S(1)}, s32[]{:S(2)}) async-start(s8[6291456]{0:T(1024)(128)(4,1)} %bitcast.33), calls=%async_computation.8 | async-start | bytes 8388608
  97.3 9.6 %collective-permute-start.16 = (bf16[32,4096]{1,0:T(8,128)(2,1)S(1)}, bf16[32,4096]{1,0:T(8,128)(2,1)S(1)}, u32[]{:S(2)}, u32[]{:S(2)}) collective-permute-start(bf16[32,4096]{1,0:T(8,128)(2,1)S(1)} %get-tuple-element.90), channel_id=1, source_target_pairs={{0,2},{1,3},{2,4},{3,5},{4,6},{5,7},{6,0},{7,1},{8,10},{9,11},{10,... | collective-permute-start | bytes 786440 | tf_op jit(solution)/shard_map/ppermute | solution.py:497
  98.9 14.8 %collective-permute-start.17 = (bf16[32,4096]{1,0:T(8,128)(2,1)S(1)}, bf16[32,4096]{1,0:T(8,128)(2,1)S(1)}, u32[]{:S(2)}, u32[]{:S(2)}) collective-permute-start(bf16[32,4096]{1,0:T(8,128)(2,1)S(1)} %get-tuple-element.92), channel_id=1, source_target_pairs={{0,4},{1,5},{2,6},{3,7},{4,0},{5,1},{6,2},{7,3},{8,12},{9,13},{10,... | collective-permute-start | bytes 786440 | tf_op jit(solution)/shard_map/ppermute | solution.py:497
  101.8 11.9 %collective-permute-start.18 = (bf16[32,4096]{1,0:T(8,128)(2,1)S(1)}, bf16[32,4096]{1,0:T(8,128)(2,1)S(1)}, u32[]{:S(2)}, u32[]{:S(2)}) collective-permute-start(bf16[32,4096]{1,0:T(8,128)(2,1)S(1)} %get-tuple-element.91), channel_id=1, source_target_pairs={{0,6},{1,7},{2,0},{3,1},{4,2},{5,3},{6,4},{7,5},{8,14},{9,15},{10,... | collective-permute-start | bytes 786440 | tf_op jit(solution)/shard_map/ppermute | solution.py:497
  113.7 39.7 %slice-start = ((s8[6291456]{0:T(1024)(128)(4,1)}), s8[4194304]{0:T(1024)(128)(4,1)S(1)}, s32[]{:S(2)}) async-start(s8[6291456]{0:T(1024)(128)(4,1)} %bitcast.21), calls=%async_computation.3 | async-start | bytes 8388608
  114.4 39.1 %slice-start.3 = ((s8[6291456]{0:T(1024)(128)(4,1)}), s8[2097152]{0:T(1024)(128)(4,1)S(1)}, s32[]{:S(2)}) async-start(s8[6291456]{0:T(1024)(128)(4,1)} %bitcast.27), calls=%async_computation.6 | async-start | bytes 4194304
  128.7 10.4 %collective-permute-start.19 = (bf16[64,4096]{1,0:T(8,128)(2,1)S(1)}, bf16[64,4096]{1,0:T(8,128)(2,1)S(1)}, u32[]{:S(2)}, u32[]{:S(2)}) collective-permute-start(bf16[64,4096]{1,0:T(8,128)(2,1)S(1)} %bitcast.43), channel_id=1, source_target_pairs={{0,32},{32,64},{64,96},{96,0},{8,40},{40,72},{72,104},{104,8},{16,... | collective-permute-start | bytes 1572872 | tf_op jit(solution)/shard_map/ppermute | solution.py:51
  129.0 10.3 %collective-permute-start.21 = (bf16[64,4096]{1,0:T(8,128)(2,1)S(1)}, bf16[64,4096]{1,0:T(8,128)(2,1)S(1)}, u32[]{:S(2)}, u32[]{:S(2)}) collective-permute-start(bf16[64,4096]{1,0:T(8,128)(2,1)S(1)} %bitcast.44), channel_id=1, source_target_pairs={{0,96},{32,0},{64,32},{96,64},{8,104},{40,8},{72,40},{104,72},{16,... | collective-permute-start | bytes 1572872 | tf_op jit(solution)/shard_map/ppermute | solution.py:51
  139.1 10.5 %collective-permute-start.23 = (bf16[32,4096]{1,0:T(8,128)(2,1)S(1)}, bf16[32,4096]{1,0:T(8,128)(2,1)S(1)}, u32[]{:S(2)}, u32[]{:S(2)}) collective-permute-start(bf16[32,4096]{1,0:T(8,128)(2,1)S(1)} %slice.111), channel_id=1, source_target_pairs={{0,32},{32,64},{64,96},{96,0},{8,40},{40,72},{72,104},{104,8},{16,... | collective-permute-start | bytes 786440 | tf_op jit(solution)/shard_map/ppermute | solution.py:51
  139.3 14.2 %slice-start.1 = ((s8[6291456]{0:T(1024)(128)(4,1)}), s8[2097152]{0:T(1024)(128)(4,1)S(1)}, s32[]{:S(2)}) async-start(s8[6291456]{0:T(1024)(128)(4,1)} %bitcast.21), calls=%async_computation.4 | async-start | bytes 4194304
  139.3 10.4 %collective-permute-start.24 = (bf16[32,4096]{1,0:T(8,128)(2,1)S(1)}, bf16[32,4096]{1,0:T(8,128)(2,1)S(1)}, u32[]{:S(2)}, u32[]{:S(2)}) collective-permute-start(bf16[32,4096]{1,0:T(8,128)(2,1)S(1)} %slice.112), channel_id=1, source_target_pairs={{0,96},{32,0},{64,32},{96,64},{8,104},{40,8},{72,40},{104,72},{16,... | collective-permute-start | bytes 786440 | tf_op jit(solution)/shard_map/ppermute | solution.py:51
  142.6 19.4 %collective-permute-start.20 = (bf16[128,4096]{1,0:T(8,128)(2,1)S(1)}, bf16[128,4096]{1,0:T(8,128)(2,1)S(1)}, u32[]{:S(2)}, u32[]{:S(2)}) collective-permute-start(bf16[128,4096]{1,0:T(8,128)(2,1)S(1)} %pad_maximum_fusion.4), channel_id=1, source_target_pairs={{0,8},{8,16},{16,24},{24,0},{32,40},{40,48},{48,56},{56,32},{64,72... | collective-permute-start | bytes 3145736 | tf_op jit(solution)/shard_map/ppermute | solution.py:51
  143.3 18.6 %collective-permute-start.22 = (bf16[64,4096]{1,0:T(8,128)(2,1)S(1)}, bf16[64,4096]{1,0:T(8,128)(2,1)S(1)}, u32[]{:S(2)}, u32[]{:S(2)}) collective-permute-start(bf16[64,4096]{1,0:T(8,128)(2,1)S(1)} %collective-permute-done.21), channel_id=1, source_target_pairs={{0,24},{8,0},{16,8},{24,16},{32,56},{40,32},{48,40},{56,48},{64,88... | collective-permute-start | bytes 1572872 | tf_op jit(solution)/shard_map/ppermute | solution.py:51
  149.7 12.2 %collective-permute-start.25 = (bf16[64,4096]{1,0:T(8,128)(2,1)S(1)}, bf16[64,4096]{1,0:T(8,128)(2,1)S(1)}, u32[]{:S(2)}, u32[]{:S(2)}) collective-permute-start(bf16[64,4096]{1,0:T(8,128)(2,1)S(1)} %pad_maximum_fusion.7), channel_id=1, source_target_pairs={{0,24},{8,0},{16,8},{24,16},{32,56},{40,32},{48,40},{56,48},{64,88... | collective-permute-start | bytes 1572872 | tf_op jit(solution)/shard_map/ppermute | solution.py:51
  150.7 23.3 %collective-permute-start.28 = (bf16[128,4096]{1,0:T(8,128)(2,1)S(1)}, bf16[128,4096]{1,0:T(8,128)(2,1)S(1)}, u32[]{:S(2)}, u32[]{:S(2)}) collective-permute-start(bf16[128,4096]{1,0:T(8,128)(2,1)S(1)} %pad_maximum_fusion.6), channel_id=1, source_target_pairs={{0,8},{8,16},{16,24},{24,0},{32,40},{40,48},{48,56},{56,32},{64,72... | collective-permute-start | bytes 3145736 | tf_op jit(solution)/shard_map/ppermute | solution.py:51
  153.2 24.1 %collective-permute-start.29 = (bf16[128,4096]{1,0:T(8,128)(2,1)S(1)}, bf16[128,4096]{1,0:T(8,128)(2,1)S(1)}, u32[]{:S(2)}, u32[]{:S(2)}) collective-permute-start(bf16[128,4096]{1,0:T(8,128)(2,1)S(1)} %pad_maximum_fusion.4), channel_id=1, source_target_pairs={{0,24},{8,0},{16,8},{24,16},{32,56},{40,32},{48,40},{56,48},{64,88... | collective-permute-start | bytes 3145736 | tf_op jit(solution)/shard_map/ppermute | solution.py:51
  162.0 23.9 %collective-permute-start.26 = (bf16[128,4096]{1,0:T(8,128)(2,1)S(1)}, bf16[128,4096]{1,0:T(8,128)(2,1)S(1)}, u32[]{:S(2)}, u32[]{:S(2)}) collective-permute-start(bf16[128,4096]{1,0:T(8,128)(2,1)S(1)} %collective-permute-done.20), channel_id=1, source_target_pairs={{0,8},{8,16},{16,24},{24,0},{32,40},{40,48},{48,56},{56,32},{64,72... | collective-permute-start | bytes 3145736 | tf_op jit(solution)/shard_map/ppermute | solution.py:51
  165.3 20.6 %collective-permute-start.27 = (bf16[128,4096]{1,0:T(8,128)(2,1)S(1)}, bf16[128,4096]{1,0:T(8,128)(2,1)S(1)}, u32[]{:S(2)}, u32[]{:S(2)}) collective-permute-start(bf16[128,4096]{1,0:T(8,128)(2,1)S(1)} %pad_maximum_fusion.5), channel_id=1, source_target_pairs={{0,24},{8,0},{16,8},{24,16},{32,56},{40,32},{48,40},{56,48},{64,88... | collective-permute-start | bytes 3145736 | tf_op jit(solution)/shard_map/ppermute | solution.py:51
  173.9 20.6 %collective-permute-start.30 = (bf16[128,4096]{1,0:T(8,128)(2,1)S(1)}, bf16[128,4096]{1,0:T(8,128)(2,1)S(1)}, u32[]{:S(2)}, u32[]{:S(2)}) collective-permute-start(bf16[128,4096]{1,0:T(8,128)(2,1)S(1)} %get-tuple-element.61), channel_id=1, source_target_pairs={{0,24},{8,0},{16,8},{24,16},{32,56},{40,32},{48,40},{56,48},{64,88... | collective-permute-start | bytes 3145736 | tf_op jit(solution)/shard_map/ppermute | solution.py:51
  174.0 20.5 %collective-permute-start.31 = (bf16[128,4096]{1,0:T(8,128)(2,1)S(1)}, bf16[128,4096]{1,0:T(8,128)(2,1)S(1)}, u32[]{:S(2)}, u32[]{:S(2)}) collective-permute-start(bf16[128,4096]{1,0:T(8,128)(2,1)S(1)} %get-tuple-element.69), channel_id=1, source_target_pairs={{0,8},{8,16},{16,24},{24,0},{32,40},{40,48},{48,56},{56,32},{64,72... | collective-permute-start | bytes 3145736 | tf_op jit(solution)/shard_map/ppermute | solution.py:51
  194.5 16.1 %collective-permute-start.34 = (bf16[128,4096]{1,0:T(8,128)(2,1)S(1)}, bf16[128,4096]{1,0:T(8,128)(2,1)S(1)}, u32[]{:S(2)}, u32[]{:S(2)}) collective-permute-start(bf16[128,4096]{1,0:T(8,128)(2,1)S(1)} %get-tuple-element.76), channel_id=1, source_target_pairs={{0,24},{8,0},{16,8},{24,16},{32,56},{40,32},{48,40},{56,48},{64,88... | collective-permute-start | bytes 3145736 | tf_op jit(solution)/shard_map/ppermute | solution.py:51
  194.6 16.6 %collective-permute-start.32 = (bf16[128,4096]{1,0:T(8,128)(2,1)S(1)}, bf16[128,4096]{1,0:T(8,128)(2,1)S(1)}, u32[]{:S(2)}, u32[]{:S(2)}) collective-permute-start(bf16[128,4096]{1,0:T(8,128)(2,1)S(1)} %get-tuple-element.72), channel_id=1, source_target_pairs={{0,8},{8,16},{16,24},{24,0},{32,40},{40,48},{48,56},{56,32},{64,72... | collective-permute-start | bytes 3145736 | tf_op jit(solution)/shard_map/ppermute | solution.py:51
  210.9 16.4 %collective-permute-start.35 = (bf16[128,4096]{1,0:T(8,128)(2,1)S(1)}, bf16[128,4096]{1,0:T(8,128)(2,1)S(1)}, u32[]{:S(2)}, u32[]{:S(2)}) collective-permute-start(bf16[128,4096]{1,0:T(8,128)(2,1)S(1)} %add_convert_fusion.1), channel_id=1, source_target_pairs={{0,24},{8,0},{16,8},{24,16},{32,56},{40,32},{48,40},{56,48},{64,88... | collective-permute-start | bytes 3145736 | tf_op jit(solution)/shard_map/ppermute | solution.py:51
  211.4 19.8 %collective-permute-start.33 = (bf16[128,4096]{1,0:T(8,128)(2,1)S(1)}, bf16[128,4096]{1,0:T(8,128)(2,1)S(1)}, u32[]{:S(2)}, u32[]{:S(2)}) collective-permute-start(bf16[128,4096]{1,0:T(8,128)(2,1)S(1)} %add_convert_fusion.3), channel_id=1, source_target_pairs={{0,8},{8,16},{16,24},{24,0},{32,40},{40,48},{48,56},{56,32},{64,72... | collective-permute-start | bytes 3145736 | tf_op jit(solution)/shard_map/ppermute | solution.py:51
  227.8 7.7 %collective-permute-start.36 = (bf16[32,4096]{1,0:T(8,128)(2,1)S(1)}, bf16[32,4096]{1,0:T(8,128)(2,1)S(1)}, u32[]{:S(2)}, u32[]{:S(2)}) collective-permute-start(bf16[32,4096]{1,0:T(8,128)(2,1)S(1)} %get-tuple-element.87), channel_id=1, source_target_pairs={{0,32},{32,64},{64,96},{96,0},{8,40},{40,72},{72,104},{104,8},{16,... | collective-permute-start | bytes 786440 | tf_op jit(solution)/shard_map/ppermute | solution.py:51
  227.8 7.8 %collective-permute-start.38 = (bf16[32,4096]{1,0:T(8,128)(2,1)S(1)}, bf16[32,4096]{1,0:T(8,128)(2,1)S(1)}, u32[]{:S(2)}, u32[]{:S(2)}) collective-permute-start(bf16[32,4096]{1,0:T(8,128)(2,1)S(1)} %get-tuple-element.88), channel_id=1, source_target_pairs={{0,96},{32,0},{64,32},{96,64},{8,104},{40,8},{72,40},{104,72},{16,... | collective-permute-start | bytes 786440 | tf_op jit(solution)/shard_map/ppermute | solution.py:51
  235.6 10.5 %collective-permute-start.37 = (bf16[64,4096]{1,0:T(8,128)(2,1)S(1)}, bf16[64,4096]{1,0:T(8,128)(2,1)S(1)}, u32[]{:S(2)}, u32[]{:S(2)}) collective-permute-start(bf16[64,4096]{1,0:T(8,128)(2,1)S(1)} %pad_maximum_fusion.8), channel_id=1, source_target_pairs={{0,32},{32,64},{64,96},{96,0},{8,40},{40,72},{72,104},{104,8},{16,... | collective-permute-start | bytes 1572872 | tf_op jit(solution)/shard_map/ppermute | solution.py:51
  235.8 10.3 %collective-permute-start.39 = (bf16[64,4096]{1,0:T(8,128)(2,1)S(1)}, bf16[64,4096]{1,0:T(8,128)(2,1)S(1)}, u32[]{:S(2)}, u32[]{:S(2)}) collective-permute-start(bf16[64,4096]{1,0:T(8,128)(2,1)S(1)} %pad_maximum_fusion.9), channel_id=1, source_target_pairs={{0,96},{32,0},{64,32},{96,64},{8,104},{40,8},{72,40},{104,72},{16,... | collective-permute-start | bytes 1572872 | tf_op jit(solution)/shard_map/ppermute | solution.py:51
Sparse Core Ops, SparseCore 0:
  9.5 74.2 all-gather.2
